TPU v7x, 32 devices: a whole 2x2x4 slice. The times are simulated.
32 devices in a mesh: head: 4 (over y, x), wide: 8 (over z, core).
Axes of the slice: x: 2, y: 2, z: 4, core: 2. Of those that a mesh axis runs over, the one named last changes fastest.
Arguments:
- inputs: bfloat16 [4096, 2048], P(('head', 'wide')), may hold values from -6 to 6
- attn_gain: float32 [2048], replicated, may hold values from 0.1 to 1.9
- query_weight: bfloat16 [2048, 2048], P(None, 'head'), may hold values from -0.125 to 0.125
- key_projection: bfloat16 [2048, 1024], P(None, 'head'), may hold values from -0.125 to 0.125
- value_projection: bfloat16 [2048, 1024], P(None, 'head'), may hold values from -0.125 to 0.125
- attn_gate_weight: bfloat16 [2048, 2048], P(None, 'head'), may hold values from -0.125 to 0.125
- output_weight: bfloat16 [2048, 2048], P('head'), may hold values from -1.5 to 1.5
- query_gain: float32 [128], replicated, may hold values from 0.1 to 1.9
- key_gain: float32 [128], replicated, may hold values from 0.1 to 1.9
- ffn_gain: float32 [2048], replicated, may hold values from 0.1 to 1.9
- ffn_gate_weight: bfloat16 [2048, 6144], P(None, 'wide'), may hold values from -0.125 to 0.125
- ffn_up_weight: bfloat16 [2048, 6144], P(None, 'wide'), may hold values from -0.125 to 0.125
- ffn_down_weight: bfloat16 [6144, 2048], P('wide'), may hold values from -0.109375 to 0.109375
- doc_lengths: int32 [1, 8], replicated, may hold values from 1 to 2560, 4096 in all within a row
- cotangent: bfloat16 [4096, 2048], P(('head', 'wide')), may hold values from -11 to 11
Outputs:
- outputs: bfloat16 [4096, 2048], P(('head', 'wide'))
- input_grad: float32 [4096, 2048], P(('head', 'wide'))
- attn_gain_grad: float32 [2048], replicated
- query_grad: float32 [2048, 2048], P('wide', 'head')
- key_grad: float32 [2048, 1024], P('wide', 'head')
- value_grad: float32 [2048, 1024], P('wide', 'head')
- attn_gate_grad: float32 [2048, 2048], P('wide', 'head')
- output_grad: float32 [2048, 2048], P('head', 'wide')
- query_gain_grad: float32 [128], replicated
- key_gain_grad: float32 [128], replicated
- ffn_gain_grad: float32 [2048], replicated
- ffn_gate_grad: float32 [2048, 6144], P('head', 'wide')
- ffn_up_grad: float32 [2048, 6144], P('head', 'wide')
- ffn_down_grad: float32 [6144, 2048], P('wide', 'head')
Inputs may be any that keep to these rules, and one draw needn't show every extreme that they name: `doc_lengths`: each row's 8 lengths sum to 4096, and the longest of each row is 2560.
All inputs are finite; a program needn't handle non-finite values.
Results may differ from a plain program's by a relative error of at most 0.024.
Values may be sent and summed in bfloat16 or wider, within the bound.
A program may use at most 256 MiB of HBM per device.

v0:
```python
import jax
import jax.numpy as jnp
from jax import lax
from jax.sharding import PartitionSpec as P

EPS = 1e-06
THETA = 1000000.0
NEG = -1e30


def rms_apply(values, gain_vec):
    return values * lax.rsqrt(jnp.mean(values * values, axis=-1, keepdims=True) + EPS) * gain_vec


def token_tables(doc_lengths, token_ids):
    lengths = doc_lengths.reshape(-1)
    doc_ends = jnp.cumsum(lengths)
    before = doc_ends[None, :] <= token_ids[:, None]
    document_segment = jnp.sum(before.astype(jnp.int32), axis=1)
    doc_first = jnp.sum(jnp.where(before, lengths[None, :], 0), axis=1)
    return (document_segment, token_ids - doc_first)


def rotary(position, head_width):
    half_width = head_width // 2
    inverse = THETA ** (-(jnp.arange(half_width, dtype=jnp.float32) * 2.0 / head_width))
    angles = position.astype(jnp.float32)[:, None] * inverse[None, :]
    cosine = jnp.cos(angles)
    sine_tab = jnp.sin(angles)
    return (
        jnp.concatenate([cosine, cosine], axis=1),
        jnp.concatenate([sine_tab, sine_tab], axis=1),
    )


def head_prep(pre_proj, gain_vec, cosine, sine_tab):
    row_count = pre_proj.shape[0]
    head_width = gain_vec.shape[0]
    half_width = head_width // 2
    per_head = rms_apply(pre_proj.reshape(row_count, -1, head_width), gain_vec)
    turned = jnp.concatenate([-per_head[..., half_width:], per_head[..., :half_width]], axis=-1)
    rotated = per_head * cosine[:, None, :] + turned * sine_tab[:, None, :]
    return rotated.reshape(row_count, -1)


def swiglu(gate_in, up_in):
    return jax.nn.silu(gate_in) * up_in


def to_heads(matrix, group_id, per_group, head_width):
    columns = per_group * head_width
    picked = matrix[:, group_id * columns : (group_id + 1) * columns]
    return picked.reshape(matrix.shape[0], per_group, head_width).transpose(1, 0, 2)


def from_heads(stacked_rows):
    return stacked_rows.transpose(1, 0, 2).reshape(stacked_rows.shape[1], -1)


def allowed_tile(query_tok, query_seg, tile_tok, tile_seg):
    return (query_seg[:, None] == tile_seg[None, :]) & (tile_tok[None, :] <= query_tok[:, None])


def score_tile(query_blk, key_tile, allowed, per_group):
    raw_scores = lax.dot_general(
        query_blk, key_tile, (((1,), (1,)), ((), ())), preferred_element_type=jnp.float32
    )
    scores = raw_scores.reshape(per_group, allowed.shape[0], allowed.shape[1]) * query_blk.shape[
        1
    ] ** (-0.5)
    return jnp.where(allowed[None], scores, NEG)


def forward_block(
    query_blk, key_tiles, value_tiles, tok_tiles, seg_tiles, query_tok, query_seg, per_group
):
    block_rows = query_tok.shape[0]

    def first_pass(carried, tile_set):
        run_max, run_tot = carried
        key_tile, tile_tok, tile_seg = tile_set
        scores = score_tile(
            query_blk, key_tile, allowed_tile(query_tok, query_seg, tile_tok, tile_seg), per_group
        )
        new_max = jnp.maximum(run_max, jnp.max(scores, axis=2))
        run_tot = run_tot * jnp.exp(run_max - new_max) + jnp.sum(
            jnp.exp(scores - new_max[..., None]), axis=2
        )
        return ((new_max, run_tot), None)

    start_state = (
        jnp.full((per_group, block_rows), NEG, jnp.float32),
        jnp.zeros((per_group, block_rows), jnp.float32),
    )
    (run_max, run_tot), unused = lax.scan(
        first_pass, start_state, (key_tiles, tok_tiles, seg_tiles)
    )
    log_tot = run_max + jnp.log(run_tot)

    def second_pass(running, tile_set):
        key_tile, value_tile, tile_tok, tile_seg = tile_set
        scores = score_tile(
            query_blk, key_tile, allowed_tile(query_tok, query_seg, tile_tok, tile_seg), per_group
        )
        prob_low = jnp.exp(scores - log_tot[..., None]).astype(jnp.bfloat16)
        running = running + jnp.dot(
            prob_low.reshape(-1, prob_low.shape[2]), value_tile, preferred_element_type=jnp.float32
        )
        return (running, None)

    zero_out = jnp.zeros((query_blk.shape[0], query_blk.shape[1]), jnp.float32)
    total_out, unused = lax.scan(
        second_pass, zero_out, (key_tiles, value_tiles, tok_tiles, seg_tiles)
    )
    return (total_out, log_tot)


def backward_block(
    query_blk,
    grad_blk,
    log_tot,
    row_delta,
    key_tiles,
    value_tiles,
    tok_tiles,
    seg_tiles,
    query_tok,
    query_seg,
    per_group,
):
    scale_f = query_blk.shape[1] ** (-0.5)

    def step_back(query_acc, tile_set):
        key_tile, value_tile, tile_tok, tile_seg = tile_set
        scores = score_tile(
            query_blk, key_tile, allowed_tile(query_tok, query_seg, tile_tok, tile_seg), per_group
        )
        prob_tile = jnp.exp(scores - log_tot[..., None])
        tile_width = prob_tile.shape[2]
        prob_low = prob_tile.astype(jnp.bfloat16).reshape(-1, tile_width)
        value_part = lax.dot_general(
            prob_low, grad_blk, (((0,), (0,)), ((), ())), preferred_element_type=jnp.float32
        )
        prob_grad = lax.dot_general(
            grad_blk, value_tile, (((1,), (1,)), ((), ())), preferred_element_type=jnp.float32
        )
        prob_grad = prob_grad.reshape(prob_tile.shape)
        score_grad = (prob_tile * (prob_grad - row_delta[..., None]) * scale_f).astype(jnp.bfloat16)
        score_grad = score_grad.reshape(-1, tile_width)
        query_acc = query_acc + jnp.dot(score_grad, key_tile, preferred_element_type=jnp.float32)
        key_part = lax.dot_general(
            score_grad, query_blk, (((0,), (0,)), ((), ())), preferred_element_type=jnp.float32
        )
        return (query_acc, (key_part, value_part))

    zero_grad = jnp.zeros((query_blk.shape[0], query_blk.shape[1]), jnp.float32)
    query_acc, (key_parts, value_parts) = lax.scan(
        step_back, zero_grad, (key_tiles, value_tiles, tok_tiles, seg_tiles)
    )
    return (
        query_acc,
        key_parts.reshape(-1, query_blk.shape[1]),
        value_parts.reshape(-1, query_blk.shape[1]),
    )


def block_plan(tok_dev, head_count, wide_count, row_len):
    group_tok = wide_count * tok_dev
    heads_per = max(min(row_len // group_tok, head_count), 1)
    span = heads_per * tok_dev
    plans = []
    for first_row in range(0, head_count * tok_dev, span):
        plans.append((first_row, span, first_row // tok_dev * group_tok, heads_per * group_tok))
    return plans


def key_step_of():
    return 2048


def attention_forward(
    query_low,
    key_entire,
    value_entire,
    query_tok,
    query_seg,
    key_tok,
    key_seg,
    per_group,
    head_width,
    plans,
):
    group_total = key_entire.shape[1] // head_width
    out_columns = []
    lse_list = []
    for group_id in range(group_total):
        key_cols = key_entire[:, group_id * head_width : (group_id + 1) * head_width]
        value_cols = value_entire[:, group_id * head_width : (group_id + 1) * head_width]
        stacked_rows = to_heads(query_low, group_id, per_group, head_width)
        pieces = []
        for first_row, span, key_first, key_width in plans:
            key_step = key_step_of()
            key_tiles = key_cols[key_first : key_first + key_width].reshape(
                -1, key_step, head_width
            )
            value_tiles = value_cols[key_first : key_first + key_width].reshape(
                -1, key_step, head_width
            )
            tok_tiles = key_tok[key_first : key_first + key_width].reshape(-1, key_step)
            seg_tiles = key_seg[key_first : key_first + key_width].reshape(-1, key_step)
            query_blk = stacked_rows[:, first_row : first_row + span].reshape(-1, head_width)
            total_out, log_tot = forward_block(
                query_blk,
                key_tiles,
                value_tiles,
                tok_tiles,
                seg_tiles,
                query_tok[first_row : first_row + span],
                query_seg[first_row : first_row + span],
                per_group,
            )
            pieces.append(total_out.reshape(per_group, span, head_width))
            lse_list.append(log_tot)
        out_columns.append(from_heads(jnp.concatenate(pieces, axis=1)))
    return (jnp.concatenate(out_columns, axis=1), lse_list)


def attention_backward(
    query_low,
    grad_low,
    attended,
    lse_list,
    key_entire,
    value_entire,
    query_tok,
    query_seg,
    key_tok,
    key_seg,
    per_group,
    head_width,
    plans,
):
    group_total = key_entire.shape[1] // head_width
    query_columns = []
    key_columns = []
    value_columns = []
    block_index = 0
    for group_id in range(group_total):
        key_cols = key_entire[:, group_id * head_width : (group_id + 1) * head_width]
        value_cols = value_entire[:, group_id * head_width : (group_id + 1) * head_width]
        stacked_rows = to_heads(query_low, group_id, per_group, head_width)
        grad_stack = to_heads(grad_low, group_id, per_group, head_width)
        out_stack = to_heads(attended, group_id, per_group, head_width)
        pieces = []
        key_sum = jnp.zeros((key_entire.shape[0], head_width), jnp.float32)
        value_sum = jnp.zeros((key_entire.shape[0], head_width), jnp.float32)
        for first_row, span, key_first, key_width in plans:
            key_step = key_step_of()
            key_tiles = key_cols[key_first : key_first + key_width].reshape(
                -1, key_step, head_width
            )
            value_tiles = value_cols[key_first : key_first + key_width].reshape(
                -1, key_step, head_width
            )
            tok_tiles = key_tok[key_first : key_first + key_width].reshape(-1, key_step)
            seg_tiles = key_seg[key_first : key_first + key_width].reshape(-1, key_step)
            grad_part = grad_stack[:, first_row : first_row + span]
            row_delta = jnp.sum(
                grad_part.astype(jnp.float32) * out_stack[:, first_row : first_row + span], axis=2
            )
            query_acc, key_part, value_part = backward_block(
                stacked_rows[:, first_row : first_row + span].reshape(-1, head_width),
                grad_part.reshape(-1, head_width),
                lse_list[block_index],
                row_delta,
                key_tiles,
                value_tiles,
                tok_tiles,
                seg_tiles,
                query_tok[first_row : first_row + span],
                query_seg[first_row : first_row + span],
                per_group,
            )
            block_index += 1
            pieces.append(query_acc.reshape(per_group, span, head_width))
            key_sum = key_sum.at[key_first : key_first + key_width].add(key_part)
            value_sum = value_sum.at[key_first : key_first + key_width].add(value_part)
        query_columns.append(from_heads(jnp.concatenate(pieces, axis=1)))
        key_columns.append(key_sum)
        value_columns.append(value_sum)
    return (
        jnp.concatenate(query_columns, axis=1),
        jnp.concatenate(key_columns, axis=1),
        jnp.concatenate(value_columns, axis=1),
    )


def contract_rows(left_mat, right_mat):
    return lax.dot_general(
        left_mat, right_mat, (((0,), (0,)), ((), ())), preferred_element_type=jnp.float32
    )


def contract_cols(left_mat, right_mat):
    return lax.dot_general(
        left_mat, right_mat, (((1,), (1,)), ((), ())), preferred_element_type=jnp.float32
    )


def shards(
    inputs,
    attn_gain,
    query_weight,
    key_projection,
    value_projection,
    attn_gate_weight,
    output_weight,
    query_gain,
    key_gain,
    ffn_gain,
    ffn_gate_weight,
    ffn_up_weight,
    ffn_down_weight,
    doc_lengths,
    cotangent,
):
    tok_dev = inputs.shape[0]
    head_width = query_gain.shape[0]
    head_count = lax.axis_size("head")
    wide_count = lax.axis_size("wide")
    per_group = query_weight.shape[1] // key_projection.shape[1]
    query_rows = tok_dev * head_count
    total_tok = query_rows * wide_count
    row_len = min(tok_dev * 64, total_tok)
    plans = block_plan(tok_dev, head_count, wide_count, row_len)
    wide_pos = lax.axis_index("wide")
    local_ids = jnp.arange(query_rows, dtype=jnp.int32)
    query_tok = (local_ids // tok_dev * wide_count + wide_pos) * tok_dev + local_ids % tok_dev
    key_tok = jnp.arange(total_tok, dtype=jnp.int32)
    query_seg, query_pos = token_tables(doc_lengths, query_tok)
    key_seg = token_tables(doc_lengths, key_tok)[0]
    cosine, sine_tab = rotary(query_pos, head_width)
    block_in = inputs.astype(jnp.float32)
    normed, input_norm_back = jax.vjp(rms_apply, block_in, attn_gain)
    normed_low = normed.astype(jnp.bfloat16)
    gathered = lax.all_gather(normed_low, "head", axis=0, tiled=True)
    query_pre = jnp.dot(gathered, query_weight, preferred_element_type=jnp.float32)
    key_pre = jnp.dot(gathered, key_projection, preferred_element_type=jnp.float32)
    value_pre = jnp.dot(gathered, value_projection, preferred_element_type=jnp.float32)
    gate_pre = jnp.dot(gathered, attn_gate_weight, preferred_element_type=jnp.float32)

    def prep_heads(pre_proj, gain_vec):
        return head_prep(pre_proj, gain_vec, cosine, sine_tab)

    query_rot, query_back = jax.vjp(prep_heads, query_pre, query_gain)
    key_rot, key_back = jax.vjp(prep_heads, key_pre, key_gain)
    query_low = query_rot.astype(jnp.bfloat16)
    key_low = key_rot.astype(jnp.bfloat16)
    value_low = value_pre.astype(jnp.bfloat16)
    key_wide, value_wide = (
        lax.all_gather(key_low, "wide", axis=0, tiled=True),
        lax.all_gather(value_low, "wide", axis=0, tiled=True),
    )
    kv_width = key_wide.shape[1]

    def natural_order(matrix):
        return (
            matrix.reshape(wide_count, head_count, tok_dev, kv_width)
            .transpose(1, 0, 2, 3)
            .reshape(-1, kv_width)
        )

    def gathered_order(matrix):
        return (
            matrix.reshape(head_count, wide_count, tok_dev, kv_width)
            .transpose(1, 0, 2, 3)
            .reshape(-1, kv_width)
        )

    key_entire = natural_order(key_wide)
    value_entire = natural_order(value_wide)
    attended, lse_list = attention_forward(
        query_low,
        key_entire,
        value_entire,
        query_tok,
        query_seg,
        key_tok,
        key_seg,
        per_group,
        head_width,
        plans,
    )
    gate_sig = jax.nn.sigmoid(gate_pre)
    gated_low = (attended * gate_sig).astype(jnp.bfloat16)
    attn_terms = jnp.dot(gated_low, output_weight, preferred_element_type=jnp.float32)
    attn_out = lax.psum_scatter(
        attn_terms.astype(jnp.bfloat16), "head", scatter_dimension=0, tiled=True
    ).astype(jnp.float32)
    middle = block_in + attn_out
    ffn_normed, ffn_norm_back = jax.vjp(rms_apply, middle, ffn_gain)
    ffn_low = ffn_normed.astype(jnp.bfloat16)
    ffn_rows, cot_rows = (
        lax.all_gather(ffn_low, "wide", axis=0, tiled=True),
        lax.all_gather(cotangent, "wide", axis=0, tiled=True),
    )
    gate_val = jnp.dot(ffn_rows, ffn_gate_weight, preferred_element_type=jnp.float32)
    up_val = jnp.dot(ffn_rows, ffn_up_weight, preferred_element_type=jnp.float32)
    hidden_val, swiglu_back = jax.vjp(swiglu, gate_val, up_val)
    hidden_low = hidden_val.astype(jnp.bfloat16)
    down_terms = jnp.dot(hidden_low, ffn_down_weight, preferred_element_type=jnp.float32)
    ffn_out = lax.psum_scatter(
        down_terms.astype(jnp.bfloat16), "wide", scatter_dimension=0, tiled=True
    ).astype(jnp.float32)
    outputs = (middle + ffn_out).astype(jnp.bfloat16)
    hidden_grad = contract_cols(cot_rows, ffn_down_weight)
    gate_grad, up_grad = swiglu_back(hidden_grad)
    gate_grad_low = gate_grad.astype(jnp.bfloat16)
    up_grad_low = up_grad.astype(jnp.bfloat16)
    down_wgrad = contract_rows(hidden_low, cot_rows)
    gate_wgrad = contract_rows(ffn_rows, gate_grad_low)
    up_wgrad = contract_rows(ffn_rows, up_grad_low)
    ffn_terms = contract_cols(gate_grad_low, ffn_gate_weight) + contract_cols(
        up_grad_low, ffn_up_weight
    )
    ffn_normed_grad = lax.psum_scatter(
        ffn_terms.astype(jnp.bfloat16), "wide", scatter_dimension=0, tiled=True
    ).astype(jnp.float32)
    middle_norm_grad, ffn_gain_part = ffn_norm_back(ffn_normed_grad)
    middle_grad = cotangent.astype(jnp.float32) + middle_norm_grad
    middle_low = middle_grad.astype(jnp.bfloat16)
    back_rows = lax.all_gather(middle_low, "head", axis=0, tiled=True)
    gated_grad = contract_cols(back_rows, output_weight)
    out_wgrad = contract_rows(gated_low, back_rows)
    attended_grad_low = (gated_grad * gate_sig).astype(jnp.bfloat16)
    gate_pre_grad_low = (gated_grad * attended * gate_sig * (1.0 - gate_sig)).astype(jnp.bfloat16)
    query_rot_grad, key_natural, value_natural = attention_backward(
        query_low,
        attended_grad_low,
        attended,
        lse_list,
        key_entire,
        value_entire,
        query_tok,
        query_seg,
        key_tok,
        key_seg,
        per_group,
        head_width,
        plans,
    )
    key_terms = gathered_order(key_natural)
    value_terms = gathered_order(value_natural)
    key_rot_grad, value_sum = (
        lax.psum_scatter(
            key_terms.astype(jnp.bfloat16), "wide", scatter_dimension=0, tiled=True
        ).astype(jnp.float32),
        lax.psum_scatter(
            value_terms.astype(jnp.bfloat16), "wide", scatter_dimension=0, tiled=True
        ).astype(jnp.float32),
    )
    query_pre_grad, query_gain_part = query_back(query_rot_grad)
    key_pre_grad, key_gain_part = key_back(key_rot_grad)
    query_pre_low = query_pre_grad.astype(jnp.bfloat16)
    key_pre_low = key_pre_grad.astype(jnp.bfloat16)
    value_grad_low = value_sum.astype(jnp.bfloat16)
    query_wgrad = contract_rows(gathered, query_pre_low)
    key_wgrad = contract_rows(gathered, key_pre_low)
    value_wgrad = contract_rows(gathered, value_grad_low)
    attn_gate_wgrad = contract_rows(gathered, gate_pre_grad_low)
    normed_terms = (
        contract_cols(query_pre_low, query_weight)
        + contract_cols(key_pre_low, key_projection)
        + contract_cols(value_grad_low, value_projection)
        + contract_cols(gate_pre_grad_low, attn_gate_weight)
    )
    normed_grad = lax.psum_scatter(
        normed_terms.astype(jnp.bfloat16), "head", scatter_dimension=0, tiled=True
    ).astype(jnp.float32)
    input_norm_grad, attn_gain_part = input_norm_back(normed_grad)
    input_grad = middle_grad + input_norm_grad
    query_grad, key_grad, value_grad, attn_gate_grad, output_grad = (
        lax.psum_scatter(
            query_wgrad.astype(jnp.bfloat16), "wide", scatter_dimension=0, tiled=True
        ).astype(jnp.float32),
        lax.psum_scatter(
            key_wgrad.astype(jnp.bfloat16), "wide", scatter_dimension=0, tiled=True
        ).astype(jnp.float32),
        lax.psum_scatter(
            value_wgrad.astype(jnp.bfloat16), "wide", scatter_dimension=0, tiled=True
        ).astype(jnp.float32),
        lax.psum_scatter(
            attn_gate_wgrad.astype(jnp.bfloat16), "wide", scatter_dimension=0, tiled=True
        ).astype(jnp.float32),
        lax.psum_scatter(
            out_wgrad.astype(jnp.bfloat16), "wide", scatter_dimension=1, tiled=True
        ).astype(jnp.float32),
    )
    ffn_gate_grad, ffn_up_grad, ffn_down_grad = (
        lax.psum_scatter(
            gate_wgrad.astype(jnp.bfloat16), "head", scatter_dimension=0, tiled=True
        ).astype(jnp.float32),
        lax.psum_scatter(
            up_wgrad.astype(jnp.bfloat16), "head", scatter_dimension=0, tiled=True
        ).astype(jnp.float32),
        lax.psum_scatter(
            down_wgrad.astype(jnp.bfloat16), "head", scatter_dimension=1, tiled=True
        ).astype(jnp.float32),
    )
    attn_gain_grad, ffn_gain_grad, query_gain_grad, key_gain_grad = lax.psum(
        (attn_gain_part, ffn_gain_part, query_gain_part, key_gain_part), ("head", "wide")
    )
    return (
        outputs,
        input_grad,
        attn_gain_grad,
        query_grad,
        key_grad,
        value_grad,
        attn_gate_grad,
        output_grad,
        query_gain_grad,
        key_gain_grad,
        ffn_gain_grad,
        ffn_gate_grad,
        ffn_up_grad,
        ffn_down_grad,
    )


def solution(mesh):
    placed = (
        P(("head", "wide"), None),
        P(),
        P(None, "head"),
        P(None, "head"),
        P(None, "head"),
        P(None, "head"),
        P("head", None),
        P(),
        P(),
        P(),
        P(None, "wide"),
        P(None, "wide"),
        P("wide", None),
        P(),
        P(("head", "wide"), None),
    )
    return jax.shard_map(
        shards,
        mesh=mesh,
        in_specs=placed,
        out_specs=(
            P(("head", "wide"), None),
            P(("head", "wide"), None),
            P(),
            P("wide", "head"),
            P("wide", "head"),
            P("wide", "head"),
            P("wide", "head"),
            P("head", "wide"),
            P(),
            P(),
            P(),
            P("head", "wide"),
            P("head", "wide"),
            P("wide", "head"),
        ),
        check_vma=False,
    )
```

profile of v0, /device:TPU:0, one launch (start us, length us, event | category | flops | bytes accessed | tf_op | source)
XLA Modules:
  0.0 1061.3 jit_solution(17429723864827085667)
XLA Ops:
  11.8 38.1 %all-gather.7.cloned.1.call-done = bf16[512,2048]{1,0:T(8,128)(2,1)} async-done(((bf16[128,2048]{1,0:T(8,128)(2,1)}), bf16[512,2048]{1,0:T(8,128)(2,1)}) %all-gather.7.cloned.1.call-update) | async-done | bytes 2097168 | tf_op jit(solution)/shard_map/all_gather | solution.py:346
  68.0 14.5 %all-gather.11.cloned.1.call-done = bf16[4096,256]{1,0:T(8,128)(2,1)} async-done(((bf16[512,256]{1,0:T(8,128)(2,1)}), bf16[4096,256]{1,0:T(8,128)(2,1)}) %all-gather.11.cloned.1.call-update) | async-done | bytes 2097168 | tf_op jit(solution)/shard_map/all_gather | solution.py:362
  85.7 27.7 %all-gather.9.cloned.1.call-done = bf16[4096,256]{0,1:T(8,128)(2,1)} async-done(((bf16[512,256]{0,1:T(8,128)(2,1)}), bf16[4096,256]{0,1:T(8,128)(2,1)}) %all-gather.9.cloned.1.call-update) | async-done | bytes 2097168 | tf_op jit(solution)/shard_map/all_gather | solution.py:361
  125.4 31.2 %while.88 = (s32[]{:T(128)}, f32[2,512]{1,0:T(2,128)S(1)}, f32[2,512]{1,0:T(2,128)S(1)}, s32[512]{0:T(512)S(1)}, s32[2,2048]{1,0:T(2,128)S(1)}, /*index=5*/s32[2...) while((s32[]{:T(128)}, f32[2,512]{1,0:T(2,128)S(1)}, ...), condition=%wide.region_16.17_spmd.clone, body=%wide.region_13.16_spmd.clone.sunk | while | flops 554710016 | bytes 43911388 | solution.py:95
  130.9 4.8 fusion.356
  135.7 5.2 exponential_reduce_fusion.5
  146.5 4.8 fusion.356
  151.3 5.2 exponential_reduce_fusion.5
  156.6 23.2 %while.89 = (s32[]{:T(128)}, f32[1024,128]{1,0:T(8,128)}, s32[512]{0:T(512)S(1)}, s32[2,2048]{1,0:T(2,128)S(1)}, s32[2,2048]{1,0:T(2,128)S(1)}, /*index=5*/bf16[...) while((s32[]{:T(128)}, f32[1024,128]{1,0:T(8,128)}, ...), condition=%wide.region_18.19_spmd.clone, body=%wide.region_17.18_spmd.clone.sunk | while | flops 1085546496 | bytes 12914318 | solution.py:112
  162.2 5.9 fusion.363
  173.7 6.1 fusion.363
  181.8 31.5 %while.86 = (s32[]{:T(128)}, f32[2,512]{1,0:T(2,128)S(1)}, f32[2,512]{1,0:T(2,128)S(1)}, s32[512]{0:T(512)S(1)}, s32[2,2048]{1,0:T(2,128)S(1)}, /*index=5*/s32[2...) while((s32[]{:T(128)}, f32[2,512]{1,0:T(2,128)S(1)}, ...), condition=%wide.region_10.11_spmd.clone, body=%wide.region_7.10_spmd.clone.sunk | while | flops 554710016 | bytes 42862784 | solution.py:95
  187.7 4.8 fusion.346
  192.5 5.2 exponential_reduce_fusion.4
  203.3 4.8 fusion.346
  208.1 5.2 exponential_reduce_fusion.4
  213.4 23.0 %while.87 = (s32[]{:T(128)}, f32[1024,128]{1,0:T(8,128)}, s32[512]{0:T(512)S(1)}, s32[2,2048]{1,0:T(2,128)S(1)}, s32[2,2048]{1,0:T(2,128)S(1)}, /*index=5*/bf16[...) while((s32[]{:T(128)}, f32[1024,128]{1,0:T(8,128)}, ...), condition=%wide.region_12.13_spmd.clone, body=%wide.region_11.12_spmd.clone.sunk | while | flops 1085546496 | bytes 12914318 | solution.py:112
  219.0 5.8 fusion.353
  230.4 6.0 fusion.353
  238.5 5.0 multiply_convert_fusion.5
  247.1 34.8 %reduce-scatter.15.cloned.1.call-done = bf16[128,2048]{1,0:T(8,128)(2,1)} async-done(((bf16[512,2048]{1,0:T(8,128)(2,1)}), bf16[128,2048]{1,0:T(8,128)(2,1)}) %reduce-scatter.15.cloned.1.call-update) | async-done | bytes 524304 | tf_op jit(solution)/shard_map/reduce_scatter | solution.py:397
  286.4 46.5 %all-gather.13.cloned.1.call-done = bf16[1024,2048]{1,0:T(8,128)(2,1)} async-done(((bf16[128,2048]{1,0:T(8,128)(2,1)}), bf16[1024,2048]{1,0:T(8,128)(2,1)}) %all-gather.13.cloned.1.call-update) | async-done | bytes 4194320 | tf_op jit(solution)/shard_map/all_gather | solution.py:404
  332.9 8.4 fusion.225
  341.3 5.1 fusion.224
  346.4 33.9 %all-gather.15.cloned.1.call-done = bf16[1024,2048]{1,0:T(8,128)(2,1)} async-done(((bf16[128,2048]{1,0:T(8,128)(2,1)}), bf16[1024,2048]{1,0:T(8,128)(2,1)}) %all-gather.15.cloned.1.call-update) | async-done | bytes 4194320 | tf_op jit(solution)/shard_map/all_gather | solution.py:405
  380.3 9.8 multiply_convert_fusion
  393.6 5.3 add_convert_fusion
  398.9 48.8 %reduce-scatter.19.cloned.1.call-done = bf16[128,2048]{1,0:T(8,128)(2,1)} async-done(((bf16[1024,2048]{1,0:T(8,128)(2,1)}), bf16[128,2048]{1,0:T(8,128)(2,1)}) %reduce-scatter.19.cloned.1.call-update) | async-done | bytes 524304 | tf_op jit(solution)/shard_map/reduce_scatter | solution.py:426
  453.1 33.6 %all-gather.17.cloned.1.call-done = bf16[512,2048]{1,0:T(8,128)(2,1)} async-done(((bf16[128,2048]{1,0:T(8,128)(2,1)}), bf16[512,2048]{1,0:T(8,128)(2,1)}) %all-gather.17.cloned.1.call-update) | async-done | bytes 2097168 | tf_op jit(solution)/shard_map/all_gather | solution.py:432
  486.6 5.0 multiply_convert_fusion.2
  497.4 33.0 %while.91 = (s32[]{:T(128)}, f32[1024,128]{1,0:T(8,128)}, bf16[2,2048,128]{2,1,0:T(8,128)(2,1)}, bf16[2,2048,128]{2,1,0:T(8,128)(2,1)}, s32[512]{0:T(512)S(1)}, ...) while((s32[]{:T(128)}, f32[1024,128]{1,0:T(8,128)}, ...), condition=%wide.region_29.30_spmd.clone, body=%wide.region_28.29_spmd.clone.sunk | while | flops 2710839296 | bytes 87640528 | solution.py:157
  532.7 33.4 %while.90 = (s32[]{:T(128)}, f32[1024,128]{1,0:T(8,128)}, bf16[2,2048,128]{2,1,0:T(8,128)(2,1)}, bf16[2,2048,128]{2,1,0:T(8,128)(2,1)}, s32[512]{0:T(512)S(1)}, ...) while((s32[]{:T(128)}, f32[1024,128]{1,0:T(8,128)}, ...), condition=%wide.region_26.27_spmd.clone, body=%wide.region_25.26_spmd.clone.sunk | while | flops 2710839296 | bytes 86591936 | solution.py:157
  573.0 8.0 convolution_convert_fusion.1
  581.0 8.0 convolution_convert_fusion.2
  589.1 7.9 convolution_convert_fusion.3
  620.1 21.8 %reduce-scatter.21.cloned.1.call-done = bf16[512,256]{1,0:T(8,128)(2,1)} async-done(((bf16[4096,256]{1,0:T(8,128)(2,1)}), bf16[512,256]{1,0:T(8,128)(2,1)}) %reduce-scatter.21.cloned.1.call-update) | async-done | bytes 262160 | tf_op jit(solution)/shard_map/reduce_scatter | solution.py:455
  658.0 6.4 convolution_convert_fusion
  664.5 23.4 %reduce-scatter.41.cloned.1.call-done = bf16[768,512]{1,0:T(8,128)(2,1)} async-done(((bf16[768,2048]{1,0:T(8,128)(2,1)}), bf16[768,512]{1,0:T(8,128)(2,1)}) %reduce-scatter.41.cloned.1.call-update) | async-done | bytes 786448 | tf_op jit(solution)/shard_map/reduce_scatter | solution.py:506
  690.4 44.6 %reduce-scatter.39.cloned.1.call-done = bf16[512,768]{1,0:T(8,128)(2,1)} async-done(((bf16[2048,768]{1,0:T(8,128)(2,1)}), bf16[512,768]{1,0:T(8,128)(2,1)}) %reduce-scatter.39.cloned.1.call-update) | async-done | bytes 786448 | tf_op jit(solution)/shard_map/reduce_scatter | solution.py:503
  737.4 44.8 %reduce-scatter.37.cloned.1.call-done = bf16[512,768]{1,0:T(8,128)(2,1)} async-done(((bf16[2048,768]{1,0:T(8,128)(2,1)}), bf16[512,768]{1,0:T(8,128)(2,1)}) %reduce-scatter.37.cloned.1.call-update) | async-done | bytes 786448 | tf_op jit(solution)/shard_map/reduce_scatter | solution.py:500
  784.6 35.8 %reduce-scatter.35.cloned.1.call-done = bf16[512,256]{1,0:T(8,128)(2,1)} async-done(((bf16[512,2048]{1,0:T(8,128)(2,1)}), bf16[512,256]{1,0:T(8,128)(2,1)}) %reduce-scatter.35.cloned.1.call-update) | async-done | bytes 262160 | tf_op jit(solution)/shard_map/reduce_scatter | solution.py:495
  822.1 35.0 %reduce-scatter.27.cloned.1.call-done = bf16[256,512]{1,0:T(8,128)(2,1)} async-done(((bf16[2048,512]{1,0:T(8,128)(2,1)}), bf16[256,512]{1,0:T(8,128)(2,1)}) %reduce-scatter.27.cloned.1.call-update) | async-done | bytes 262160 | tf_op jit(solution)/shard_map/reduce_scatter | solution.py:483
  858.9 34.9 %reduce-scatter.33.cloned.1.call-done = bf16[256,512]{1,0:T(8,128)(2,1)} async-done(((bf16[2048,512]{1,0:T(8,128)(2,1)}), bf16[256,512]{1,0:T(8,128)(2,1)}) %reduce-scatter.33.cloned.1.call-update) | async-done | bytes 262160 | tf_op jit(solution)/shard_map/reduce_scatter | solution.py:492
  895.6 31.1 %reduce-scatter.31.cloned.1.call-done = bf16[256,256]{1,0:T(8,128)(2,1)} async-done(((bf16[2048,256]{1,0:T(8,128)(2,1)}), bf16[256,256]{1,0:T(8,128)(2,1)}) %reduce-scatter.31.cloned.1.call-update) | async-done | bytes 131088 | tf_op jit(solution)/shard_map/reduce_scatter | solution.py:489
  928.4 31.8 %reduce-scatter.29.cloned.1.call-done = bf16[256,256]{1,0:T(8,128)(2,1)} async-done(((bf16[2048,256]{1,0:T(8,128)(2,1)}), bf16[256,256]{1,0:T(8,128)(2,1)}) %reduce-scatter.29.cloned.1.call-update) | async-done | bytes 131088 | tf_op jit(solution)/shard_map/reduce_scatter | solution.py:486
  961.8 35.4 %reduce-scatter.25.cloned.1.call-done = bf16[128,2048]{1,0:T(8,128)(2,1)} async-done(((bf16[512,2048]{1,0:T(8,128)(2,1)}), bf16[128,2048]{1,0:T(8,128)(2,1)}) %reduce-scatter.25.cloned.1.call-update) | async-done | bytes 524304 | tf_op jit(solution)/shard_map/reduce_scatter | solution.py:477
  999.0 41.5 %all-reduce.4 = (f32[2048]{0:T(1024)}, f32[128]{0:T(128)}, f32[128]{0:T(128)}, f32[2048]{0:T(1024)}) all-reduce(f32[2048]{0:T(1024)S(1)} %get-tuple-element.692, f32[128]{0:T(128)S(1)} %get-tuple-element.690, f32[128]{0:T(128)S(1)} %get-tuple-element.694, f32[2048]{0:T(1024)S(1)} %copy-done.55), channel_id=1, replica_groups=mesh['head'=4,'wide'=8] {'head','wide'}, use_global_device_ids=true, to_apply=%region_37.38 | all-reduce | flops 4352 | bytes 34816 | tf_op jit(solution)/shard_map/psum | solution.py:510
  1040.5 9.9 reduce-scatter.17.cloned.1.call-done
  (472 shorter events, 243.3 us)
Async XLA Ops:
  7.2 373.1 %copy-start = (bf16[768,2048]{1,0:T(8,128)(2,1)S(1)}, bf16[768,2048]{1,0:T(8,128)(2,1)}, u32[]{:S(2)}) copy-start(bf16[768,2048]{1,0:T(8,128)(2,1)} %param.55) | copy-start | bytes 9437188
  7.2 46.1 %copy-start.72 = (s32[1,8]{1,0:T(1,128)S(1)}, s32[1,8]{1,0:T(1,128)}, u32[]{:S(2)}) copy-start(s32[1,8]{1,0:T(1,128)} %param.56) | copy-start | bytes 100
  7.2 42.8 %all-gather.7.cloned.1.call-start = ((), (), s32[]{:S(2)}) async-start(), calls=%async_computation.14 | async-start | bytes 2621440 | tf_op jit(solution)/shard_map/all_gather | solution.py:346
  11.8 42.4 %copy-start.66 = (f32[128]{0:T(128)S(1)}, f32[128]{0:T(128)}, u32[]{:S(2)}) copy-start(f32[128]{0:T(128)} %param.51) | copy-start | bytes 1540
  11.8 70.7 %all-gather.11.cloned.1.call-start = ((), (), s32[]{:S(2)}) async-start(), calls=%async_computation.16 | async-start | bytes 2359296 | tf_op jit(solution)/shard_map/all_gather | solution.py:362
  53.3 60.1 %all-gather.9.cloned.1.call-start = ((), (), s32[]{:S(2)}) async-start(), calls=%async_computation.15 | async-start | bytes 2359296 | tf_op jit(solution)/shard_map/all_gather | solution.py:361
  54.2 8.9 copy-start.19
  58.7 223.2 %reduce-scatter.15.cloned.1.call-start = ((), (), s32[]{:S(2)}) async-start(), calls=%async_computation.17 | async-start | bytes 2621440 | tf_op jit(solution)/shard_map/reduce_scatter | solution.py:397
  236.4 7.2 copy-start.7
  236.4 7.2 copy-start.43
  238.5 5.8 copy-start.77
  244.3 39.0 %copy-start.50 = (f32[2048]{0:T(1024)S(1)}, f32[2048]{0:T(1024)}, u32[]{:S(2)}) copy-start(f32[2048]{0:T(1024)} %param.52) | copy-start | bytes 24580
  247.0 85.9 %all-gather.13.cloned.1.call-start = ((), (), s32[]{:S(2)}) async-start(), calls=%async_computation.18 | async-start | bytes 4718592 | tf_op jit(solution)/shard_map/all_gather | solution.py:404
  283.4 166.8 %copy-start.60 = (f32[128]{0:T(128)}, f32[128]{0:T(128)S(1)}, u32[]{:S(2)}) copy-start(f32[128]{0:T(128)S(1)} %fusion.216) | copy-start | bytes 1540
  285.6 94.7 %all-gather.15.cloned.1.call-start = ((), (), s32[]{:S(2)}) async-start(), calls=%async_computation.20 | async-start | bytes 4718592 | tf_op jit(solution)/shard_map/all_gather | solution.py:405
  286.2 161.6 %reduce-scatter.19.cloned.1.call-start = ((), (), s32[]{:S(2)}) async-start(), calls=%async_computation.21 | async-start | bytes 4718592 | tf_op jit(solution)/shard_map/reduce_scatter | solution.py:426
  332.9 8.4 copy-start.73
  332.9 8.4 copy-start.74
  380.3 9.8 copy-start.75
  398.9 87.7 %all-gather.17.cloned.1.call-start = ((), (), s32[]{:S(2)}) async-start(), calls=%async_computation.22 | async-start | bytes 2621440 | tf_op jit(solution)/shard_map/all_gather | solution.py:432
  450.2 41.4 %copy-start.68 = (f32[128]{0:T(128)}, f32[128]{0:T(128)S(1)}, u32[]{:S(2)}) copy-start(f32[128]{0:T(128)S(1)} %multiply_multiply_fusion.5) | copy-start | bytes 1540
  453.0 163.6 %reduce-scatter.23.cloned.1.call-start = ((), (), s32[]{:S(2)}) async-start(), calls=%async_computation.24 | async-start | bytes 2359296 | tf_op jit(solution)/shard_map/reduce_scatter | solution.py:458
  486.6 5.0 copy-start.37
  497.4 35.3 %copy-start.8 = (bf16[1024,128]{1,0:T(8,128)(2,1)S(1)}, bf16[1024,128]{1,0:T(8,128)(2,1)}, u32[]{:S(2)}) copy-start(bf16[1024,128]{1,0:T(8,128)(2,1)} %copy-done.7) | copy-start | bytes 786436
  497.4 35.3 %copy-start.44 = (f32[2,512]{1,0:T(2,128)S(1)}, f32[2,512]{1,0:T(2,128)}, u32[]{:S(2)}) copy-start(f32[2,512]{1,0:T(2,128)} %copy-done.43) | copy-start | bytes 12292
  569.3 72.6 %reduce-scatter.21.cloned.1.call-start = ((), (), s32[]{:S(2)}) async-start(), calls=%async_computation.23 | async-start | bytes 2359296 | tf_op jit(solution)/shard_map/reduce_scatter | solution.py:455
  572.8 115.1 %reduce-scatter.41.cloned.1.call-start = ((), (), s32[]{:S(2)}) async-start(), calls=%async_computation.33 | async-start | bytes 3932160 | tf_op jit(solution)/shard_map/reduce_scatter | solution.py:506
  581.0 154.0 %reduce-scatter.39.cloned.1.call-start = ((), (), s32[]{:S(2)}) async-start(), calls=%async_computation.32 | async-start | bytes 3932160 | tf_op jit(solution)/shard_map/reduce_scatter | solution.py:503
  589.0 193.2 %reduce-scatter.37.cloned.1.call-start = ((), (), s32[]{:S(2)}) async-start(), calls=%async_computation.31 | async-start | bytes 3932160 | tf_op jit(solution)/shard_map/reduce_scatter | solution.py:500
  597.0 223.3 %reduce-scatter.35.cloned.1.call-start = ((), (), s32[]{:S(2)}) async-start(), calls=%async_computation.30 | async-start | bytes 2359296 | tf_op jit(solution)/shard_map/reduce_scatter | solution.py:495
  601.5 255.6 %reduce-scatter.27.cloned.1.call-start = ((), (), s32[]{:S(2)}) async-start(), calls=%async_computation.26 | async-start | bytes 2359296 | tf_op jit(solution)/shard_map/reduce_scatter | solution.py:483
  601.8 5.8 copy-start.49
  601.8 5.8 copy-start.63
  612.1 281.7 %reduce-scatter.33.cloned.1.call-start = ((), (), s32[]{:S(2)}) async-start(), calls=%async_computation.29 | async-start | bytes 2359296 | tf_op jit(solution)/shard_map/reduce_scatter | solution.py:492
  616.6 310.2 %reduce-scatter.31.cloned.1.call-start = ((), (), s32[]{:S(2)}) async-start(), calls=%async_computation.28 | async-start | bytes 1179648 | tf_op jit(solution)/shard_map/reduce_scatter | solution.py:489
  620.0 25.1 %copy-start.53 = (f32[512,2]{0,1:T(2,128)S(1)}, f32[512,2]{0,1:T(2,128)}, u32[]{:S(2)}) copy-start(f32[512,2]{0,1:T(2,128)} %copy-done.52) | copy-start | bytes 12292
  620.0 25.1 %copy-start.67 = (f32[128]{0:T(128)S(1)}, f32[128]{0:T(128)}, u32[]{:S(2)}) copy-start(f32[128]{0:T(128)} %param.51) | copy-start | bytes 1540
  620.1 26.7 %copy-start.59 = (f32[512,2]{0,1:T(2,128)S(1)}, f32[512,2]{0,1:T(2,128)}, u32[]{:S(2)}) copy-start(f32[512,2]{0,1:T(2,128)} %copy-done.58) | copy-start | bytes 12292
  620.1 340.1 %reduce-scatter.29.cloned.1.call-start = ((), (), s32[]{:S(2)}) async-start(), calls=%async_computation.27 | async-start | bytes 1179648 | tf_op jit(solution)/shard_map/reduce_scatter | solution.py:486
  648.7 348.5 %reduce-scatter.25.cloned.1.call-start = ((), (), s32[]{:S(2)}) async-start(), calls=%async_computation.25 | async-start | bytes 2621440 | tf_op jit(solution)/shard_map/reduce_scatter | solution.py:477
  657.7 392.7 %reduce-scatter.17.cloned.1.call-start = ((), (), s32[]{:S(2)}) async-start(), calls=%async_computation.19 | async-start | bytes 4718592 | tf_op jit(solution)/shard_map/reduce_scatter | solution.py:412
  737.3 259.9 %copy-start.54 = (f32[2048]{0:T(1024)S(1)}, f32[2048]{0:T(1024)}, u32[]{:S(2)}) copy-start(f32[2048]{0:T(1024)} %param.44) | copy-start | bytes 24580
  737.3 259.9 %copy-start.65 = (f32[128]{0:T(128)S(1)}, f32[128]{0:T(128)}, u32[]{:S(2)}) copy-start(f32[128]{0:T(128)} %copy-done.64) | copy-start | bytes 1540
  737.3 261.6 %copy-start.55 = (f32[2048]{0:T(1024)S(1)}, f32[2048]{0:T(1024)}, u32[]{:S(2)}) copy-start(f32[2048]{0:T(1024)} %get-tuple-element.688) | copy-start | bytes 24580
  737.3 303.2 %copy-start.71 = (f32[128]{0:T(128)S(1)}, f32[128]{0:T(128)}, u32[]{:S(2)}) copy-start(f32[128]{0:T(128)} %copy-done.70) | copy-start | bytes 1540
  737.3 313.1 %copy-start.51 = (f32[2048]{0:T(1024)S(1)}, f32[2048]{0:T(1024)}, u32[]{:S(2)}) copy-start(f32[2048]{0:T(1024)} %param.52) | copy-start | bytes 24580
  737.4 313.1 %copy-start.61 = (f32[128]{0:T(128)S(1)}, f32[128]{0:T(128)}, u32[]{:S(2)}) copy-start(f32[128]{0:T(128)} %copy-done.60) | copy-start | bytes 1540
  737.4 313.0 %copy-start.69 = (f32[128]{0:T(128)S(1)}, f32[128]{0:T(128)}, u32[]{:S(2)}) copy-start(f32[128]{0:T(128)} %copy-done.68) | copy-start | bytes 1540
  (79 other events, 196.0 us)
Sparse Core Ops, SparseCore 0:
  11.9 38.0 all-gather.6
  53.4 29.0 all-gather.10
  84.6 28.6 all-gather.8
  247.1 34.7 reduce-scatter.14
  285.7 47.1 all-gather.12
  334.4 45.8 all-gather.14
  399.0 48.7 reduce-scatter.18
  453.1 33.4 all-gather.16
  569.5 35.7 reduce-scatter.22
  607.5 34.3 reduce-scatter.20
  645.2 42.6 reduce-scatter.40
  691.0 43.9 reduce-scatter.38
  738.2 43.9 reduce-scatter.36
  784.4 35.8 reduce-scatter.34
  822.6 34.4 reduce-scatter.26
  859.4 34.4 reduce-scatter.32
  896.0 30.6 reduce-scatter.30
  929.5 30.6 reduce-scatter.28
  963.4 33.7 reduce-scatter.24
  999.3 51.0 reduce-scatter.16
where the time goes:
time: 1070 us; the launch traced here: 1060 us
  waiting for transfers between devices  627 us (59%)
  matrix products  191 us (18%)
  local copies, waits for them, and re-layouts  105 us (10%)
  other arithmetic  77.6 us (7%)
  blocking collectives  41.5 us (4%)
  between operations  15.4 us (1%)
    broadcast_in_dim x24, local copies, waits for them, and re-layouts, score_tile(): return jnp.where(allowed[None], scores, NEG)  54.4 us
    reduce_scatter x1, waiting for transfers between devices, shards(): lax.psum_scatter(ffn_terms.astype(jnp.bfloat16), 'wide', scatter_dimensio...  48.8 us
    all_gather x1, waiting for transfers between devices, shards(): lax.all_gather(ffn_low, 'wide', axis=0, tiled=True)  46.5 us
    reduce_scatter x1, waiting for transfers between devices, shards(): lax.psum_scatter(gate_wgrad.astype(jnp.bfloat16), 'head', scatter_dimensi...  44.8 us
    reduce_scatter x1, waiting for transfers between devices, shards(): lax.psum_scatter(up_wgrad.astype(jnp.bfloat16), 'head', scatter_dimension...  44.6 us
    psum x1, blocking collectives, shards(): lax.psum((attn_gain_part, ffn_gain_part, query_gain_part, key_gain_part),...  41.5 us
    dot_general x8, matrix products, contract_rows(): lax.dot_general(left_mat, right_mat, (((0,), (0,)), ((), ())), preferred_...  40.4 us
    all_gather x1, waiting for transfers between devices, shards(): gathered = lax.all_gather(normed_low, 'head', axis=0, tiled=True)  38.1 us
  transfers between devices with their start and end apart: 20, of which 19 were waited for; matrix products, arithmetic and copies ran while one was open for 11% of the time, Pallas kernels for 0%

commit v1 on v0

v1 whole, which is shorter than its diff:
```python
import jax
import jax.numpy as jnp
from jax import lax
from jax.experimental import pallas as pl
from jax.experimental.pallas import tpu as pltpu
from jax.sharding import PartitionSpec as P

EPS = 1e-06
THETA = 1000000.0
VMEM_LIMIT = 56 << 20


def rms_apply(values, gain_vec):
    return values * lax.rsqrt(jnp.mean(values * values, axis=-1, keepdims=True) + EPS) * gain_vec


def token_tables(doc_lengths, token_ids):
    lengths = doc_lengths.reshape(-1)
    doc_ends = jnp.cumsum(lengths)
    before = doc_ends[None, :] <= token_ids[:, None]
    document_segment = jnp.sum(before.astype(jnp.int32), axis=1)
    doc_first = jnp.sum(jnp.where(before, lengths[None, :], 0), axis=1)
    return (document_segment, token_ids - doc_first, doc_first)


def rotary(position, head_width):
    half_width = head_width // 2
    inverse = THETA ** (-(jnp.arange(half_width, dtype=jnp.float32) * 2.0 / head_width))
    angles = position.astype(jnp.float32)[:, None] * inverse[None, :]
    cosine = jnp.cos(angles)
    sine_tab = jnp.sin(angles)
    return (
        jnp.concatenate([cosine, cosine], axis=1),
        jnp.concatenate([sine_tab, sine_tab], axis=1),
    )


def head_prep(pre_proj, gain_vec, cosine, sine_tab):
    row_count = pre_proj.shape[0]
    head_width = gain_vec.shape[0]
    half_width = head_width // 2
    per_head = rms_apply(pre_proj.reshape(row_count, -1, head_width), gain_vec)
    turned = jnp.concatenate([-per_head[..., half_width:], per_head[..., :half_width]], axis=-1)
    rotated = per_head * cosine[:, None, :] + turned * sine_tab[:, None, :]
    return rotated.reshape(row_count, -1)


def swiglu(gate_in, up_in):
    return jax.nn.silu(gate_in) * up_in


LANES = 128
KEY_BLOCK = 512
LOG2E = 1.4426950408889634


def attention_forward_kernel(
    start_ref, query_ref, key_ref, value_ref, first_ref, gate_ref, att_ref, inv_ref, gated_ref, acc
):
    blocks = start_ref.shape[0]
    groups = key_ref.shape[1] // LANES
    per = query_ref.shape[1] // key_ref.shape[1]
    rows = query_ref.shape[0] // blocks
    wide_count = key_ref.shape[0] // query_ref.shape[0]
    wide_pos = lax.axis_index("wide")
    step = KEY_BLOCK
    factor = LANES ** (-0.5) * LOG2E

    @pl.loop(0, blocks)
    def _(blk):
        here = pl.ds(pl.multiple_of(blk * rows, rows), rows)
        first_tok = (blk * wide_count + wide_pos) * rows
        key_lane = lax.broadcasted_iota(jnp.int32, (rows, step), 1)
        query_row = lax.broadcasted_iota(jnp.int32, (rows, step), 0) + first_tok
        upper = key_lane - query_row
        lower = key_lane - first_ref[here, :]
        queries = [
            jnp.concatenate(
                [
                    query_ref[here, (g * per + j) * LANES : (g * per + j + 1) * LANES]
                    for j in range(per)
                ],
                axis=0,
            )
            for g in range(groups)
        ]
        acc[...] = jnp.zeros_like(acc)

        @pl.loop(start_ref[blk] // step, (first_tok + rows + step - 1) // step)
        def _(tile):
            base = tile * step
            there = pl.ds(pl.multiple_of(base, step), step)
            allowed = (upper <= -base) & (lower >= -base)
            allowed = jnp.concatenate([allowed] * per, axis=0)
            for g in range(groups):
                cols = slice(g * LANES, (g + 1) * LANES)
                scores = lax.dot_general(
                    queries[g], key_ref[there, cols], (((1,), (1,)), ((), ())),
                    preferred_element_type=jnp.float32,
                )
                probs = jnp.where(allowed, jnp.exp2(scores * factor), 0.0).astype(jnp.bfloat16)
                values = jnp.concatenate(
                    [value_ref[there, cols], jnp.ones((step, LANES), jnp.bfloat16)], axis=1
                )
                acc[g] += jnp.dot(probs, values, preferred_element_type=jnp.float32)

        for g in range(groups):
            for j in range(per):
                part = acc[g, j * rows : (j + 1) * rows, :]
                cols = slice((g * per + j) * LANES, (g * per + j + 1) * LANES)
                inverse = 1.0 / part[:, LANES:]
                out = part[:, :LANES] * inverse
                att_ref[here, cols] = out
                inv_ref[here, cols] = inverse
                gated_ref[here, cols] = (out * jax.nn.sigmoid(gate_ref[here, cols])).astype(
                    jnp.bfloat16
                )


def attention_forward(query_low, key_all, value_all, starts, firsts, gate_pre):
    rows, width = query_low.shape
    groups = key_all.shape[1] // LANES
    per = width // key_all.shape[1]
    blocks = starts.shape[0]
    vmem = pl.BlockSpec(memory_space=pltpu.VMEM)
    return pl.pallas_call(
        attention_forward_kernel,
        out_shape=(
            jax.ShapeDtypeStruct((rows, width), jnp.float32),
            jax.ShapeDtypeStruct((rows, width), jnp.float32),
            jax.ShapeDtypeStruct((rows, width), jnp.bfloat16),
        ),
        in_specs=[pl.BlockSpec(memory_space=pltpu.SMEM)] + [vmem] * 5,
        out_specs=(vmem, vmem, vmem),
        scratch_shapes=[pltpu.VMEM((groups, per * (rows // blocks), 2 * LANES), jnp.float32)],
        compiler_params=pltpu.CompilerParams(vmem_limit_bytes=VMEM_LIMIT),
        cost_estimate=pl.CostEstimate(
            flops=4 * rows * width * 2048, bytes_accessed=12 << 20, transcendentals=0
        ),
        name="attention_forward",
    )(starts, query_low, key_all, value_all, firsts, gate_pre)


def attention_backward_kernel(
    start_ref, query_ref, grad_ref, att_ref, inv_ref, key_ref, keyt_ref, value_ref, first_ref,
    dq_ref, dk_ref, dv_ref, dk_acc, dv_acc, dqt,
):
    blocks = start_ref.shape[0]
    groups = key_ref.shape[1] // LANES
    per = query_ref.shape[1] // key_ref.shape[1]
    rows = query_ref.shape[0] // blocks
    wide_count = key_ref.shape[0] // query_ref.shape[0]
    wide_pos = lax.axis_index("wide")
    step = KEY_BLOCK
    scale = LANES ** (-0.5)
    dk_acc[...] = jnp.zeros_like(dk_acc)
    dv_acc[...] = jnp.zeros_like(dv_acc)

    @pl.loop(0, blocks)
    def _(blk):
        here = pl.ds(pl.multiple_of(blk * rows, rows), rows)
        first_tok = (blk * wide_count + wide_pos) * rows
        key_row = lax.broadcasted_iota(jnp.int32, (step, rows), 0)
        query_lane = lax.broadcasted_iota(jnp.int32, (step, rows), 1) + first_tok
        upper = key_row - query_lane
        lower = key_row - jnp.transpose(
            jnp.broadcast_to(first_ref[here, :], (rows, LANES))
        )[0:1, :]
        queries, grads, deltas = [], [], []
        for g in range(groups):
            qs, gs, ds = [], [], []
            for j in range(per):
                cols = slice((g * per + j) * LANES, (g * per + j + 1) * LANES)
                grad = grad_ref[here, cols].astype(jnp.float32)
                inverse = inv_ref[here, cols]
                both = grad * inverse
                delta = jnp.sum(both * att_ref[here, cols], axis=1, keepdims=True)
                ds.append(jnp.transpose(jnp.broadcast_to(delta, (rows, LANES)))[0:1, :])
                qs.append(query_ref[here, cols])
                gs.append(both.astype(jnp.bfloat16))
            queries.append(jnp.concatenate(qs, axis=0))
            grads.append(jnp.concatenate(gs, axis=0))
            deltas.append(jnp.concatenate(ds, axis=1))
        dqt[...] = jnp.zeros_like(dqt)

        @pl.loop(start_ref[blk] // step, (first_tok + rows + step - 1) // step)
        def _(tile):
            base = tile * step
            there = pl.ds(pl.multiple_of(base, step), step)
            allowed = (upper <= -base) & (lower >= -base)
            allowed = jnp.concatenate([allowed] * per, axis=1)
            for g in range(groups):
                cols = slice(g * LANES, (g + 1) * LANES)
                scores = lax.dot_general(
                    key_ref[there, cols], queries[g], (((1,), (1,)), ((), ())),
                    preferred_element_type=jnp.float32,
                )
                probs = jnp.where(allowed, jnp.exp2(scores * (scale * LOG2E)), 0.0)
                dprobs = lax.dot_general(
                    value_ref[there, cols], grads[g], (((1,), (1,)), ((), ())),
                    preferred_element_type=jnp.float32,
                )
                dscores = (probs * (dprobs - deltas[g]) * scale).astype(jnp.bfloat16)
                dv_acc[there, cols] += jnp.dot(
                    probs.astype(jnp.bfloat16), grads[g], preferred_element_type=jnp.float32
                )
                dk_acc[there, cols] += jnp.dot(
                    dscores, queries[g], preferred_element_type=jnp.float32
                )
                dqt[g] += jnp.dot(
                    keyt_ref[cols, there], dscores, preferred_element_type=jnp.float32
                )

        for g in range(groups):
            for j in range(per):
                cols = slice((g * per + j) * LANES, (g * per + j + 1) * LANES)
                dq_ref[here, cols] = jnp.transpose(dqt[g, :, j * rows : (j + 1) * rows])

    dk_ref[...] = dk_acc[...].astype(dk_ref.dtype)
    dv_ref[...] = dv_acc[...].astype(dv_ref.dtype)


def attention_backward(
    query_low, grad_low, attended, inverse, key_all, value_all, starts, firsts
):
    rows, width = query_low.shape
    keys, kv_width = key_all.shape
    groups = kv_width // LANES
    per = width // kv_width
    blocks = starts.shape[0]
    vmem = pl.BlockSpec(memory_space=pltpu.VMEM)
    return pl.pallas_call(
        attention_backward_kernel,
        out_shape=(
            jax.ShapeDtypeStruct((rows, width), jnp.float32),
            jax.ShapeDtypeStruct((keys, kv_width), jnp.bfloat16),
            jax.ShapeDtypeStruct((keys, kv_width), jnp.bfloat16),
        ),
        in_specs=[pl.BlockSpec(memory_space=pltpu.SMEM)] + [vmem] * 8,
        out_specs=(vmem, vmem, vmem),
        scratch_shapes=[
            pltpu.VMEM((keys, kv_width), jnp.float32),
            pltpu.VMEM((keys, kv_width), jnp.float32),
            pltpu.VMEM((groups, LANES, per * (rows // blocks)), jnp.float32),
        ],
        compiler_params=pltpu.CompilerParams(vmem_limit_bytes=VMEM_LIMIT),
        cost_estimate=pl.CostEstimate(
            flops=10 * rows * width * 2048, bytes_accessed=20 << 20, transcendentals=0
        ),
        name="attention_backward",
    )(starts, query_low, grad_low, attended, inverse, key_all, key_all.T, value_all, firsts)


def contract_rows(left_mat, right_mat):
    return lax.dot_general(
        left_mat, right_mat, (((0,), (0,)), ((), ())), preferred_element_type=jnp.float32
    )


def contract_cols(left_mat, right_mat):
    return lax.dot_general(
        left_mat, right_mat, (((1,), (1,)), ((), ())), preferred_element_type=jnp.float32
    )


def shards(
    inputs,
    attn_gain,
    query_weight,
    key_projection,
    value_projection,
    attn_gate_weight,
    output_weight,
    query_gain,
    key_gain,
    ffn_gain,
    ffn_gate_weight,
    ffn_up_weight,
    ffn_down_weight,
    doc_lengths,
    cotangent,
):
    tok_dev = inputs.shape[0]
    head_width = query_gain.shape[0]
    head_count = lax.axis_size("head")
    wide_count = lax.axis_size("wide")
    query_rows = tok_dev * head_count
    wide_pos = lax.axis_index("wide")
    local_ids = jnp.arange(query_rows, dtype=jnp.int32)
    query_tok = (local_ids // tok_dev * wide_count + wide_pos) * tok_dev + local_ids % tok_dev
    query_seg, query_pos, query_first = token_tables(doc_lengths, query_tok)
    starts = query_first[::tok_dev]
    firsts = query_first[:, None]
    cosine, sine_tab = rotary(query_pos, head_width)
    block_in = inputs.astype(jnp.float32)
    normed, input_norm_back = jax.vjp(rms_apply, block_in, attn_gain)
    normed_low = normed.astype(jnp.bfloat16)
    gathered = lax.all_gather(normed_low, "head", axis=0, tiled=True)
    query_pre = jnp.dot(gathered, query_weight, preferred_element_type=jnp.float32)
    key_pre = jnp.dot(gathered, key_projection, preferred_element_type=jnp.float32)
    value_pre = jnp.dot(gathered, value_projection, preferred_element_type=jnp.float32)
    gate_pre = jnp.dot(gathered, attn_gate_weight, preferred_element_type=jnp.float32)

    def prep_heads(pre_proj, gain_vec):
        return head_prep(pre_proj, gain_vec, cosine, sine_tab)

    query_rot, query_back = jax.vjp(prep_heads, query_pre, query_gain)
    key_rot, key_back = jax.vjp(prep_heads, key_pre, key_gain)
    query_low = query_rot.astype(jnp.bfloat16)
    key_low = key_rot.astype(jnp.bfloat16)
    value_low = value_pre.astype(jnp.bfloat16)
    key_wide, value_wide = (
        lax.all_gather(key_low, "wide", axis=0, tiled=True),
        lax.all_gather(value_low, "wide", axis=0, tiled=True),
    )
    kv_width = key_wide.shape[1]

    def natural_order(matrix):
        return (
            matrix.reshape(wide_count, head_count, tok_dev, kv_width)
            .transpose(1, 0, 2, 3)
            .reshape(-1, kv_width)
        )

    def gathered_order(matrix):
        return (
            matrix.reshape(head_count, wide_count, tok_dev, kv_width)
            .transpose(1, 0, 2, 3)
            .reshape(-1, kv_width)
        )

    key_entire = natural_order(key_wide)
    value_entire = natural_order(value_wide)
    attended, inverse, gated_low = attention_forward(
        query_low, key_entire, value_entire, starts, firsts, gate_pre
    )
    gate_sig = jax.nn.sigmoid(gate_pre)
    attn_terms = jnp.dot(gated_low, output_weight, preferred_element_type=jnp.float32)
    attn_out = lax.psum_scatter(
        attn_terms.astype(jnp.bfloat16), "head", scatter_dimension=0, tiled=True
    ).astype(jnp.float32)
    middle = block_in + attn_out
    ffn_normed, ffn_norm_back = jax.vjp(rms_apply, middle, ffn_gain)
    ffn_low = ffn_normed.astype(jnp.bfloat16)
    ffn_rows, cot_rows = (
        lax.all_gather(ffn_low, "wide", axis=0, tiled=True),
        lax.all_gather(cotangent, "wide", axis=0, tiled=True),
    )
    gate_val = jnp.dot(ffn_rows, ffn_gate_weight, preferred_element_type=jnp.float32)
    up_val = jnp.dot(ffn_rows, ffn_up_weight, preferred_element_type=jnp.float32)
    hidden_val, swiglu_back = jax.vjp(swiglu, gate_val, up_val)
    hidden_low = hidden_val.astype(jnp.bfloat16)
    down_terms = jnp.dot(hidden_low, ffn_down_weight, preferred_element_type=jnp.float32)
    ffn_out = lax.psum_scatter(
        down_terms.astype(jnp.bfloat16), "wide", scatter_dimension=0, tiled=True
    ).astype(jnp.float32)
    outputs = (middle + ffn_out).astype(jnp.bfloat16)
    hidden_grad = contract_cols(cot_rows, ffn_down_weight)
    gate_grad, up_grad = swiglu_back(hidden_grad)
    gate_grad_low = gate_grad.astype(jnp.bfloat16)
    up_grad_low = up_grad.astype(jnp.bfloat16)
    down_wgrad = contract_rows(hidden_low, cot_rows)
    gate_wgrad = contract_rows(ffn_rows, gate_grad_low)
    up_wgrad = contract_rows(ffn_rows, up_grad_low)
    ffn_terms = contract_cols(gate_grad_low, ffn_gate_weight) + contract_cols(
        up_grad_low, ffn_up_weight
    )
    ffn_normed_grad = lax.psum_scatter(
        ffn_terms.astype(jnp.bfloat16), "wide", scatter_dimension=0, tiled=True
    ).astype(jnp.float32)
    middle_norm_grad, ffn_gain_part = ffn_norm_back(ffn_normed_grad)
    middle_grad = cotangent.astype(jnp.float32) + middle_norm_grad
    middle_low = middle_grad.astype(jnp.bfloat16)
    back_rows = lax.all_gather(middle_low, "head", axis=0, tiled=True)
    gated_grad = contract_cols(back_rows, output_weight)
    out_wgrad = contract_rows(gated_low, back_rows)
    attended_grad_low = (gated_grad * gate_sig).astype(jnp.bfloat16)
    gate_pre_grad_low = (gated_grad * attended * gate_sig * (1.0 - gate_sig)).astype(jnp.bfloat16)
    query_rot_grad, key_natural, value_natural = attention_backward(
        query_low, attended_grad_low, attended, inverse, key_entire, value_entire, starts, firsts
    )
    key_terms = gathered_order(key_natural)
    value_terms = gathered_order(value_natural)
    key_rot_grad, value_sum = (
        lax.psum_scatter(
            key_terms.astype(jnp.bfloat16), "wide", scatter_dimension=0, tiled=True
        ).astype(jnp.float32),
        lax.psum_scatter(
            value_terms.astype(jnp.bfloat16), "wide", scatter_dimension=0, tiled=True
        ).astype(jnp.float32),
    )
    query_pre_grad, query_gain_part = query_back(query_rot_grad)
    key_pre_grad, key_gain_part = key_back(key_rot_grad)
    query_pre_low = query_pre_grad.astype(jnp.bfloat16)
    key_pre_low = key_pre_grad.astype(jnp.bfloat16)
    value_grad_low = value_sum.astype(jnp.bfloat16)
    query_wgrad = contract_rows(gathered, query_pre_low)
    key_wgrad = contract_rows(gathered, key_pre_low)
    value_wgrad = contract_rows(gathered, value_grad_low)
    attn_gate_wgrad = contract_rows(gathered, gate_pre_grad_low)
    normed_terms = (
        contract_cols(query_pre_low, query_weight)
        + contract_cols(key_pre_low, key_projection)
        + contract_cols(value_grad_low, value_projection)
        + contract_cols(gate_pre_grad_low, attn_gate_weight)
    )
    normed_grad = lax.psum_scatter(
        normed_terms.astype(jnp.bfloat16), "head", scatter_dimension=0, tiled=True
    ).astype(jnp.float32)
    input_norm_grad, attn_gain_part = input_norm_back(normed_grad)
    input_grad = middle_grad + input_norm_grad
    query_grad, key_grad, value_grad, attn_gate_grad, output_grad = (
        lax.psum_scatter(
            query_wgrad.astype(jnp.bfloat16), "wide", scatter_dimension=0, tiled=True
        ).astype(jnp.float32),
        lax.psum_scatter(
            key_wgrad.astype(jnp.bfloat16), "wide", scatter_dimension=0, tiled=True
        ).astype(jnp.float32),
        lax.psum_scatter(
            value_wgrad.astype(jnp.bfloat16), "wide", scatter_dimension=0, tiled=True
        ).astype(jnp.float32),
        lax.psum_scatter(
            attn_gate_wgrad.astype(jnp.bfloat16), "wide", scatter_dimension=0, tiled=True
        ).astype(jnp.float32),
        lax.psum_scatter(
            out_wgrad.astype(jnp.bfloat16), "wide", scatter_dimension=1, tiled=True
        ).astype(jnp.float32),
    )
    ffn_gate_grad, ffn_up_grad, ffn_down_grad = (
        lax.psum_scatter(
            gate_wgrad.astype(jnp.bfloat16), "head", scatter_dimension=0, tiled=True
        ).astype(jnp.float32),
        lax.psum_scatter(
            up_wgrad.astype(jnp.bfloat16), "head", scatter_dimension=0, tiled=True
        ).astype(jnp.float32),
        lax.psum_scatter(
            down_wgrad.astype(jnp.bfloat16), "head", scatter_dimension=1, tiled=True
        ).astype(jnp.float32),
    )
    attn_gain_grad, ffn_gain_grad, query_gain_grad, key_gain_grad = lax.psum(
        (attn_gain_part, ffn_gain_part, query_gain_part, key_gain_part), ("head", "wide")
    )
    return (
        outputs,
        input_grad,
        attn_gain_grad,
        query_grad,
        key_grad,
        value_grad,
        attn_gate_grad,
        output_grad,
        query_gain_grad,
        key_gain_grad,
        ffn_gain_grad,
        ffn_gate_grad,
        ffn_up_grad,
        ffn_down_grad,
    )


def solution(mesh):
    placed = (
        P(("head", "wide"), None),
        P(),
        P(None, "head"),
        P(None, "head"),
        P(None, "head"),
        P(None, "head"),
        P("head", None),
        P(),
        P(),
        P(),
        P(None, "wide"),
        P(None, "wide"),
        P("wide", None),
        P(),
        P(("head", "wide"), None),
    )
    return jax.shard_map(
        shards,
        mesh=mesh,
        in_specs=placed,
        out_specs=(
            P(("head", "wide"), None),
            P(("head", "wide"), None),
            P(),
            P("wide", "head"),
            P("wide", "head"),
            P("wide", "head"),
            P("wide", "head"),
            P("head", "wide"),
            P(),
            P(),
            P(),
            P("head", "wide"),
            P("head", "wide"),
            P("wide", "head"),
        ),
        check_vma=False,
    )
```

time: 1070 us -> 908 us (0.85)
  matrix products: 191 us -> 108 us
  local copies, waits for them, and re-layouts: 105 us -> 48.2 us
  other arithmetic: 77.6 us -> 45.2 us
  Pallas kernels: 0 us -> 28.7 us
  waiting for transfers between devices: 627 us -> 607 us
    dot_general x28 -> x0, matrix products: 82.3 us -> none  [the longest x8 24.1 us: score_tile(): lax.dot_general(query_blk, key_tile, (((1,), (1,)), ((), ())), preferred_...]
    broadcast_in_dim x24 -> x0, local copies, waits for them, and re-layouts: 54.4 us -> none  [score_tile(): return jnp.where(allowed[None], scores, NEG)]
    pallas_call x0 -> x2, Pallas kernels: none -> 28.7 us  [the longest x1 17.3 us: attention_backward(): pl.pallas_call(attention_backward_kernel, out_shape=(jax.ShapeDtypeStruct...]
    reduce_scatter x1, waiting for transfers between devices: 21.8 us -> 0.02 us  [shards(): lax.psum_scatter(key_terms.astype(jnp.bfloat16), 'wide', scatter_dimensio...]
    reduce_sum x6 -> x0, other arithmetic: 21.1 us -> none  [the longest x4 20.8 us: first_pass(): jnp.sum(jnp.exp(scores - new_max[..., None]), axis=2)]
    reduce_scatter x1, waiting for transfers between devices: 0.02 us -> 17.8 us  [shards(): lax.psum_scatter(value_terms.astype(jnp.bfloat16), 'wide', scatter_dimens...]
    all_gather x1, waiting for transfers between devices: 14.5 us -> 0.01 us  [shards(): lax.all_gather(value_low, 'wide', axis=0, tiled=True)]
    and x12 -> x0, other arithmetic: 11 us -> none  [allowed_tile(): (query_seg[:, None] == tile_seg[None, :]) & (tile_tok[None, :] <= query_t...]
  transfers between devices with their start and end apart: 20 -> 20, of which waited for: 19 -> 18; matrix products, arithmetic and copies ran while one was open for 11% -> 15% of each run, Pallas kernels for 0% -> 0%
where the time goes in v1:
time: 908 us; the launch traced here: 895 us
  waiting for transfers between devices  607 us (67%)
  matrix products  108 us (12%)
  local copies, waits for them, and re-layouts  48.2 us (5%)
  other arithmetic  45.2 us (5%)
  blocking collectives  41.6 us (5%)
  Pallas kernels  28.7 us (3%)
  between operations  15.1 us (2%)
    reduce_scatter x1, waiting for transfers between devices, shards(): lax.psum_scatter(ffn_terms.astype(jnp.bfloat16), 'wide', scatter_dimensio...  48.8 us
    all_gather x1, waiting for transfers between devices, shards(): lax.all_gather(ffn_low, 'wide', axis=0, tiled=True)  46.2 us
    reduce_scatter x1, waiting for transfers between devices, shards(): lax.psum_scatter(gate_wgrad.astype(jnp.bfloat16), 'head', scatter_dimensi...  44.8 us
    reduce_scatter x1, waiting for transfers between devices, shards(): lax.psum_scatter(up_wgrad.astype(jnp.bfloat16), 'head', scatter_dimension...  44.6 us
    psum x1, blocking collectives, shards(): lax.psum((attn_gain_part, ffn_gain_part, query_gain_part, key_gain_part),...  41.6 us
    dot_general x8, matrix products, contract_rows(): lax.dot_general(left_mat, right_mat, (((0,), (0,)), ((), ())), preferred_...  40.4 us
    all_gather x1, waiting for transfers between devices, shards(): gathered = lax.all_gather(normed_low, 'head', axis=0, tiled=True)  38.1 us
    reduce_scatter x1, waiting for transfers between devices, shards(): lax.psum_scatter(out_wgrad.astype(jnp.bfloat16), 'wide', scatter_dimensio...  35.6 us
  transfers between devices with their start and end apart: 20, of which 18 were waited for; matrix products, arithmetic and copies ran while one was open for 15% of the time, Pallas kernels for 0%

profile of v1, /device:TPU:0, one launch (start us, length us, event | category | flops | bytes accessed | tf_op | source)
XLA Modules:
  0.0 895.5 jit_solution(2600941748247977463)
XLA Ops:
  11.8 38.1 %all-gather.7.cloned.1.call-done = bf16[512,2048]{1,0:T(8,128)(2,1)} async-done(((bf16[128,2048]{1,0:T(8,128)(2,1)}), bf16[512,2048]{1,0:T(8,128)(2,1)}) %all-gather.7.cloned.1.call-update) | async-done | bytes 2097168 | tf_op jit(solution)/shard_map/all_gather | solution.py:298
  49.9 3.3 convolution_convert_fusion.10
  54.2 2.7 multiply_reduce_fusion.6
  64.7 4.5 multiply_reduce_fusion.3
  80.6 3.6 add_convert_fusion.3.query_ref
  86.5 3.2 copy.76
  89.7 23.5 %all-gather.9.cloned.1.call-done = bf16[4096,256]{0,1:T(8,128)(2,1)} async-done(((bf16[512,256]{0,1:T(8,128)(2,1)}), bf16[4096,256]{0,1:T(8,128)(2,1)}) %all-gather.9.cloned.1.call-update) | async-done | bytes 2097168 | tf_op jit(solution)/shard_map/all_gather | solution.py:313
  113.2 4.4 reshape.232
  121.9 4.1 copy.77.key_ref
  126.0 11.3 %attention_forward.1 = (f32[512,512]{1,0:T(8,128)}, f32[512,512]{1,0:T(8,128)}, bf16[512,512]{1,0:T(8,128)(2,1)}) custom-call(s32[4]{0:T(128)} %slice.15.start_ref, bf16[512,512]{1,0:T(8,128)(2,1)} %add_convert_fusion.3.query_ref, bf16[4096,256]{1,0:T(8,128)(2,1)} %copy.77.key_ref, bf16[4096,256]{1,0:T(8,128)(2,1)} %bitcast.130, s32[512,1]{1,0:T(8,128)} %copy.78.first_ref, ...), custom_call_target="tpu_custom_call" | custom-call | flops 2147483648 | bytes 12582912 | tf_op jit(solution)/shard_map/attention_forward/pallas_call | solution.py:126
  137.3 3.6 convolution_convert_fusion.7
  141.0 34.4 %reduce-scatter.15.cloned.1.call-done = bf16[128,2048]{1,0:T(8,128)(2,1)} async-done(((bf16[512,2048]{1,0:T(8,128)(2,1)}), bf16[128,2048]{1,0:T(8,128)(2,1)}) %reduce-scatter.15.cloned.1.call-update) | async-done | bytes 524304 | tf_op jit(solution)/shard_map/reduce_scatter | solution.py:339
  180.1 46.2 %all-gather.13.cloned.1.call-done = bf16[1024,2048]{1,0:T(8,128)(2,1)} async-done(((bf16[128,2048]{1,0:T(8,128)(2,1)}), bf16[1024,2048]{1,0:T(8,128)(2,1)}) %all-gather.13.cloned.1.call-update) | async-done | bytes 4194320 | tf_op jit(solution)/shard_map/all_gather | solution.py:346
  226.3 8.4 fusion.41
  234.8 5.1 fusion.40
  239.9 33.9 %all-gather.15.cloned.1.call-done = bf16[1024,2048]{1,0:T(8,128)(2,1)} async-done(((bf16[128,2048]{1,0:T(8,128)(2,1)}), bf16[1024,2048]{1,0:T(8,128)(2,1)}) %all-gather.15.cloned.1.call-update) | async-done | bytes 4194320 | tf_op jit(solution)/shard_map/all_gather | solution.py:347
  273.8 9.8 %multiply_convert_fusion = (bf16[1024,768]{1,0:T(8,128)(2,1)S(1)}, bf16[1024,768]{1,0:T(8,128)(2,1)S(1)}, bf16[1024,768]{1,0:T(8,128)(2,1)}) fusion(f32[1024,768]{1,0:T(8,128)} %fusion.40, f32[1024,768]{1,0:T(8,128)} %fusion.41, bf16[1024,2048]{1,0:T(8,128)(2,1)} %all-gather.15.cloned.1.call-done, bf16[768,2048]{1,0:T(8,128)(2,1)S(1)} %copy-done), kind=kOutput, calls=%fused_computation.10 | convolution fusion | flops 3233808384 | bytes 18350080 | tf_op jit(solution)/shard_map/dot_general | solution.py:261
  283.6 3.4 fusion.42
  287.0 5.2 add_convert_fusion
  292.3 48.8 %reduce-scatter.19.cloned.1.call-done = bf16[128,2048]{1,0:T(8,128)(2,1)} async-done(((bf16[1024,2048]{1,0:T(8,128)(2,1)}), bf16[128,2048]{1,0:T(8,128)(2,1)}) %reduce-scatter.19.cloned.1.call-update) | async-done | bytes 524304 | tf_op jit(solution)/shard_map/reduce_scatter | solution.py:368
  343.0 2.8 fusion.35
  345.8 33.6 %all-gather.17.cloned.1.call-done = bf16[512,2048]{1,0:T(8,128)(2,1)} async-done(((bf16[128,2048]{1,0:T(8,128)(2,1)}), bf16[512,2048]{1,0:T(8,128)(2,1)}) %all-gather.17.cloned.1.call-update) | async-done | bytes 2097168 | tf_op jit(solution)/shard_map/all_gather | solution.py:374
  379.4 5.3 multiply_convert_fusion.2
  384.7 17.3 %attention_backward.1 = (f32[512,512]{1,0:T(8,128)}, bf16[4096,256]{1,0:T(8,128)(2,1)}, bf16[4096,256]{1,0:T(8,128)(2,1)}) custom-call(s32[4]{0:T(128)} %slice.15.start_ref, bf16[512,512]{1,0:T(8,128)(2,1)} %add_convert_fusion.3.query_ref, bf16[512,512]{1,0:T(8,128)(2,1)} %get-tuple-element.44.grad_ref, f32[512,512]{1,0:T(8,128)} %get-tuple-element.21.att_ref, ...), custom_call_target="tpu_custom_call" | custom-call | flops 5368709120 | bytes 20971520 | tf_op jit(solution)/shard_map/attention_backward/pallas_call | solution.py:232
  402.0 3.2 copy.83
  405.3 3.2 copy.86
  408.6 8.1 convolution_convert_fusion.1
  416.9 7.9 convolution_convert_fusion.2
  424.9 8.0 convolution_convert_fusion.3
  433.0 4.4 convolution_convert_fusion.4
  447.0 4.3 convolution_convert_fusion.5
  458.2 17.8 %reduce-scatter.23.cloned.1.call-done = bf16[512,256]{1,0:T(8,128)(2,1)} async-done(((bf16[4096,256]{1,0:T(8,128)(2,1)}), bf16[512,256]{1,0:T(8,128)(2,1)}) %reduce-scatter.23.cloned.1.call-update) | async-done | bytes 262160 | tf_op jit(solution)/shard_map/reduce_scatter | solution.py:388
  476.0 3.3 convolution_convert_fusion.8
  479.4 3.1 fusion.43
  485.9 2.7 add_convert_fusion.1
  488.7 6.4 convolution_convert_fusion
  495.1 26.8 %reduce-scatter.41.cloned.1.call-done = bf16[768,512]{1,0:T(8,128)(2,1)} async-done(((bf16[768,2048]{1,0:T(8,128)(2,1)}), bf16[768,512]{1,0:T(8,128)(2,1)}) %reduce-scatter.41.cloned.1.call-update) | async-done | bytes 786448 | tf_op jit(solution)/shard_map/reduce_scatter | solution.py:436
  524.4 44.6 %reduce-scatter.39.cloned.1.call-done = bf16[512,768]{1,0:T(8,128)(2,1)} async-done(((bf16[2048,768]{1,0:T(8,128)(2,1)}), bf16[512,768]{1,0:T(8,128)(2,1)}) %reduce-scatter.39.cloned.1.call-update) | async-done | bytes 786448 | tf_op jit(solution)/shard_map/reduce_scatter | solution.py:433
  571.4 44.8 %reduce-scatter.37.cloned.1.call-done = bf16[512,768]{1,0:T(8,128)(2,1)} async-done(((bf16[2048,768]{1,0:T(8,128)(2,1)}), bf16[512,768]{1,0:T(8,128)(2,1)}) %reduce-scatter.37.cloned.1.call-update) | async-done | bytes 786448 | tf_op jit(solution)/shard_map/reduce_scatter | solution.py:430
  618.7 35.6 %reduce-scatter.35.cloned.1.call-done = bf16[512,256]{1,0:T(8,128)(2,1)} async-done(((bf16[512,2048]{1,0:T(8,128)(2,1)}), bf16[512,256]{1,0:T(8,128)(2,1)}) %reduce-scatter.35.cloned.1.call-update) | async-done | bytes 262160 | tf_op jit(solution)/shard_map/reduce_scatter | solution.py:425
  656.1 34.9 %reduce-scatter.27.cloned.1.call-done = bf16[256,512]{1,0:T(8,128)(2,1)} async-done(((bf16[2048,512]{1,0:T(8,128)(2,1)}), bf16[256,512]{1,0:T(8,128)(2,1)}) %reduce-scatter.27.cloned.1.call-update) | async-done | bytes 262160 | tf_op jit(solution)/shard_map/reduce_scatter | solution.py:413
  692.8 34.7 %reduce-scatter.33.cloned.1.call-done = bf16[256,512]{1,0:T(8,128)(2,1)} async-done(((bf16[2048,512]{1,0:T(8,128)(2,1)}), bf16[256,512]{1,0:T(8,128)(2,1)}) %reduce-scatter.33.cloned.1.call-update) | async-done | bytes 262160 | tf_op jit(solution)/shard_map/reduce_scatter | solution.py:422
  729.3 32.0 %reduce-scatter.29.cloned.1.call-done = bf16[256,256]{1,0:T(8,128)(2,1)} async-done(((bf16[2048,256]{1,0:T(8,128)(2,1)}), bf16[256,256]{1,0:T(8,128)(2,1)}) %reduce-scatter.29.cloned.1.call-update) | async-done | bytes 131088 | tf_op jit(solution)/shard_map/reduce_scatter | solution.py:416
  763.0 31.4 %reduce-scatter.31.cloned.1.call-done = bf16[256,256]{1,0:T(8,128)(2,1)} async-done(((bf16[2048,256]{1,0:T(8,128)(2,1)}), bf16[256,256]{1,0:T(8,128)(2,1)}) %reduce-scatter.31.cloned.1.call-update) | async-done | bytes 131088 | tf_op jit(solution)/shard_map/reduce_scatter | solution.py:419
  796.0 35.2 %reduce-scatter.25.cloned.1.call-done = bf16[128,2048]{1,0:T(8,128)(2,1)} async-done(((bf16[512,2048]{1,0:T(8,128)(2,1)}), bf16[128,2048]{1,0:T(8,128)(2,1)}) %reduce-scatter.25.cloned.1.call-update) | async-done | bytes 524304 | tf_op jit(solution)/shard_map/reduce_scatter | solution.py:407
  832.9 41.6 %all-reduce.4 = (f32[2048]{0:T(1024)}, f32[128]{0:T(128)}, f32[128]{0:T(128)}, f32[2048]{0:T(1024)}) all-reduce(f32[2048]{0:T(1024)S(1)} %get-tuple-element.30, f32[128]{0:T(128)S(1)} %get-tuple-element.28, f32[128]{0:T(128)S(1)} %get-tuple-element.32, ...), channel_id=1, replica_groups=mesh['head'=4,'wide'=8] {'head','wide'}, use_global_device_ids=true, to_apply=%region_17.18 | all-reduce | flops 4352 | bytes 34816 | tf_op jit(solution)/shard_map/psum | solution.py:440
  874.5 9.9 %reduce-scatter.17.cloned.1.call-done = bf16[128,2048]{1,0:T(8,128)(2,1)} async-done(((bf16[1024,2048]{1,0:T(8,128)(2,1)}), bf16[128,2048]{1,0:T(8,128)(2,1)}) %reduce-scatter.17.cloned.1.call-update) | async-done | bytes 524304 | tf_op jit(solution)/shard_map/reduce_scatter | solution.py:354
  884.4 3.8 fusion.14
  (175 shorter events, 75.9 us)
Async XLA Ops:
  7.2 266.6 %copy-start = (bf16[768,2048]{1,0:T(8,128)(2,1)S(1)}, bf16[768,2048]{1,0:T(8,128)(2,1)}, u32[]{:S(2)}) copy-start(bf16[768,2048]{1,0:T(8,128)(2,1)} %param.27) | copy-start | bytes 9437188
  7.2 42.7 %all-gather.7.cloned.1.call-start = ((), (), s32[]{:S(2)}) async-start(), calls=%async_computation.14 | async-start | bytes 2621440 | tf_op jit(solution)/shard_map/all_gather | solution.py:298
  11.7 41.5 %copy-start.24 = (s32[1,8]{1,0:T(1,128)S(1)}, s32[1,8]{1,0:T(1,128)}, u32[]{:S(2)}) copy-start(s32[1,8]{1,0:T(1,128)} %param.28) | copy-start | bytes 100
  11.7 42.4 %copy-start.21 = (f32[128]{0:T(128)S(1)}, f32[128]{0:T(128)}, u32[]{:S(2)}) copy-start(f32[128]{0:T(128)} %param.23) | copy-start | bytes 1540
  11.7 74.8 %all-gather.11.cloned.1.call-start = ((), (), s32[]{:S(2)}) async-start(), calls=%async_computation.16 | async-start | bytes 2359296 | tf_op jit(solution)/shard_map/all_gather | solution.py:314
  53.2 60.1 %all-gather.9.cloned.1.call-start = ((), (), s32[]{:S(2)}) async-start(), calls=%async_computation.15 | async-start | bytes 2359296 | tf_op jit(solution)/shard_map/all_gather | solution.py:313
  54.1 3.0 copy-start.5
  58.5 6.2 copy-start.18
  58.5 116.8 %reduce-scatter.15.cloned.1.call-start = ((), (), s32[]{:S(2)}) async-start(), calls=%async_computation.17 | async-start | bytes 2621440 | tf_op jit(solution)/shard_map/reduce_scatter | solution.py:339
  80.6 3.7 copy-start.10
  80.6 3.7 copy-start.30
  126.0 11.4 %copy-start.29 = (bf16[512,2048]{1,0:T(8,128)(2,1)S(1)}, bf16[512,2048]{1,0:T(8,128)(2,1)}, u32[]{:S(2)}) copy-start(bf16[512,2048]{1,0:T(8,128)(2,1)} %param.21) | copy-start | bytes 6291460
  140.9 35.9 %copy-start.16 = (f32[2048]{0:T(1024)S(1)}, f32[2048]{0:T(1024)}, u32[]{:S(2)}) copy-start(f32[2048]{0:T(1024)} %param.24) | copy-start | bytes 24580
  140.9 85.4 %all-gather.13.cloned.1.call-start = ((), (), s32[]{:S(2)}) async-start(), calls=%async_computation.18 | async-start | bytes 4718592 | tf_op jit(solution)/shard_map/all_gather | solution.py:346
  179.0 94.7 %all-gather.15.cloned.1.call-start = ((), (), s32[]{:S(2)}) async-start(), calls=%async_computation.20 | async-start | bytes 4718592 | tf_op jit(solution)/shard_map/all_gather | solution.py:347
  179.6 161.5 %reduce-scatter.19.cloned.1.call-start = ((), (), s32[]{:S(2)}) async-start(), calls=%async_computation.21 | async-start | bytes 4718592 | tf_op jit(solution)/shard_map/reduce_scatter | solution.py:368
  226.3 8.4 copy-start.25
  226.3 8.4 copy-start.26
  273.8 9.8 %copy-start.27 = (bf16[2048,768]{1,0:T(8,128)(2,1)S(1)}, bf16[2048,768]{1,0:T(8,128)(2,1)}, u32[]{:S(2)}) copy-start(bf16[2048,768]{1,0:T(8,128)(2,1)} %param.25) | copy-start | bytes 9437188
  283.5 3.5 copy-start.33
  283.5 3.5 copy-start.34
  283.5 3.5 copy-start.28
  292.3 87.1 %all-gather.17.cloned.1.call-start = ((), (), s32[]{:S(2)}) async-start(), calls=%async_computation.22 | async-start | bytes 2621440 | tf_op jit(solution)/shard_map/all_gather | solution.py:374
  345.8 105.6 %reduce-scatter.21.cloned.1.call-start = ((), (), s32[]{:S(2)}) async-start(), calls=%async_computation.23 | async-start | bytes 2359296 | tf_op jit(solution)/shard_map/reduce_scatter | solution.py:385
  405.2 70.7 %reduce-scatter.23.cloned.1.call-start = ((), (), s32[]{:S(2)}) async-start(), calls=%async_computation.24 | async-start | bytes 2359296 | tf_op jit(solution)/shard_map/reduce_scatter | solution.py:388
  408.5 113.4 %reduce-scatter.41.cloned.1.call-start = ((), (), s32[]{:S(2)}) async-start(), calls=%async_computation.33 | async-start | bytes 3932160 | tf_op jit(solution)/shard_map/reduce_scatter | solution.py:436
  416.7 152.4 %reduce-scatter.39.cloned.1.call-start = ((), (), s32[]{:S(2)}) async-start(), calls=%async_computation.32 | async-start | bytes 3932160 | tf_op jit(solution)/shard_map/reduce_scatter | solution.py:433
  424.8 191.4 %reduce-scatter.37.cloned.1.call-start = ((), (), s32[]{:S(2)}) async-start(), calls=%async_computation.31 | async-start | bytes 3932160 | tf_op jit(solution)/shard_map/reduce_scatter | solution.py:430
  432.9 221.4 %reduce-scatter.35.cloned.1.call-start = ((), (), s32[]{:S(2)}) async-start(), calls=%async_computation.30 | async-start | bytes 2359296 | tf_op jit(solution)/shard_map/reduce_scatter | solution.py:425
  437.4 253.6 %reduce-scatter.27.cloned.1.call-start = ((), (), s32[]{:S(2)}) async-start(), calls=%async_computation.26 | async-start | bytes 2359296 | tf_op jit(solution)/shard_map/reduce_scatter | solution.py:413
  440.0 1.6 copy-start.1
  440.0 1.9 copy-start.4
  440.0 1.9 copy-start.6
  442.2 1.8 copy-start.31
  446.7 280.9 %reduce-scatter.33.cloned.1.call-start = ((), (), s32[]{:S(2)}) async-start(), calls=%async_computation.29 | async-start | bytes 2359296 | tf_op jit(solution)/shard_map/reduce_scatter | solution.py:422
  451.3 310.0 %reduce-scatter.29.cloned.1.call-start = ((), (), s32[]{:S(2)}) async-start(), calls=%async_computation.27 | async-start | bytes 1179648 | tf_op jit(solution)/shard_map/reduce_scatter | solution.py:416
  453.3 1.3 copy-start.7
  453.3 1.5 copy-start.8
  454.7 1.6 copy-start.32
  458.1 336.3 %reduce-scatter.31.cloned.1.call-start = ((), (), s32[]{:S(2)}) async-start(), calls=%async_computation.28 | async-start | bytes 1179648 | tf_op jit(solution)/shard_map/reduce_scatter | solution.py:419
  479.3 351.9 %reduce-scatter.25.cloned.1.call-start = ((), (), s32[]{:S(2)}) async-start(), calls=%async_computation.25 | async-start | bytes 2621440 | tf_op jit(solution)/shard_map/reduce_scatter | solution.py:407
  479.4 3.2 copy-start.13
  483.8 2.0 copy-start.11
  483.8 2.1 copy-start.14
  488.6 395.8 %reduce-scatter.17.cloned.1.call-start = ((), (), s32[]{:S(2)}) async-start(), calls=%async_computation.19 | async-start | bytes 4718592 | tf_op jit(solution)/shard_map/reduce_scatter | solution.py:354
  618.7 212.5 %copy-start.17 = (f32[2048]{0:T(1024)S(1)}, f32[2048]{0:T(1024)}, u32[]{:S(2)}) copy-start(f32[2048]{0:T(1024)} %param.16) | copy-start | bytes 24580
  618.7 212.5 %copy-start.20 = (f32[128]{0:T(128)S(1)}, f32[128]{0:T(128)}, u32[]{:S(2)}) copy-start(f32[128]{0:T(128)} %copy-done.19) | copy-start | bytes 1540
  618.7 255.8 %copy-start.23 = (f32[128]{0:T(128)S(1)}, f32[128]{0:T(128)}, u32[]{:S(2)}) copy-start(f32[128]{0:T(128)} %copy-done.22) | copy-start | bytes 1540
  (7 other events, 6.4 us)
Sparse Core Ops, SparseCore 0:
  11.8 38.0 all-gather.6
  53.3 29.0 all-gather.10
  84.6 28.5 all-gather.8
  141.1 34.2 reduce-scatter.14
  179.2 47.1 all-gather.12
  227.9 45.8 all-gather.14
  292.4 48.7 reduce-scatter.18
  345.9 33.4 all-gather.16
  405.3 33.9 reduce-scatter.20
  441.6 34.3 reduce-scatter.22
  479.2 42.6 reduce-scatter.40
  525.1 43.9 reduce-scatter.38
  572.3 43.9 reduce-scatter.36
  618.5 35.7 reduce-scatter.34
  656.5 34.4 reduce-scatter.26
  693.2 34.2 reduce-scatter.32
  730.3 30.9 reduce-scatter.28
  763.6 30.7 reduce-scatter.30
  797.6 33.5 reduce-scatter.24
  833.3 51.0 reduce-scatter.16

commit v2 on v1

--- a/solution.py
+++ b/solution.py
@@ -7,7 +7,7 @@
 
 EPS = 1e-06
 THETA = 1000000.0
-VMEM_LIMIT = 56 << 20
+VMEM_LIMIT = 62 << 20
 
 
 def rms_apply(values, gain_vec):
@@ -45,8 +45,290 @@
     return rotated.reshape(row_count, -1)
 
 
-def swiglu(gate_in, up_in):
-    return jax.nn.silu(gate_in) * up_in
+MESH = pl.DeviceIdType.MESH
+ANY = pl.BlockSpec(memory_space=pl.ANY)
+VMEM = pl.BlockSpec(memory_space=pltpu.VMEM)
+DMA = pltpu.SemaphoreType.DMA
+SIDES = (0, 1)
+
+
+class Ring:
+    def __init__(self, size, pos, index, device):
+        self.size, self.pos, self.half = size, pos, size // 2
+        self._index, self._device = index, device
+
+    def at(self, offset):
+        return lax.rem(self.pos + (offset + 2 * self.size), self.size)
+
+    def index(self, offset):
+        return self._index(self.at(offset))
+
+    def device(self, offset):
+        return self._device(self.at(offset))
+
+
+def head_ring():
+    size = lax.axis_size("head")
+    spread = size // 2
+    own, wide = lax.axis_index("head"), lax.axis_index("wide")
+    major, minor = lax.div(own, 2), lax.rem(own, 2)
+    pos = major + minor * (size - 1 - 2 * major)
+
+    def index(place):
+        upper = lax.div(place, spread)
+        return 2 * (place + upper * (size - 1 - 2 * place)) + upper
+
+    return Ring(size, pos, index, lambda place: (index(place), wide))
+
+
+def wide_ring():
+    size = lax.axis_size("wide") // 2
+    head, wide = lax.axis_index("head"), lax.axis_index("wide")
+    core = lax.rem(wide, 2)
+    ring = Ring(
+        size, lax.div(wide, 2), lambda place: place, lambda place: (head, 2 * place + core)
+    )
+    ring.core = core
+    ring.sibling = (head, wide + 1 - 2 * core)
+    return ring
+
+
+def meet(devices):
+    barrier = pltpu.get_barrier_semaphore()
+    for device in devices:
+        pl.semaphore_signal(barrier, inc=1, device_id=device, device_id_type=MESH)
+    pl.semaphore_wait(barrier, len(devices))
+
+
+def neighbours(*rings):
+    found = []
+    for ring in rings:
+        found += [ring.device(1), ring.device(-1)]
+        if hasattr(ring, "sibling"):
+            found.append(ring.sibling)
+    return found
+
+
+def remote(src, dst, send, recv, device):
+    return pltpu.make_async_remote_copy(
+        src_ref=src, dst_ref=dst, send_sem=send, recv_sem=recv, device_id=device,
+        device_id_type=MESH,
+    )
+
+
+class Gather:
+    def __init__(self, ring, slot, rows, send, recv):
+        self.ring, self.slot, self.rows = ring, slot, rows
+        self.send, self.recv = send, recv
+
+    def span(self, hop, side):
+        if 2 * hop == self.ring.size:
+            return side * (self.rows // 2), self.rows // 2
+        return 0, self.rows
+
+    def copy(self, hop, side):
+        way = 1 - 2 * side
+        ref = self.slot(self.ring.index(-way * (hop - 1)), *self.span(hop, side))
+        return remote(
+            ref, ref, self.send.at[side, hop - 1], self.recv.at[side, hop - 1],
+            self.ring.device(way),
+        )
+
+    def start(self, hop):
+        for side in SIDES:
+            self.copy(hop, side).start()
+
+    def arrive(self, hop):
+        for side in SIDES:
+            self.copy(hop, side).wait_recv()
+
+    def finish(self):
+        for hop in range(1, self.ring.half + 1):
+            for side in SIDES:
+                self.copy(hop, side).wait_send()
+
+
+class PairGather(Gather):
+    def __init__(self, ring, slot, rows, send, recv, pass_send, pass_recv):
+        core = ring.core
+        super().__init__(
+            ring, lambda index, start, size: slot(2 * index + core, start, size), rows, send, recv
+        )
+        self.pass_send, self.pass_recv = pass_send, pass_recv
+
+    def handed(self, hop, side):
+        way = 1 - 2 * side
+        span = self.span(hop, side) if hop else (0, self.rows)
+        ref = self.slot(self.ring.index(-way * hop), *span)
+        return remote(
+            ref, ref, self.pass_send.at[side, hop], self.pass_recv.at[side, hop],
+            self.ring.sibling,
+        )
+
+    def hand(self, hop):
+        for side in SIDES if hop else (0,):
+            self.handed(hop, side).start()
+
+    def take(self, hop):
+        for side in SIDES if hop else (0,):
+            self.handed(hop, side).wait_recv()
+
+    def begin(self):
+        self.start(1)
+        self.hand(0)
+
+    def finish(self):
+        super().finish()
+        for hop in range(self.ring.half + 1):
+            for side in SIDES if hop else (0,):
+                self.handed(hop, side).wait_send()
+
+
+def row_loop(rows, chunk, body):
+    @pl.loop(0, rows // chunk)
+    def _(step):
+        body(pl.multiple_of(step * chunk, chunk))
+
+
+class Scatter:
+    def __init__(self, ring, part, rows, into, send, recv):
+        self.ring, self.part, self.rows, self.into = ring, part, rows, into
+        self.send, self.recv = send, recv
+
+    def span(self, hop, side):
+        if 2 * hop == self.ring.size:
+            return side * (self.rows // 2), self.rows // 2
+        return 0, self.rows
+
+    def copy(self, hop, side):
+        way = 1 - 2 * side
+        first, count = self.span(hop, side)
+        ref, base = self.part(self.ring.index(way * hop))
+        return remote(
+            ref.at[pl.ds(base + first, count)],
+            self.into.at[side, hop - 1, pl.ds(first, count)],
+            self.send.at[side, hop - 1], self.recv.at[side, hop - 1], self.ring.device(way),
+        )
+
+    def start(self, hop, sides=SIDES):
+        for side in sides:
+            self.copy(hop, side).start()
+
+    def fold(self, hop, side):
+        way = 1 - 2 * side
+        self.copy(hop + 1, side).wait_recv()
+        first, count = self.span(hop + 1, side)
+        ref, base = self.part(self.ring.index(way * hop))
+        chunk = min(count, 32)
+
+        def add(row):
+            there = pl.ds(pl.multiple_of(base + first + row, chunk), chunk)
+            here = pl.ds(pl.multiple_of(first + row, chunk), chunk)
+            ref[there, :] = (
+                ref[there, :].astype(jnp.float32)
+                + self.into[side, hop, here, :].astype(jnp.float32)
+            ).astype(ref.dtype)
+
+        row_loop(count, chunk, add)
+
+    def advance(self, hop):
+        for side in SIDES:
+            self.fold(hop, side)
+            self.copy(hop, side).start()
+
+    def arrive(self):
+        for side in SIDES:
+            self.copy(1, side).wait_recv()
+
+    def total(self, row, count):
+        ref, base = self.part(self.ring.index(0))
+        there = pl.ds(pl.multiple_of(base + row, count), count)
+        here = pl.ds(row, count)
+        return (
+            ref[there, :].astype(jnp.float32)
+            + self.into[0, 0, here, :].astype(jnp.float32)
+            + self.into[1, 0, here, :].astype(jnp.float32)
+        )
+
+    def finish(self):
+        for hop in range(1, self.ring.half + 1):
+            for side in SIDES:
+                self.copy(hop, side).wait_send()
+
+
+class PairScatter(Scatter):
+    def __init__(self, ring, terms, rows, passed, into, send, recv, pass_send, pass_recv):
+        core = ring.core
+        super().__init__(
+            ring, lambda index: (terms, (2 * index + core) * rows), rows, into, send, recv
+        )
+        self.terms, self.passed = terms, passed
+        self.pass_send, self.pass_recv = pass_send, pass_recv
+
+    def handed(self, offset):
+        ring = self.ring
+        index = ring.index(offset)
+        other = pl.multiple_of((2 * index + 1 - ring.core) * self.rows, self.rows)
+        slot = offset % ring.size
+        return remote(
+            self.terms.at[pl.ds(other, self.rows)],
+            self.passed.at[slot],
+            self.pass_send.at[slot], self.pass_recv.at[slot], ring.sibling,
+        )
+
+    def hand(self, offset):
+        self.handed(offset).start()
+
+    def merge(self, offset):
+        self.handed(offset).wait_recv()
+        slot = offset % self.ring.size
+        ref, base = self.part(self.ring.index(offset))
+        chunk = 32
+
+        def add(row):
+            there = pl.ds(pl.multiple_of(base + row, chunk), chunk)
+            ref[there, :] = (
+                ref[there, :].astype(jnp.float32)
+                + self.passed[slot, pl.ds(row, chunk), :].astype(jnp.float32)
+            ).astype(ref.dtype)
+
+        row_loop(self.rows, chunk, add)
+
+    def finish(self):
+        super().finish()
+        for offset in range(self.ring.size):
+            self.handed(offset).wait_send()
+
+
+def offsets(ring):
+    order = [ring.half]
+    for hop in range(ring.half - 1, 0, -1):
+        order += [hop, -hop]
+    return order + [0]
+
+
+def ring_sems(size):
+    return [DMA((2, size // 2)), DMA((2, size // 2))]
+
+
+def pass_sems(size):
+    return [DMA((2, size // 2 + 1)), DMA((2, size // 2 + 1))]
+
+
+def dot_nn(left, right):
+    return jnp.dot(left, right, preferred_element_type=jnp.float32)
+
+
+def dot_nt(left, right):
+    return lax.dot_general(
+        left, right, (((1,), (1,)), ((), ())), preferred_element_type=jnp.float32
+    )
+
+
+def dot_tn(left, right):
+    return lax.dot_general(
+        left, right, (((0,), (0,)), ((), ())), preferred_element_type=jnp.float32
+    )
 
 
 LANES = 128
@@ -249,6 +531,297 @@
         ),
         name="attention_backward",
     )(starts, query_low, grad_low, attended, inverse, key_all, key_all.T, value_all, firsts)
+
+
+def ffn_kernel(
+    gated_ref, x_ref, cot_ref, gain_ref, wo_any, wg_any, wu_any, wd_any,
+    out_ref, mgrad_ref, gain_out, back_any, rows_any, cots_any, hid_any, gg_any, ug_any,
+    wo, wg, wu, wd, cots, rows, hidden_grad, hid, gg, ug, passed, into, passed2,
+    into2, hterms, hinto, middle, back, local_sem,
+    hs, hr, cs, cr, cps, cpr, fs, fr, fps, fpr, s1, r1, ps1, pr1, s2, r2, ps2, pr2, bs, br,
+):
+    tok, width = x_ref.shape
+    hidden_width = wg_any.shape[1]
+    head, wide = head_ring(), wide_ring()
+    pair = 2 * tok
+    loads = [
+        pltpu.make_async_copy(src, dst, local_sem.at[i])
+        for i, (src, dst) in enumerate(((wo_any, wo), (wd_any, wd), (wg_any, wg), (wu_any, wu)))
+    ]
+    for load in loads:
+        load.start()
+    own_wide = pl.multiple_of(lax.axis_index("wide") * tok, tok)
+    own_head = pl.multiple_of(lax.axis_index("head") * tok, tok)
+    cots[pl.ds(own_wide, tok), :] = cot_ref[...]
+    meet(neighbours(head, wide))
+
+    def slot_of(ref):
+        return lambda index, start, size: ref.at[pl.ds(index * tok + start, size)]
+
+    cot_gather = PairGather(wide, slot_of(cots), tok, cs, cr, cps, cpr)
+    row_gather = PairGather(wide, slot_of(rows), tok, fs, fr, fps, fpr)
+    back_gather = Gather(head, slot_of(back), tok, bs, br)
+    head_scatter = Scatter(head, lambda index: (hterms, index * tok), tok, hinto, hs, hr)
+    grad_scatter = PairScatter(wide, cots, tok, passed, into, s1, r1, ps1, pr1)
+    out_scatter = PairScatter(wide, rows, tok, passed2, into2, s2, r2, ps2, pr2)
+
+    def group_of(offset):
+        return pl.ds(pl.multiple_of(wide.index(offset) * pair, pair), pair)
+
+    def col_loop(total, step, body):
+        @pl.loop(0, total // step)
+        def _(i):
+            body(pl.ds(pl.multiple_of(i * step, step), step))
+
+    tile = 256
+    cot_gather.begin()
+
+    def out_part(offset, own):
+        index = head.index(offset)
+        here = pl.ds(pl.multiple_of(index * tok, tok), tok)
+
+        def body(cols):
+            value = dot_nn(gated_ref[here, :], wo[:, cols])
+            if own:
+                middle[:, cols] = x_ref[:, cols].astype(jnp.float32) + value
+            else:
+                hterms[here, cols] = value.astype(jnp.bfloat16)
+
+        col_loop(width, tile, body)
+
+    def hidden_part(offset):
+        here = group_of(offset)
+
+        def body(cols):
+            hidden_grad[here, cols] = dot_nt(cots[here, :], wd[cols, :])
+
+        col_loop(hidden_width, tile if hidden_width % tile == 0 else LANES, body)
+
+    loads[0].wait()
+    out_part(head.half, False)
+    head_scatter.start(head.half)
+    for hop in range(head.half - 1, 0, -1):
+        out_part(hop, False)
+        out_part(-hop, False)
+    out_part(0, True)
+    loads[1].wait()
+    cot_gather.take(0)
+    hidden_part(0)
+    for hop in range(head.half - 1, 0, -1):
+        head_scatter.advance(hop)
+    for hop in range(1, wide.half):
+        cot_gather.arrive(hop)
+        cot_gather.start(hop + 1)
+        cot_gather.hand(hop)
+        cot_gather.take(hop)
+        hidden_part(hop)
+        hidden_part(-hop)
+    head_scatter.arrive()
+
+    gain = gain_ref[...]
+
+    def forward_norm(row):
+        here = pl.ds(row, 32)
+        value = (
+            middle[here, :]
+            + hinto[0, 0, here, :].astype(jnp.float32)
+            + hinto[1, 0, here, :].astype(jnp.float32)
+        )
+        middle[here, :] = value
+        scale = lax.rsqrt(jnp.mean(value * value, axis=-1, keepdims=True) + EPS)
+        rows[pl.ds(pl.multiple_of(own_wide + row, 32), 32), :] = (value * scale * gain).astype(
+            jnp.bfloat16
+        )
+
+    row_loop(tok, 32, forward_norm)
+    row_gather.begin()
+    cot_gather.arrive(wide.half)
+    cot_gather.hand(wide.half)
+    cot_gather.take(wide.half)
+    hidden_part(wide.half)
+    cot_gather.finish()
+    stores = [
+        pltpu.make_async_copy(src, dst, local_sem.at[4 + i])
+        for i, (src, dst) in enumerate(
+            ((rows, rows_any), (cots, cots_any), (hid, hid_any), (gg, gg_any), (ug, ug_any))
+        )
+    ]
+    stores[1].start()
+    loads[2].wait()
+    loads[3].wait()
+
+    def unit(offset):
+        here = group_of(offset)
+
+        def body(cols):
+            gate = dot_nn(rows[here, :], wg[:, cols])
+            up = dot_nn(rows[here, :], wu[:, cols])
+            grad = hidden_grad[here, cols]
+            sig = jax.nn.sigmoid(gate)
+            act = gate * sig
+            hid[here, cols] = (act * up).astype(jnp.bfloat16)
+            gg[here, cols] = (grad * up * (sig + act * (1.0 - sig))).astype(jnp.bfloat16)
+            ug[here, cols] = (grad * act).astype(jnp.bfloat16)
+
+        col_loop(hidden_width, tile if hidden_width % tile == 0 else LANES, body)
+
+    row_gather.take(0)
+    unit(0)
+    for hop in range(1, wide.half):
+        row_gather.arrive(hop)
+        row_gather.start(hop + 1)
+        row_gather.hand(hop)
+        row_gather.take(hop)
+        unit(hop)
+        unit(-hop)
+    row_gather.arrive(wide.half)
+    row_gather.hand(wide.half)
+    row_gather.take(wide.half)
+    unit(wide.half)
+
+    def grad_terms(offset):
+        here = group_of(offset)
+
+        def body(cols):
+            value = dot_nt(gg[here, :], wg[cols, :]) + dot_nt(ug[here, :], wu[cols, :])
+            cots[here, cols] = value.astype(jnp.bfloat16)
+
+        col_loop(width, tile, body)
+        grad_scatter.hand(offset)
+
+    def down_terms(offset):
+        here = group_of(offset)
+
+        def body(cols):
+            rows[here, cols] = dot_nn(hid[here, :], wd[:, cols]).astype(jnp.bfloat16)
+
+        col_loop(width, tile, body)
+        out_scatter.hand(offset)
+
+    order = offsets(wide)
+    stores[1].wait()
+    grad_terms(order[0])
+    grad_terms(order[1])
+    grad_scatter.merge(order[0])
+    grad_scatter.start(wide.half)
+    for offset in order[2:]:
+        grad_terms(offset)
+    for hop in range(wide.half - 1, 0, -1):
+        grad_scatter.merge(hop)
+        grad_scatter.merge(-hop)
+        grad_scatter.advance(hop)
+    grad_scatter.merge(0)
+
+    for store in stores[2:]:
+        store.start()
+    row_gather.finish()
+    stores[0].start()
+    stores[0].wait()
+    for offset in order:
+        down_terms(offset)
+    out_scatter.merge(order[0])
+    grad_scatter.arrive()
+
+    def backward_norm(row, gain_sum):
+        here = pl.ds(row, 32)
+        value = middle[here, :]
+        grad = grad_scatter.total(row, 32)
+        scale = lax.rsqrt(jnp.mean(value * value, axis=-1, keepdims=True) + EPS)
+        scaled = value * scale
+        weighted = grad * gain
+        mean = jnp.mean(scaled * weighted, axis=-1, keepdims=True)
+        total = cot_ref[here, :].astype(jnp.float32) + scale * (weighted - scaled * mean)
+        mgrad_ref[here, :] = total
+        back[pl.ds(pl.multiple_of(own_head + row, 32), 32), :] = total.astype(jnp.bfloat16)
+        return gain_sum + jnp.sum(grad * scaled, axis=0, keepdims=True)
+
+    gain_out[...] = lax.fori_loop(
+        0, tok // 32,
+        lambda i, carried: backward_norm(pl.multiple_of(i * 32, 32), carried),
+        jnp.zeros((1, width), jnp.float32),
+    )
+    back_gather.start(1)
+    out_scatter.start(wide.half)
+    for offset in order[1:]:
+        out_scatter.merge(offset)
+    for hop in range(wide.half - 1, 0, -1):
+        out_scatter.advance(hop)
+    for hop in range(1, head.half):
+        back_gather.arrive(hop)
+        back_gather.start(hop + 1)
+    back_gather.arrive(head.half)
+    back_gather.finish()
+    keep = pltpu.make_async_copy(back, back_any, local_sem.at[9])
+    keep.start()
+    out_scatter.arrive()
+
+    def finish_out(row):
+        here = pl.ds(row, 32)
+        out_ref[here, :] = (middle[here, :] + out_scatter.total(row, 32)).astype(jnp.bfloat16)
+
+    row_loop(tok, 32, finish_out)
+    head_scatter.finish()
+    grad_scatter.finish()
+    out_scatter.finish()
+    for store in stores[2:]:
+        store.wait()
+    keep.wait()
+
+
+def ffn_block(gated_low, inputs, cotangent, ffn_gain, out_w, gate_w, up_w, down_w):
+    tok, width = inputs.shape
+    head_count, wide_count = lax.axis_size("head"), lax.axis_size("wide")
+    chips = wide_count // 2
+    hidden_width = gate_w.shape[1]
+    low, full = jnp.bfloat16, jnp.float32
+    all_rows = wide_count * tok
+    back_rows = head_count * tok
+    shape = jax.ShapeDtypeStruct
+    vm = pltpu.VMEM
+    return pl.pallas_call(
+        ffn_kernel,
+        out_shape=(
+            shape((tok, width), low),
+            shape((tok, width), full),
+            shape((1, width), full),
+            shape((back_rows, width), low),
+            shape((all_rows, width), low),
+            shape((all_rows, width), low),
+            shape((all_rows, hidden_width), low),
+            shape((all_rows, hidden_width), low),
+            shape((all_rows, hidden_width), low),
+        ),
+        in_specs=[VMEM] * 4 + [ANY] * 4,
+        out_specs=tuple([VMEM] * 3 + [ANY] * 6),
+        scratch_shapes=[
+            vm(out_w.shape, low), vm(gate_w.shape, low), vm(up_w.shape, low),
+            vm(down_w.shape, low),
+            vm((all_rows, width), low), vm((all_rows, width), low),
+            vm((all_rows, hidden_width), full),
+            vm((all_rows, hidden_width), low), vm((all_rows, hidden_width), low),
+            vm((all_rows, hidden_width), low),
+            vm((chips, tok, width), low),
+            vm((2, chips // 2, tok, width), low),
+            vm((chips, tok, width), low),
+            vm((2, chips // 2, tok, width), low),
+            vm((back_rows, width), low), vm((2, head_count // 2, tok, width), low),
+            vm((tok, width), full), vm((back_rows, width), low),
+            DMA((10,)),
+            *ring_sems(head_count),
+            *ring_sems(chips), *pass_sems(chips),
+            *ring_sems(chips), *pass_sems(chips),
+            *ring_sems(chips), DMA((chips,)), DMA((chips,)),
+            *ring_sems(chips), DMA((chips,)), DMA((chips,)),
+            *ring_sems(head_count),
+        ],
+        compiler_params=pltpu.CompilerParams(
+            collective_id=1, has_side_effects=True, vmem_limit_bytes=VMEM_LIMIT
+        ),
+        cost_estimate=pl.CostEstimate(
+            flops=10 * all_rows * width * hidden_width, bytes_accessed=200 << 20, transcendentals=0
+        ),
+        name="ffn_block",
+    )(gated_low, inputs, cotangent, ffn_gain[None], out_w, gate_w, up_w, down_w)
 
 
 def contract_rows(left_mat, right_mat):
@@ -335,43 +908,30 @@
         query_low, key_entire, value_entire, starts, firsts, gate_pre
     )
     gate_sig = jax.nn.sigmoid(gate_pre)
-    attn_terms = jnp.dot(gated_low, output_weight, preferred_element_type=jnp.float32)
-    attn_out = lax.psum_scatter(
-        attn_terms.astype(jnp.bfloat16), "head", scatter_dimension=0, tiled=True
-    ).astype(jnp.float32)
-    middle = block_in + attn_out
-    ffn_normed, ffn_norm_back = jax.vjp(rms_apply, middle, ffn_gain)
-    ffn_low = ffn_normed.astype(jnp.bfloat16)
-    ffn_rows, cot_rows = (
-        lax.all_gather(ffn_low, "wide", axis=0, tiled=True),
-        lax.all_gather(cotangent, "wide", axis=0, tiled=True),
-    )
-    gate_val = jnp.dot(ffn_rows, ffn_gate_weight, preferred_element_type=jnp.float32)
-    up_val = jnp.dot(ffn_rows, ffn_up_weight, preferred_element_type=jnp.float32)
-    hidden_val, swiglu_back = jax.vjp(swiglu, gate_val, up_val)
-    hidden_low = hidden_val.astype(jnp.bfloat16)
-    down_terms = jnp.dot(hidden_low, ffn_down_weight, preferred_element_type=jnp.float32)
-    ffn_out = lax.psum_scatter(
-        down_terms.astype(jnp.bfloat16), "wide", scatter_dimension=0, tiled=True
-    ).astype(jnp.float32)
-    outputs = (middle + ffn_out).astype(jnp.bfloat16)
-    hidden_grad = contract_cols(cot_rows, ffn_down_weight)
-    gate_grad, up_grad = swiglu_back(hidden_grad)
-    gate_grad_low = gate_grad.astype(jnp.bfloat16)
-    up_grad_low = up_grad.astype(jnp.bfloat16)
+    (
+        outputs,
+        middle_grad,
+        ffn_gain_part,
+        back_rows,
+        ffn_rows,
+        cot_rows,
+        hidden_low,
+        gate_grad_low,
+        up_grad_low,
+    ) = ffn_block(
+        gated_low,
+        inputs,
+        cotangent,
+        ffn_gain,
+        output_weight,
+        ffn_gate_weight,
+        ffn_up_weight,
+        ffn_down_weight,
+    )
+    ffn_gain_part = ffn_gain_part[0]
     down_wgrad = contract_rows(hidden_low, cot_rows)
     gate_wgrad = contract_rows(ffn_rows, gate_grad_low)
     up_wgrad = contract_rows(ffn_rows, up_grad_low)
-    ffn_terms = contract_cols(gate_grad_low, ffn_gate_weight) + contract_cols(
-        up_grad_low, ffn_up_weight
-    )
-    ffn_normed_grad = lax.psum_scatter(
-        ffn_terms.astype(jnp.bfloat16), "wide", scatter_dimension=0, tiled=True
-    ).astype(jnp.float32)
-    middle_norm_grad, ffn_gain_part = ffn_norm_back(ffn_normed_grad)
-    middle_grad = cotangent.astype(jnp.float32) + middle_norm_grad
-    middle_low = middle_grad.astype(jnp.bfloat16)
-    back_rows = lax.all_gather(middle_low, "head", axis=0, tiled=True)
     gated_grad = contract_cols(back_rows, output_weight)
     out_wgrad = contract_rows(gated_low, back_rows)
     attended_grad_low = (gated_grad * gate_sig).astype(jnp.bfloat16)

time: 908 us -> 798 us (0.88)
  waiting for transfers between devices: 607 us -> 410 us
  Pallas kernels: 28.7 us -> 190 us
  matrix products: 108 us -> 63.7 us
  other arithmetic: 45.2 us -> 30.7 us
    pallas_call x0 -> x1, Pallas kernels: none -> 162 us  [ffn_block(): pl.pallas_call(ffn_kernel, out_shape=(shape((tok, width), low), shape((to...]
    all_gather x3 -> x0, waiting for transfers between devices: 114 us -> none  [the longest x1 46.2 us: shards(): lax.all_gather(ffn_low, 'wide', axis=0, tiled=True)]
    reduce_scatter x3 -> x0, waiting for transfers between devices: 93.1 us -> none  [the longest x1 48.8 us: shards(): lax.psum_scatter(ffn_terms.astype(jnp.bfloat16), 'wide', scatter_dimensio...]
    dot_general x4 -> x0, matrix products: 23.5 us -> none  [the longest x1 8.42 us: shards(): jnp.dot(ffn_rows, ffn_up_weight, preferred_element_type=jnp.float32)]
    dot_general x8 -> x5, matrix products: 31 us -> 12.4 us  [contract_cols(): lax.dot_general(left_mat, right_mat, (((1,), (1,)), ((), ())), preferred_...]
    all_gather x1, waiting for transfers between devices: 0.01 us -> 17.9 us  [shards(): lax.all_gather(value_low, 'wide', axis=0, tiled=True)]
    reduce_scatter x1, waiting for transfers between devices: 26.8 us -> 44.4 us  [shards(): lax.psum_scatter(down_wgrad.astype(jnp.bfloat16), 'head', scatter_dimensi...]
    all_gather x1, waiting for transfers between devices: 23.5 us -> 8.74 us  [shards(): lax.all_gather(key_low, 'wide', axis=0, tiled=True)]
  transfers between devices with their start and end apart: 20 -> 14, of which waited for: 18 -> 13; matrix products, arithmetic and copies ran while one was open for 15% -> 13% of each run, Pallas kernels for 0% -> 0%
where the time goes in v2:
time: 798 us; the launch traced here: 790 us
  waiting for transfers between devices  410 us (51%)
  Pallas kernels  190 us (24%)
  matrix products  63.7 us (8%)
  local copies, waits for them, and re-layouts  40 us (5%)
  blocking collectives  39.8 us (5%)
  other arithmetic  30.7 us (4%)
  between operations  14.5 us (2%)
    pallas_call x1, Pallas kernels, ffn_block(): pl.pallas_call(ffn_kernel, out_shape=(shape((tok, width), low), shape((to...  162 us
    reduce_scatter x1, waiting for transfers between devices, shards(): lax.psum_scatter(gate_wgrad.astype(jnp.bfloat16), 'head', scatter_dimensi...  44.5 us
    reduce_scatter x1, waiting for transfers between devices, shards(): lax.psum_scatter(down_wgrad.astype(jnp.bfloat16), 'head', scatter_dimensi...  44.4 us
    reduce_scatter x1, waiting for transfers between devices, shards(): lax.psum_scatter(up_wgrad.astype(jnp.bfloat16), 'head', scatter_dimension...  43.8 us
    dot_general x8, matrix products, contract_rows(): lax.dot_general(left_mat, right_mat, (((0,), (0,)), ((), ())), preferred_...  39.9 us
    psum x1, blocking collectives, shards(): lax.psum((attn_gain_part, ffn_gain_part, query_gain_part, key_gain_part),...  39.8 us
    all_gather x1, waiting for transfers between devices, shards(): gathered = lax.all_gather(normed_low, 'head', axis=0, tiled=True)  37.2 us
    reduce_scatter x1, waiting for transfers between devices, shards(): lax.psum_scatter(query_wgrad.astype(jnp.bfloat16), 'wide', scatter_dimens...  35.1 us
  transfers between devices with their start and end apart: 14, of which 13 were waited for; matrix products, arithmetic and copies ran while one was open for 13% of the time, Pallas kernels for 0%

profile of v2, /device:TPU:0, one launch (start us, length us, event | category | flops | bytes accessed | tf_op | source)
XLA Modules:
  0.0 790.3 jit_solution(3695367145720630309)
XLA Ops:
  8.6 2.0 fusion.2
  11.6 37.2 %all-gather.4.cloned.1.call-done = bf16[512,2048]{1,0:T(8,128)(2,1)} async-done(((bf16[128,2048]{1,0:T(8,128)(2,1)}), bf16[512,2048]{1,0:T(8,128)(2,1)}) %all-gather.4.cloned.1.call-update) | async-done | bytes 2097168 | tf_op jit(solution)/shard_map/all_gather | solution.py:871
  48.8 2.4 multiply_reduce_fusion.5
  52.6 3.0 convolution_convert_fusion.8
  58.6 3.7 multiply_reduce_fusion.2
  66.9 3.7 add_convert_fusion.1.query_ref
  70.6 2.2 fusion.28.gate_ref
  72.8 8.7 %all-gather.6.cloned.1.call-done = bf16[4096,256]{0,1:T(8,128)(2,1)} async-done(((bf16[512,256]{0,1:T(8,128)(2,1)}), bf16[4096,256]{0,1:T(8,128)(2,1)}) %all-gather.6.cloned.1.call-update) | async-done | bytes 2097168 | tf_op jit(solution)/shard_map/all_gather | solution.py:886
  81.5 4.6 reshape.212
  86.1 2.0 copy.75
  88.1 2.3 copy.96
  90.4 4.1 copy.77.key_ref
  94.5 17.9 %all-gather.8.cloned.1.call-done = bf16[4096,256]{1,0:T(8,128)(2,1)} async-done(((bf16[512,256]{1,0:T(8,128)(2,1)}), bf16[4096,256]{1,0:T(8,128)(2,1)}) %all-gather.8.cloned.1.call-update) | async-done | bytes 2097168 | tf_op jit(solution)/shard_map/all_gather | solution.py:887
  112.3 3.1 copy.76
  115.5 11.2 %attention_forward.1 = (f32[512,512]{1,0:T(8,128)}, f32[512,512]{1,0:T(8,128)}, bf16[512,512]{1,0:T(8,128)(2,1)}) custom-call(s32[4]{0:T(128)} %slice.15.start_ref, bf16[512,512]{1,0:T(8,128)(2,1)} %add_convert_fusion.1.query_ref, bf16[4096,256]{1,0:T(8,128)(2,1)} %copy.77.key_ref, bf16[4096,256]{1,0:T(8,128)(2,1)} %bitcast.119, s32[512,1]{1,0:T(8,128)} %copy.78.first_ref, ...), custom_call_target="tpu_custom_call" | custom-call | flops 2147483648 | bytes 12582912 | tf_op jit(solution)/shard_map/attention_forward/pallas_call | solution.py:408
  126.7 161.6 %ffn_block.1 = (bf16[128,2048]{1,0:T(8,128)(2,1)}, f32[128,2048]{1,0:T(8,128)}, f32[1,2048]{1,0:T(1,128)}, bf16[512,2048]{1,0:T(8,128)(2,1)}, bf16[1024,2048]{1,...) custom-call(bf16[512,512]{1,0:T(8,128)(2,1)} %get-tuple-element.29.g, ...), custom_call_target="tpu_custom_call" | custom-call | flops 16106127360 | bytes 209715200 | tf_op jit(solution)/shard_map/ffn_block/pallas_call | solution.py:781
  288.3 5.3 multiply_convert_fusion
  293.6 17.6 %attention_backward.1 = (f32[512,512]{1,0:T(8,128)}, bf16[4096,256]{1,0:T(8,128)(2,1)}, bf16[4096,256]{1,0:T(8,128)(2,1)}) custom-call(s32[4]{0:T(128)} %slice.15.start_ref, bf16[512,512]{1,0:T(8,128)(2,1)} %add_convert_fusion.1.query_ref, bf16[512,512]{1,0:T(8,128)(2,1)} %get-tuple-element.57.grad_ref, f32[512,512]{1,0:T(8,128)} %get-tuple-element.33.att_ref, ...), custom_call_target="tpu_custom_call" | custom-call | flops 5368709120 | bytes 20971520 | tf_op jit(solution)/shard_map/attention_backward/pallas_call | solution.py:514
  311.1 3.2 copy.83
  314.4 3.2 copy.86
  318.6 4.2 convolution_convert_fusion.3
  327.7 2.6 convolution_convert_fusion.5
  331.4 4.2 convolution_convert_fusion.4
  335.7 8.0 %convolution_convert_fusion.1 = bf16[2048,768]{1,0:T(8,128)(2,1)} fusion(bf16[1024,2048]{1,0:T(8,128)(2,1)} %get-tuple-element.39, bf16[1024,768]{1,0:T(8,128)(2,1)} %get-tuple-element.41), kind=kOutput, calls=%fused_computation.2 | convolution fusion | flops 3222798336 | bytes 8912896 | tf_op jit(solution)/shard_map/dot_general | solution.py:828
  344.1 7.9 convolution_convert_fusion
  352.1 7.9 convolution_convert_fusion.2
  362.9 1.7 convolution_convert_fusion.7
  364.7 20.5 %reduce-scatter.14.cloned.1.call-done = bf16[512,256]{1,0:T(8,128)(2,1)} async-done(((bf16[4096,256]{1,0:T(8,128)(2,1)}), bf16[512,256]{1,0:T(8,128)(2,1)}) %reduce-scatter.14.cloned.1.call-update) | async-done | bytes 262160 | tf_op jit(solution)/shard_map/reduce_scatter | solution.py:948
  385.3 3.4 convolution_convert_fusion.6
  388.9 2.9 fusion.29
  394.7 2.8 add_convert_fusion
  397.5 24.4 %reduce-scatter.26.cloned.1.call-done = bf16[512,256]{1,0:T(8,128)(2,1)} async-done(((bf16[512,2048]{1,0:T(8,128)(2,1)}), bf16[512,256]{1,0:T(8,128)(2,1)}) %reduce-scatter.26.cloned.1.call-update) | async-done | bytes 262160 | tf_op jit(solution)/shard_map/reduce_scatter | solution.py:985
  421.9 1.8 convert_element_type.120
  423.6 35.1 %reduce-scatter.18.cloned.1.call-done = bf16[256,512]{1,0:T(8,128)(2,1)} async-done(((bf16[2048,512]{1,0:T(8,128)(2,1)}), bf16[256,512]{1,0:T(8,128)(2,1)}) %reduce-scatter.18.cloned.1.call-update) | async-done | bytes 262160 | tf_op jit(solution)/shard_map/reduce_scatter | solution.py:973
  458.7 1.8 convert_element_type.112
  460.5 35.0 %reduce-scatter.24.cloned.1.call-done = bf16[256,512]{1,0:T(8,128)(2,1)} async-done(((bf16[2048,512]{1,0:T(8,128)(2,1)}), bf16[256,512]{1,0:T(8,128)(2,1)}) %reduce-scatter.24.cloned.1.call-update) | async-done | bytes 262160 | tf_op jit(solution)/shard_map/reduce_scatter | solution.py:982
  495.5 1.8 convert_element_type.118
  497.3 43.8 %reduce-scatter.30.cloned.1.call-done = bf16[512,768]{1,0:T(8,128)(2,1)} async-done(((bf16[2048,768]{1,0:T(8,128)(2,1)}), bf16[512,768]{1,0:T(8,128)(2,1)}) %reduce-scatter.30.cloned.1.call-update) | async-done | bytes 786448 | tf_op jit(solution)/shard_map/reduce_scatter | solution.py:993
  541.1 2.4 convert_element_type.124
  543.5 44.4 %reduce-scatter.32.cloned.1.call-done = bf16[768,512]{1,0:T(8,128)(2,1)} async-done(((bf16[768,2048]{1,0:T(8,128)(2,1)}), bf16[768,512]{1,0:T(8,128)(2,1)}) %reduce-scatter.32.cloned.1.call-update) | async-done | bytes 786448 | tf_op jit(solution)/shard_map/reduce_scatter | solution.py:996
  587.9 2.5 convert_element_type.126
  590.4 44.5 %reduce-scatter.28.cloned.1.call-done = bf16[512,768]{1,0:T(8,128)(2,1)} async-done(((bf16[2048,768]{1,0:T(8,128)(2,1)}), bf16[512,768]{1,0:T(8,128)(2,1)}) %reduce-scatter.28.cloned.1.call-update) | async-done | bytes 786448 | tf_op jit(solution)/shard_map/reduce_scatter | solution.py:990
  634.8 2.4 convert_element_type.122
  637.2 32.7 %reduce-scatter.20.cloned.1.call-done = bf16[256,256]{1,0:T(8,128)(2,1)} async-done(((bf16[2048,256]{1,0:T(8,128)(2,1)}), bf16[256,256]{1,0:T(8,128)(2,1)}) %reduce-scatter.20.cloned.1.call-update) | async-done | bytes 131088 | tf_op jit(solution)/shard_map/reduce_scatter | solution.py:976
  671.6 31.0 %reduce-scatter.22.cloned.1.call-done = bf16[256,256]{1,0:T(8,128)(2,1)} async-done(((bf16[2048,256]{1,0:T(8,128)(2,1)}), bf16[256,256]{1,0:T(8,128)(2,1)}) %reduce-scatter.22.cloned.1.call-update) | async-done | bytes 131088 | tf_op jit(solution)/shard_map/reduce_scatter | solution.py:979
  704.2 34.8 %reduce-scatter.16.cloned.1.call-done = bf16[128,2048]{1,0:T(8,128)(2,1)} async-done(((bf16[512,2048]{1,0:T(8,128)(2,1)}), bf16[128,2048]{1,0:T(8,128)(2,1)}) %reduce-scatter.16.cloned.1.call-update) | async-done | bytes 524304 | tf_op jit(solution)/shard_map/reduce_scatter | solution.py:967
  740.7 39.8 %all-reduce.4 = (f32[2048]{0:T(1024)}, f32[128]{0:T(128)}, f32[128]{0:T(128)}, f32[2048]{0:T(1024)}) all-reduce(f32[2048]{0:T(1024)S(1)} %get-tuple-element.46, f32[128]{0:T(128)S(1)} %get-tuple-element.44, f32[128]{0:T(128)S(1)} %get-tuple-element.48, f32[2048]{0:T(1024)S(1)} %bitcast.126), channel_id=1, replica_groups=mesh['head'=4,'wide'=8] {'head','wide'}, use_global_device_ids=true, to_apply=%region_12.13 | all-reduce | flops 4352 | bytes 34816 | tf_op jit(solution)/shard_map/psum | solution.py:1000
  780.4 2.3 fusion.5
  (124 shorter events, 30.5 us)
Async XLA Ops:
  7.2 41.6 %copy-start = (bf16[2048,256]{1,0:T(8,128)(2,1)S(1)}, bf16[2048,256]{1,0:T(8,128)(2,1)}, u32[]{:S(2)}) copy-start(bf16[2048,256]{1,0:T(8,128)(2,1)} %param.18) | copy-start | bytes 3145732
  7.2 3.5 copy-start.19
  7.2 4.4 copy-start.18
  7.2 41.6 %all-gather.4.cloned.1.call-start = ((), (), s32[]{:S(2)}) async-start(), calls=%async_computation.11 | async-start | bytes 2621440 | tf_op jit(solution)/shard_map/all_gather | solution.py:871
  10.6 70.9 %all-gather.6.cloned.1.call-start = ((), (), s32[]{:S(2)}) async-start(), calls=%async_computation.12 | async-start | bytes 2359296 | tf_op jit(solution)/shard_map/all_gather | solution.py:886
  11.6 44.7 %copy-start.4 = (f32[512,128]{0,1:T(8,128)}, f32[512,128]{0,1:T(8,128)S(1)}, u32[]{:S(2)}) copy-start(f32[512,128]{0,1:T(8,128)S(1)} %get-tuple-element.74) | copy-start | bytes 786436
  51.3 1.3 copy-start.9
  52.3 60.1 %all-gather.8.cloned.1.call-start = ((), (), s32[]{:S(2)}) async-start(), calls=%async_computation.13 | async-start | bytes 2359296 | tf_op jit(solution)/shard_map/all_gather | solution.py:887
  55.6 3.0 copy-start.17
  55.6 304.4 %reduce-scatter.12.cloned.1.call-start = ((), (), s32[]{:S(2)}) async-start(), calls=%async_computation.14 | async-start | bytes 2359296 | tf_op jit(solution)/shard_map/reduce_scatter | solution.py:945
  62.3 1.5 copy-start.1
  66.9 3.7 copy-start.6
  66.9 3.7 copy-start.20
  314.3 70.9 %reduce-scatter.14.cloned.1.call-start = ((), (), s32[]{:S(2)}) async-start(), calls=%async_computation.15 | async-start | bytes 2359296 | tf_op jit(solution)/shard_map/reduce_scatter | solution.py:948
  317.5 1.0 copy-start.23
  317.5 104.3 %reduce-scatter.26.cloned.1.call-start = ((), (), s32[]{:S(2)}) async-start(), calls=%async_computation.21 | async-start | bytes 2359296 | tf_op jit(solution)/shard_map/reduce_scatter | solution.py:985
  322.8 135.9 %reduce-scatter.18.cloned.1.call-start = ((), (), s32[]{:S(2)}) async-start(), calls=%async_computation.17 | async-start | bytes 2359296 | tf_op jit(solution)/shard_map/reduce_scatter | solution.py:973
  324.4 1.2 copy-start.2
  324.4 1.3 copy-start.5
  326.1 1.6 copy-start.21
  330.4 1.0 copy-start.11
  330.4 165.1 %reduce-scatter.24.cloned.1.call-start = ((), (), s32[]{:S(2)}) async-start(), calls=%async_computation.20 | async-start | bytes 2359296 | tf_op jit(solution)/shard_map/reduce_scatter | solution.py:982
  335.7 205.4 %reduce-scatter.30.cloned.1.call-start = ((), (), s32[]{:S(2)}) async-start(), calls=%async_computation.23 | async-start | bytes 3932160 | tf_op jit(solution)/shard_map/reduce_scatter | solution.py:993
  343.7 244.2 %reduce-scatter.32.cloned.1.call-start = ((), (), s32[]{:S(2)}) async-start(), calls=%async_computation.24 | async-start | bytes 3932160 | tf_op jit(solution)/shard_map/reduce_scatter | solution.py:996
  352.1 282.8 %reduce-scatter.28.cloned.1.call-start = ((), (), s32[]{:S(2)}) async-start(), calls=%async_computation.22 | async-start | bytes 3932160 | tf_op jit(solution)/shard_map/reduce_scatter | solution.py:990
  360.0 309.9 %reduce-scatter.20.cloned.1.call-start = ((), (), s32[]{:S(2)}) async-start(), calls=%async_computation.18 | async-start | bytes 1179648 | tf_op jit(solution)/shard_map/reduce_scatter | solution.py:976
  361.3 1.6 copy-start.22
  364.7 337.9 %reduce-scatter.22.cloned.1.call-start = ((), (), s32[]{:S(2)}) async-start(), calls=%async_computation.19 | async-start | bytes 1179648 | tf_op jit(solution)/shard_map/reduce_scatter | solution.py:979
  388.6 350.4 %reduce-scatter.16.cloned.1.call-start = ((), (), s32[]{:S(2)}) async-start(), calls=%async_computation.16 | async-start | bytes 2621440 | tf_op jit(solution)/shard_map/reduce_scatter | solution.py:967
  391.8 1.2 copy-start.10
  391.8 1.3 copy-start.14
  393.1 1.6 copy-start.7
  393.1 1.7 copy-start.12
  590.4 148.7 %copy-start.3 = (bf16[128,2048]{1,0:T(8,128)(2,1)S(1)}, bf16[128,2048]{1,0:T(8,128)(2,1)}, u32[]{:S(2)}) copy-start(bf16[128,2048]{1,0:T(8,128)(2,1)} %x_ref.1) | copy-start | bytes 1572868
  590.4 148.7 %copy-start.15 = (f32[2048]{0:T(1024)S(1)}, f32[2048]{0:T(1024)}, u32[]{:S(2)}) copy-start(f32[2048]{0:T(1024)} %param.16) | copy-start | bytes 24580
  590.4 150.3 %copy-start.16 = (f32[1,2048]{1,0:T(1,128)S(1)}, f32[1,2048]{1,0:T(1,128)}, u32[]{:S(2)}) copy-start(f32[1,2048]{1,0:T(1,128)} %get-tuple-element.38) | copy-start | bytes 24580
  590.4 190.0 %copy-start.8 = (f32[128,2048]{1,0:T(8,128)S(1)}, f32[128,2048]{1,0:T(8,128)}, u32[]{:S(2)}) copy-start(f32[128,2048]{1,0:T(8,128)} %get-tuple-element.31) | copy-start | bytes 3145732
  704.2 78.5 %copy-start.13 = (bf16[128,2048]{1,0:T(8,128)(2,1)S(1)}, bf16[128,2048]{1,0:T(8,128)(2,1)}, u32[]{:S(2)}) copy-start(bf16[128,2048]{1,0:T(8,128)(2,1)} %get-tuple-element.90) | copy-start | bytes 1572868
Sparse Core Ops, SparseCore 0:
  10.7 38.0 all-gather.3
  52.4 29.0 all-gather.5
  83.7 28.5 all-gather.7
  314.4 34.1 reduce-scatter.11
  350.8 34.3 reduce-scatter.13
  387.4 34.4 reduce-scatter.25
  424.2 34.5 reduce-scatter.17
  461.0 34.4 reduce-scatter.23
  498.5 42.5 reduce-scatter.29
  543.9 43.9 reduce-scatter.31
  590.9 43.9 reduce-scatter.27
  637.5 32.3 reduce-scatter.19
  672.2 30.3 reduce-scatter.21
  705.4 33.5 reduce-scatter.15

commit v3 on v2

--- a/solution.py
+++ b/solution.py
@@ -7,7 +7,7 @@
 
 EPS = 1e-06
 THETA = 1000000.0
-VMEM_LIMIT = 62 << 20
+VMEM_LIMIT = 63 << 20
 
 
 def rms_apply(values, gain_vec):
@@ -206,12 +206,15 @@
         ref, base = self.part(self.ring.index(way * hop))
         return remote(
             ref.at[pl.ds(base + first, count)],
-            self.into.at[side, hop - 1, pl.ds(first, count)],
+            self.into.at[side, pl.ds((hop - 1) * self.rows + self.inside(hop, first), count)],
             self.send.at[side, hop - 1], self.recv.at[side, hop - 1], self.ring.device(way),
         )
 
-    def start(self, hop, sides=SIDES):
-        for side in sides:
+    def inside(self, hop, row):
+        return row % (self.rows // 2) if 2 * hop == self.ring.size else row
+
+    def start(self, hop):
+        for side in SIDES:
             self.copy(hop, side).start()
 
     def fold(self, hop, side):
@@ -223,10 +226,10 @@
 
         def add(row):
             there = pl.ds(pl.multiple_of(base + first + row, chunk), chunk)
-            here = pl.ds(pl.multiple_of(first + row, chunk), chunk)
+            start = hop * self.rows + self.inside(hop + 1, first)
+            here = pl.ds(pl.multiple_of(start + row, chunk), chunk)
             ref[there, :] = (
-                ref[there, :].astype(jnp.float32)
-                + self.into[side, hop, here, :].astype(jnp.float32)
+                ref[there, :].astype(jnp.float32) + self.into[side, here, :].astype(jnp.float32)
             ).astype(ref.dtype)
 
         row_loop(count, chunk, add)
@@ -246,8 +249,8 @@
         here = pl.ds(row, count)
         return (
             ref[there, :].astype(jnp.float32)
-            + self.into[0, 0, here, :].astype(jnp.float32)
-            + self.into[1, 0, here, :].astype(jnp.float32)
+            + self.into[0, here, :].astype(jnp.float32)
+            + self.into[1, here, :].astype(jnp.float32)
         )
 
     def finish(self):
@@ -305,6 +308,19 @@
     for hop in range(ring.half - 1, 0, -1):
         order += [hop, -hop]
     return order + [0]
+
+
+def into_shape(size, rows, columns):
+    return pltpu.VMEM((2, (size - 1) * rows // 2, columns), jnp.bfloat16)
+
+
+def everyone(*rings):
+    found = []
+    for ring in rings:
+        found += [ring.device(offset) for offset in range(1, ring.size)]
+        if hasattr(ring, "sibling"):
+            found.append(ring.sibling)
+    return found
 
 
 def ring_sems(size):
@@ -425,7 +441,7 @@
 
 def attention_backward_kernel(
     start_ref, query_ref, grad_ref, att_ref, inv_ref, key_ref, keyt_ref, value_ref, first_ref,
-    dq_ref, dk_ref, dv_ref, dk_acc, dv_acc, dqt,
+    dq_ref, kv_ref, dk_acc, dv_acc, dqt,
 ):
     blocks = start_ref.shape[0]
     groups = key_ref.shape[1] // LANES
@@ -498,8 +514,15 @@
                 cols = slice((g * per + j) * LANES, (g * per + j + 1) * LANES)
                 dq_ref[here, cols] = jnp.transpose(dqt[g, :, j * rows : (j + 1) * rows])
 
-    dk_ref[...] = dk_acc[...].astype(dk_ref.dtype)
-    dv_ref[...] = dv_acc[...].astype(dv_ref.dtype)
+    width = dk_acc.shape[1]
+
+    @pl.loop(0, wide_count)
+    def _(target):
+        for blk in range(blocks):
+            source = pl.ds(pl.multiple_of((blk * wide_count + target) * rows, rows), rows)
+            there = pl.ds(pl.multiple_of((target * blocks + blk) * rows, rows), rows)
+            kv_ref[there, :width] = dk_acc[source, :].astype(jnp.bfloat16)
+            kv_ref[there, width:] = dv_acc[source, :].astype(jnp.bfloat16)
 
 
 def attention_backward(
@@ -515,11 +538,10 @@
         attention_backward_kernel,
         out_shape=(
             jax.ShapeDtypeStruct((rows, width), jnp.float32),
-            jax.ShapeDtypeStruct((keys, kv_width), jnp.bfloat16),
-            jax.ShapeDtypeStruct((keys, kv_width), jnp.bfloat16),
+            jax.ShapeDtypeStruct((keys, 2 * kv_width), jnp.bfloat16),
         ),
         in_specs=[pl.BlockSpec(memory_space=pltpu.SMEM)] + [vmem] * 8,
-        out_specs=(vmem, vmem, vmem),
+        out_specs=(vmem, vmem),
         scratch_shapes=[
             pltpu.VMEM((keys, kv_width), jnp.float32),
             pltpu.VMEM((keys, kv_width), jnp.float32),
@@ -535,15 +557,18 @@
 
 def ffn_kernel(
     gated_ref, x_ref, cot_ref, gain_ref, wo_any, wg_any, wu_any, wd_any,
-    out_ref, mgrad_ref, gain_out, back_any, rows_any, cots_any, hid_any, gg_any, ug_any,
-    wo, wg, wu, wd, cots, rows, hidden_grad, hid, gg, ug, passed, into, passed2,
-    into2, hterms, hinto, middle, back, local_sem,
-    hs, hr, cs, cr, cps, cpr, fs, fr, fps, fpr, s1, r1, ps1, pr1, s2, r2, ps2, pr2, bs, br,
+    out_any, mgrad_ref, gain_out, back_any, down_ref, fgate_any, fup_any,
+    wo, wg, wu, wd, cots, rows, hidden_grad, hid, gg, ug, terms_own, passed, into,
+    passed2, into2, dterms, dinto, stage, hterms, hinto, middle, back, local_sem,
+    ds, dr, hs, hr, cs, cr, cps, cpr, fs, fr, fps, fpr, s1, r1, ps1, pr1, s2, r2, ps2, pr2, bs, br,
 ):
     tok, width = x_ref.shape
     hidden_width = wg_any.shape[1]
     head, wide = head_ring(), wide_ring()
     pair = 2 * tok
+    separate = terms_own.shape[0] > 16
+    terms = terms_own if separate else cots
+    part = wo_any.shape[1] // lax.axis_size("head")
     loads = [
         pltpu.make_async_copy(src, dst, local_sem.at[i])
         for i, (src, dst) in enumerate(((wo_any, wo), (wd_any, wd), (wg_any, wg), (wu_any, wu)))
@@ -562,7 +587,10 @@
     row_gather = PairGather(wide, slot_of(rows), tok, fs, fr, fps, fpr)
     back_gather = Gather(head, slot_of(back), tok, bs, br)
     head_scatter = Scatter(head, lambda index: (hterms, index * tok), tok, hinto, hs, hr)
-    grad_scatter = PairScatter(wide, cots, tok, passed, into, s1, r1, ps1, pr1)
+    grad_scatter = PairScatter(wide, terms, tok, passed, into, s1, r1, ps1, pr1)
+    down_scatter = Scatter(
+        head, lambda index: (dterms, index * hidden_width), hidden_width, dinto, ds, dr
+    )
     out_scatter = PairScatter(wide, rows, tok, passed2, into2, s2, r2, ps2, pr2)
 
     def group_of(offset):
@@ -593,7 +621,9 @@
         here = group_of(offset)
 
         def body(cols):
-            hidden_grad[here, cols] = dot_nt(cots[here, :], wd[cols, :])
+            hidden_grad[here, cols] = dot_nt(cots[here, :], wd[cols, :]).astype(
+                hidden_grad.dtype
+            )
 
         col_loop(hidden_width, tile if hidden_width % tile == 0 else LANES, body)
 
@@ -624,8 +654,8 @@
         here = pl.ds(row, 32)
         value = (
             middle[here, :]
-            + hinto[0, 0, here, :].astype(jnp.float32)
-            + hinto[1, 0, here, :].astype(jnp.float32)
+            + hinto[0, here, :].astype(jnp.float32)
+            + hinto[1, here, :].astype(jnp.float32)
         )
         middle[here, :] = value
         scale = lax.rsqrt(jnp.mean(value * value, axis=-1, keepdims=True) + EPS)
@@ -640,13 +670,6 @@
     cot_gather.take(wide.half)
     hidden_part(wide.half)
     cot_gather.finish()
-    stores = [
-        pltpu.make_async_copy(src, dst, local_sem.at[4 + i])
-        for i, (src, dst) in enumerate(
-            ((rows, rows_any), (cots, cots_any), (hid, hid_any), (gg, gg_any), (ug, ug_any))
-        )
-    ]
-    stores[1].start()
     loads[2].wait()
     loads[3].wait()
 
@@ -656,7 +679,7 @@
         def body(cols):
             gate = dot_nn(rows[here, :], wg[:, cols])
             up = dot_nn(rows[here, :], wu[:, cols])
-            grad = hidden_grad[here, cols]
+            grad = hidden_grad[here, cols].astype(jnp.float32)
             sig = jax.nn.sigmoid(gate)
             act = gate * sig
             hid[here, cols] = (act * up).astype(jnp.bfloat16)
@@ -684,7 +707,7 @@
 
         def body(cols):
             value = dot_nt(gg[here, :], wg[cols, :]) + dot_nt(ug[here, :], wu[cols, :])
-            cots[here, cols] = value.astype(jnp.bfloat16)
+            terms[here, cols] = value.astype(jnp.bfloat16)
 
         col_loop(width, tile, body)
         grad_scatter.hand(offset)
@@ -698,28 +721,70 @@
         col_loop(width, tile, body)
         out_scatter.hand(offset)
 
+    def down_grads():
+        @pl.loop(0, lax.axis_size("head"))
+        def _(index):
+            cols = pl.ds(pl.multiple_of(index * part, part), part)
+
+            @pl.loop(0, hidden_width // LANES)
+            def _(i):
+                lanes = pl.ds(pl.multiple_of(i * LANES, LANES), LANES)
+                there = pl.ds(
+                    pl.multiple_of(index * hidden_width + i * LANES, LANES), LANES
+                )
+                dterms[there, :] = dot_tn(hid[:, lanes], cots[:, cols]).astype(jnp.bfloat16)
+
+        down_scatter.start(head.half)
+
+    emit = stage.shape[2]
+
+    def stage_copy(step, out, any_ref, slot):
+        there = pl.ds(pl.multiple_of(step * emit, emit), emit)
+        return pltpu.make_async_copy(
+            stage.at[slot, out], any_ref.at[there], local_sem.at[5 + 2 * slot + out]
+        )
+
+    def input_grads():
+        @pl.loop(0, width // emit // 2)
+        def _(i):
+            for slot in SIDES:
+                step = 2 * i + slot
+                cols = pl.ds(pl.multiple_of(step * emit, emit), emit)
+
+                @pl.when(i > 0)
+                def _():
+                    for out, any_ref in enumerate((fgate_any, fup_any)):
+                        stage_copy(step - 2, out, any_ref, slot).wait()
+
+                left = rows[:, cols]
+                stage[slot, 0] = dot_tn(left, gg[...]).astype(jnp.bfloat16)
+                stage[slot, 1] = dot_tn(left, ug[...]).astype(jnp.bfloat16)
+                for out, any_ref in enumerate((fgate_any, fup_any)):
+                    stage_copy(step, out, any_ref, slot).start()
+
     order = offsets(wide)
-    stores[1].wait()
+    if not separate:
+        down_grads()
     grad_terms(order[0])
     grad_terms(order[1])
     grad_scatter.merge(order[0])
     grad_scatter.start(wide.half)
     for offset in order[2:]:
         grad_terms(offset)
+    if separate:
+        down_grads()
     for hop in range(wide.half - 1, 0, -1):
         grad_scatter.merge(hop)
         grad_scatter.merge(-hop)
         grad_scatter.advance(hop)
     grad_scatter.merge(0)
-
-    for store in stores[2:]:
-        store.start()
+    input_grads()
     row_gather.finish()
-    stores[0].start()
-    stores[0].wait()
     for offset in order:
         down_terms(offset)
     out_scatter.merge(order[0])
+    for hop in range(head.half - 1, 0, -1):
+        down_scatter.advance(hop)
     grad_scatter.arrive()
 
     def backward_norm(row, gain_sum):
@@ -751,21 +816,31 @@
         back_gather.start(hop + 1)
     back_gather.arrive(head.half)
     back_gather.finish()
-    keep = pltpu.make_async_copy(back, back_any, local_sem.at[9])
+    keep = pltpu.make_async_copy(back, back_any, local_sem.at[4])
     keep.start()
     out_scatter.arrive()
 
     def finish_out(row):
         here = pl.ds(row, 32)
-        out_ref[here, :] = (middle[here, :] + out_scatter.total(row, 32)).astype(jnp.bfloat16)
-
+        back[here, :] = (middle[here, :] + out_scatter.total(row, 32)).astype(jnp.bfloat16)
+
+    keep.wait()
     row_loop(tok, 32, finish_out)
-    head_scatter.finish()
-    grad_scatter.finish()
-    out_scatter.finish()
-    for store in stores[2:]:
-        store.wait()
-    keep.wait()
+    result = pltpu.make_async_copy(back.at[pl.ds(0, tok)], out_any, local_sem.at[9])
+    result.start()
+    down_scatter.arrive()
+
+    def finish_down(row):
+        down_ref[pl.ds(row, 32), :] = down_scatter.total(row, 32)
+
+    row_loop(hidden_width, 32, finish_down)
+    for scatter in (head_scatter, grad_scatter, out_scatter, down_scatter):
+        scatter.finish()
+    last = width // emit
+    for slot in SIDES:
+        for out, any_ref in enumerate((fgate_any, fup_any)):
+            stage_copy(last - 2 + slot, out, any_ref, slot).wait()
+    result.wait()
 
 
 def ffn_block(gated_low, inputs, cotangent, ffn_gain, out_w, gate_w, up_w, down_w):
@@ -776,6 +851,7 @@
     low, full = jnp.bfloat16, jnp.float32
     all_rows = wide_count * tok
     back_rows = head_count * tok
+    roomy = all_rows * width <= 2 << 20
     shape = jax.ShapeDtypeStruct
     vm = pltpu.VMEM
     return pl.pallas_call(
@@ -785,28 +861,31 @@
             shape((tok, width), full),
             shape((1, width), full),
             shape((back_rows, width), low),
-            shape((all_rows, width), low),
-            shape((all_rows, width), low),
-            shape((all_rows, hidden_width), low),
-            shape((all_rows, hidden_width), low),
-            shape((all_rows, hidden_width), low),
+            shape((hidden_width, width // head_count), full),
+            shape((width, hidden_width), low),
+            shape((width, hidden_width), low),
         ),
         in_specs=[VMEM] * 4 + [ANY] * 4,
-        out_specs=tuple([VMEM] * 3 + [ANY] * 6),
+        out_specs=(ANY, VMEM, VMEM, ANY, VMEM, ANY, ANY),
         scratch_shapes=[
             vm(out_w.shape, low), vm(gate_w.shape, low), vm(up_w.shape, low),
             vm(down_w.shape, low),
             vm((all_rows, width), low), vm((all_rows, width), low),
-            vm((all_rows, hidden_width), full),
+            vm((all_rows, hidden_width), full if roomy else low),
             vm((all_rows, hidden_width), low), vm((all_rows, hidden_width), low),
             vm((all_rows, hidden_width), low),
+            vm((all_rows if roomy else 16, width), low),
             vm((chips, tok, width), low),
-            vm((2, chips // 2, tok, width), low),
+            into_shape(chips, tok, width),
             vm((chips, tok, width), low),
-            vm((2, chips // 2, tok, width), low),
-            vm((back_rows, width), low), vm((2, head_count // 2, tok, width), low),
+            into_shape(chips, tok, width),
+            vm((head_count * hidden_width, width // head_count), low),
+            into_shape(head_count, hidden_width, width // head_count),
+            vm((2, 2, 256 if roomy else 128, hidden_width), low),
+            vm((back_rows, width), low), into_shape(head_count, tok, width),
             vm((tok, width), full), vm((back_rows, width), low),
             DMA((10,)),
+            *ring_sems(head_count),
             *ring_sems(head_count),
             *ring_sems(chips), *pass_sems(chips),
             *ring_sems(chips), *pass_sems(chips),
@@ -824,9 +903,362 @@
     )(gated_low, inputs, cotangent, ffn_gain[None], out_w, gate_w, up_w, down_w)
 
 
-def contract_rows(left_mat, right_mat):
-    return lax.dot_general(
-        left_mat, right_mat, (((0,), (0,)), ((), ())), preferred_element_type=jnp.float32
+def turn_back(grad, cosine, sine_tab):
+    half = LANES // 2
+    lane = lax.broadcasted_iota(jnp.int32, grad.shape, 1)
+    turned = pltpu.roll(grad * sine_tab, half, 1)
+    return grad * cosine + jnp.where(lane < half, turned, -turned)
+
+
+def unprep(grad, pre_proj, gain, cosine, sine_tab):
+    turned = turn_back(grad, cosine, sine_tab)
+    scale = lax.rsqrt(jnp.mean(pre_proj * pre_proj, axis=-1, keepdims=True) + EPS)
+    scaled = pre_proj * scale
+    weighted = turned * gain
+    mean = jnp.mean(scaled * weighted, axis=-1, keepdims=True)
+    return scale * (weighted - scaled * mean), turned * scaled
+
+
+def tail_kernel(
+    dq_ref, qpre_ref, kpre_ref, ggrad_ref, cos_ref, sin_ref, qgain_ref, kgain_ref, x_ref,
+    mgrad_ref, gain_ref, ffn_gain_ref, gated_ref,
+    kvp_any, normed_any, back_any, wq_any, wk_any, wv_any, wg_any, fgate_any, fup_any,
+    igrad_ref, gains_ref, query_out, key_out, value_out, gate_out, output_out, fgate_out, fup_out,
+    kvp, normed, back, wq, wk, wv, wg, fgate, fup, qlow, klow, vlow, early, late, hterms,
+    kv_passed, kv_into, early_passed, early_into, late_passed, late_into, hinto, fgate_into,
+    fup_into, gain_slots, stage, local_sem,
+    kvs, kvr, kvps, kvpr, es, er, eps, epr, ls, lr, lps, lpr, hs, hr, gs, gr, us, ur, gain_send,
+    gain_recv,
+):
+    tok, width = x_ref.shape
+    rows = dq_ref.shape[0]
+    wide_count = lax.axis_size("wide")
+    head_count = lax.axis_size("head")
+    head, wide = head_ring(), wide_ring()
+    loads = [
+        pltpu.make_async_copy(src, dst, local_sem.at[i])
+        for i, (src, dst) in enumerate(
+            (
+                (kvp_any, kvp), (fgate_any, fgate), (fup_any, fup), (normed_any, normed),
+                (back_any, back), (wq_any, wq), (wk_any, wk), (wv_any, wv), (wg_any, wg),
+            )
+        )
+    ]
+    for load in loads:
+        load.start()
+    meet(everyone(head, wide))
+    kv_width = wk.shape[1]
+    q_width = wq.shape[1]
+    block = normed.shape[1] // wide_count
+    ffn_rows = fgate.shape[0] // head_count
+    kv_scatter = PairScatter(wide, kvp, rows, kv_passed, kv_into, kvs, kvr, kvps, kvpr)
+    early_scatter = PairScatter(wide, early, block, early_passed, early_into, es, er, eps, epr)
+    late_scatter = PairScatter(wide, late, block, late_passed, late_into, ls, lr, lps, lpr)
+    head_scatter = Scatter(head, lambda index: (hterms, index * tok), tok, hinto, hs, hr)
+    gate_scatter = Scatter(
+        head, lambda index: (fgate, index * ffn_rows), ffn_rows, fgate_into, gs, gr
+    )
+    up_scatter = Scatter(head, lambda index: (fup, index * ffn_rows), ffn_rows, fup_into, us, ur)
+    order = offsets(wide)
+
+    loads[0].wait()
+    for offset in order:
+        kv_scatter.hand(offset)
+    loads[1].wait()
+    gate_scatter.start(head.half)
+    loads[2].wait()
+    up_scatter.start(head.half)
+
+    chunk = 128
+
+    def query_back(row, total):
+        here = pl.ds(row, chunk)
+        for j in range(q_width // LANES):
+            cols = slice(j * LANES, (j + 1) * LANES)
+            value, terms = unprep(
+                dq_ref[here, cols], qpre_ref[here, cols], qgain_ref[...], cos_ref[here, :],
+                sin_ref[here, :],
+            )
+            qlow[here, cols] = value.astype(jnp.bfloat16)
+            total = total + jnp.sum(terms, axis=0, keepdims=True)
+        return total
+
+    def over_rows(count, body, start):
+        return lax.fori_loop(
+            0, count // chunk, lambda i, carried: body(pl.multiple_of(i * chunk, chunk), carried),
+            start,
+        )
+
+    qgain_sum = over_rows(rows, query_back, jnp.zeros((1, LANES), jnp.float32))
+
+    kv_scatter.merge(order[0])
+    kv_scatter.start(wide.half)
+    loads[3].wait()
+    loads[4].wait()
+
+    def early_part(offset):
+        index = wide.index(offset)
+
+        @pl.loop(0, 2)
+        def _(core):
+            target = 2 * index + core
+            cols = pl.ds(pl.multiple_of(target * block, block), block)
+            there = pl.ds(pl.multiple_of(target * block, block), block)
+            left = normed[:, cols]
+            early[there, :q_width] = dot_tn(left, qlow[...]).astype(jnp.bfloat16)
+            early[there, q_width : 2 * q_width] = dot_tn(left, ggrad_ref[...]).astype(jnp.bfloat16)
+            out = dot_tn(gated_ref[...], back[:, cols]).astype(jnp.bfloat16)
+            for piece in range(q_width // block):
+                early[there, 2 * q_width + piece * block : 2 * q_width + (piece + 1) * block] = out[
+                    piece * block : (piece + 1) * block, :
+                ]
+
+        early_scatter.hand(offset)
+
+    for offset in order:
+        early_part(offset)
+    for offset in order[1:]:
+        kv_scatter.merge(offset)
+    early_scatter.merge(order[0])
+    for hop in range(wide.half - 1, 0, -1):
+        kv_scatter.advance(hop)
+    early_scatter.start(wide.half)
+    for hop in range(head.half - 1, 0, -1):
+        gate_scatter.advance(hop)
+        up_scatter.advance(hop)
+    for offset in order[1:]:
+        early_scatter.merge(offset)
+    for load in loads[5:]:
+        load.wait()
+    kv_scatter.arrive()
+
+    def key_back(row, total):
+        here = pl.ds(row, chunk)
+        both = kv_scatter.total(row, chunk)
+        for j in range(kv_width // LANES):
+            cols = slice(j * LANES, (j + 1) * LANES)
+            value, terms = unprep(
+                both[:, cols], kpre_ref[here, cols], kgain_ref[...], cos_ref[here, :],
+                sin_ref[here, :],
+            )
+            klow[here, cols] = value.astype(jnp.bfloat16)
+            total = total + jnp.sum(terms, axis=0, keepdims=True)
+        vlow[here, :] = both[:, kv_width:].astype(jnp.bfloat16)
+        return total
+
+    kgain_sum = over_rows(rows, key_back, jnp.zeros((1, LANES), jnp.float32))
+
+    def head_part(offset):
+        here = pl.ds(pl.multiple_of(head.index(offset) * tok, tok), tok)
+
+        @pl.loop(0, width // 256)
+        def _(i):
+            cols = pl.ds(pl.multiple_of(i * 256, 256), 256)
+            value = dot_nt(qlow[here, :], wq[cols, :]) + dot_nt(ggrad_ref[here, :], wg[cols, :])
+            value += dot_nt(klow[here, :], wk[cols, :]) + dot_nt(vlow[here, :], wv[cols, :])
+            hterms[here, cols] = value.astype(jnp.bfloat16)
+
+    head_part(head.half)
+    head_scatter.start(head.half)
+
+    def late_part(offset):
+        index = wide.index(offset)
+
+        @pl.loop(0, 2)
+        def _(core):
+            target = 2 * index + core
+            cols = pl.ds(pl.multiple_of(target * block, block), block)
+            left = normed[:, cols]
+            late[cols, :kv_width] = dot_tn(left, klow[...]).astype(jnp.bfloat16)
+            late[cols, kv_width:] = dot_tn(left, vlow[...]).astype(jnp.bfloat16)
+
+        late_scatter.hand(offset)
+
+    late_part(order[0])
+    for hop in range(wide.half - 1, 0, -1):
+        early_scatter.advance(hop)
+    for offset in order[1:]:
+        late_part(offset)
+    late_scatter.merge(order[0])
+    late_scatter.start(wide.half)
+    for hop in range(head.half - 1, 0, -1):
+        head_part(hop)
+        head_part(-hop)
+        head_scatter.advance(hop)
+    head_part(0)
+    for offset in order[1:]:
+        late_scatter.merge(offset)
+    for hop in range(wide.half - 1, 0, -1):
+        late_scatter.advance(hop)
+
+    gate_scatter.arrive()
+    up_scatter.arrive()
+    emit = 64
+    pending = [None, None]
+    for step in range(ffn_rows // emit):
+        for which, (scatter, out) in enumerate(((gate_scatter, fgate_out), (up_scatter, fup_out))):
+            if pending[which] is not None:
+                pending[which].wait()
+            stage[which] = scatter.total(step * emit, emit)
+            pending[which] = pltpu.make_async_copy(
+                stage.at[which], out.at[pl.ds(step * emit, emit)], local_sem.at[9 + which]
+            )
+            pending[which].start()
+
+    head_scatter.arrive()
+    gain = gain_ref[...]
+
+    def input_back(row, total):
+        here = pl.ds(row, 32)
+        value = x_ref[here, :].astype(jnp.float32)
+        grad = head_scatter.total(row, 32)
+        scale = lax.rsqrt(jnp.mean(value * value, axis=-1, keepdims=True) + EPS)
+        scaled = value * scale
+        weighted = grad * gain
+        mean = jnp.mean(scaled * weighted, axis=-1, keepdims=True)
+        igrad_ref[here, :] = mgrad_ref[here, :] + scale * (weighted - scaled * mean)
+        return total + jnp.sum(grad * scaled, axis=0, keepdims=True)
+
+    gain_sum = lax.fori_loop(
+        0, tok // 32, lambda i, carried: input_back(pl.multiple_of(i * 32, 32), carried),
+        jnp.zeros((1, width), jnp.float32),
+    )
+    chips = wide.size
+    pair_slot, chip_slot = 0, 2
+    head_slot = 2 + chips
+    mine = gain_slots.at[pair_slot]
+    mine[...] = jnp.zeros(mine.shape, jnp.float32)
+    mine[0:1, :] = gain_sum
+    mine[1:2, :] = ffn_gain_ref[...]
+    mine[2:3, 0:LANES] = qgain_sum
+    mine[3:4, 0:LANES] = kgain_sum
+    swap = remote(
+        mine, gain_slots.at[1], gain_send.at[0], gain_recv.at[0], wide.sibling
+    )
+    swap.start()
+    swap.wait_recv()
+
+    def spread(ring, own, base, sem):
+        here = gain_slots.at[base + own]
+        copies = [
+            remote(here, here, gain_send.at[sem + d], gain_recv.at[sem + d], ring.device(d))
+            for d in range(1, ring.size)
+        ]
+        for copy in copies:
+            copy.start()
+        for copy in copies:
+            copy.wait_recv()
+        return copies
+
+    own_chip = wide.index(0)
+    gain_slots[chip_slot + own_chip] = gain_slots[0] + gain_slots[1]
+    sent = [swap] + spread(wide, own_chip, chip_slot, 0)
+    total = gain_slots[chip_slot]
+    for i in range(1, chips):
+        total = total + gain_slots[chip_slot + i]
+    own_head = lax.axis_index("head")
+    gain_slots[head_slot + own_head] = total
+    sent += spread(head, own_head, head_slot, chips - 1)
+    total = gain_slots[head_slot]
+    for i in range(1, head_count):
+        total = total + gain_slots[head_slot + i]
+    gains_ref[...] = total
+
+    early_scatter.arrive()
+
+    def early_out(row):
+        here = pl.ds(row, 32)
+        both = early_scatter.total(row, 32)
+        query_out[here, :] = both[:, :q_width]
+        gate_out[here, :] = both[:, q_width : 2 * q_width]
+        for piece in range(q_width // block):
+            output_out[pl.ds(pl.multiple_of(piece * block + row, 32), 32), :] = both[
+                :, 2 * q_width + piece * block : 2 * q_width + (piece + 1) * block
+            ]
+
+    row_loop(block, 32, early_out)
+    late_scatter.arrive()
+
+    def late_out(row):
+        here = pl.ds(row, 32)
+        both = late_scatter.total(row, 32)
+        key_out[here, :] = both[:, :kv_width]
+        value_out[here, :] = both[:, kv_width:]
+
+    row_loop(block, 32, late_out)
+    for scatter in (
+        kv_scatter, early_scatter, late_scatter, head_scatter, gate_scatter, up_scatter
+    ):
+        scatter.finish()
+    for copy in sent:
+        copy.wait_send()
+    for copy in pending:
+        copy.wait()
+
+
+def tail_block(
+    dq, kv_parts, query_pre, key_pre, gate_grad, cosine, sine_tab, query_gain, key_gain, inputs,
+    middle_grad, attn_gain, ffn_gain_part, gated_low, normed, back_rows, weights, fgate, fup,
+):
+    tok, width = inputs.shape
+    head_count, wide_count = lax.axis_size("head"), lax.axis_size("wide")
+    chips = wide_count // 2
+    rows, q_width = dq.shape
+    kv_width = key_pre.shape[1]
+    block = width // wide_count
+    hidden_width = fgate.shape[1]
+    ffn_rows = width // head_count
+    low, full = jnp.bfloat16, jnp.float32
+    shape, vm = jax.ShapeDtypeStruct, pltpu.VMEM
+    early_width = 3 * q_width
+    pair = [*ring_sems(chips), DMA((chips,)), DMA((chips,))]
+    peers = chips + head_count
+    return pl.pallas_call(
+        tail_kernel,
+        out_shape=(
+            shape((tok, width), full),
+            shape((8, width), full),
+            shape((block, q_width), full),
+            shape((block, kv_width), full),
+            shape((block, kv_width), full),
+            shape((block, q_width), full),
+            shape((q_width, block), full),
+            shape((ffn_rows, hidden_width), full),
+            shape((ffn_rows, hidden_width), full),
+        ),
+        in_specs=[VMEM] * 13 + [ANY] * 9,
+        out_specs=tuple([VMEM] * 7 + [ANY] * 2),
+        scratch_shapes=[
+            vm(kv_parts.shape, low), vm(normed.shape, low), vm(back_rows.shape, low),
+            *[vm(weight.shape, low) for weight in weights],
+            vm(fgate.shape, low), vm(fup.shape, low),
+            vm((rows, q_width), low), vm((rows, kv_width), low), vm((rows, kv_width), low),
+            vm((width, early_width), low), vm((width, 2 * kv_width), low),
+            vm((head_count * tok, width), low),
+            vm((chips, rows, 2 * kv_width), low), into_shape(chips, rows, 2 * kv_width),
+            vm((chips, block, early_width), low), into_shape(chips, block, early_width),
+            vm((chips, block, 2 * kv_width), low), into_shape(chips, block, 2 * kv_width),
+            into_shape(head_count, tok, width),
+            into_shape(head_count, ffn_rows, hidden_width),
+            into_shape(head_count, ffn_rows, hidden_width),
+            vm((2 + chips + head_count, 8, width), full),
+            vm((2, 64, hidden_width), full),
+            DMA((11,)),
+            *pair, *pair, *pair,
+            *ring_sems(head_count), *ring_sems(head_count), *ring_sems(head_count),
+            DMA((peers,)), DMA((peers,)),
+        ],
+        compiler_params=pltpu.CompilerParams(
+            collective_id=2, has_side_effects=True, vmem_limit_bytes=VMEM_LIMIT
+        ),
+        cost_estimate=pl.CostEstimate(
+            flops=20 * rows * width * q_width, bytes_accessed=300 << 20, transcendentals=0
+        ),
+        name="tail_block",
+    )(
+        dq, query_pre, key_pre, gate_grad, cosine, sine_tab, query_gain[None], key_gain[None],
+        inputs, middle_grad, attn_gain[None], ffn_gain_part, gated_low,
+        kv_parts, normed, back_rows, *weights, fgate, fup,
     )
 
 
@@ -866,8 +1298,7 @@
     firsts = query_first[:, None]
     cosine, sine_tab = rotary(query_pos, head_width)
     block_in = inputs.astype(jnp.float32)
-    normed, input_norm_back = jax.vjp(rms_apply, block_in, attn_gain)
-    normed_low = normed.astype(jnp.bfloat16)
+    normed_low = rms_apply(block_in, attn_gain).astype(jnp.bfloat16)
     gathered = lax.all_gather(normed_low, "head", axis=0, tiled=True)
     query_pre = jnp.dot(gathered, query_weight, preferred_element_type=jnp.float32)
     key_pre = jnp.dot(gathered, key_projection, preferred_element_type=jnp.float32)
@@ -877,8 +1308,8 @@
     def prep_heads(pre_proj, gain_vec):
         return head_prep(pre_proj, gain_vec, cosine, sine_tab)
 
-    query_rot, query_back = jax.vjp(prep_heads, query_pre, query_gain)
-    key_rot, key_back = jax.vjp(prep_heads, key_pre, key_gain)
+    query_rot = prep_heads(query_pre, query_gain)
+    key_rot = prep_heads(key_pre, key_gain)
     query_low = query_rot.astype(jnp.bfloat16)
     key_low = key_rot.astype(jnp.bfloat16)
     value_low = value_pre.astype(jnp.bfloat16)
@@ -895,13 +1326,6 @@
             .reshape(-1, kv_width)
         )
 
-    def gathered_order(matrix):
-        return (
-            matrix.reshape(head_count, wide_count, tok_dev, kv_width)
-            .transpose(1, 0, 2, 3)
-            .reshape(-1, kv_width)
-        )
-
     key_entire = natural_order(key_wide)
     value_entire = natural_order(value_wide)
     attended, inverse, gated_low = attention_forward(
@@ -913,11 +1337,9 @@
         middle_grad,
         ffn_gain_part,
         back_rows,
-        ffn_rows,
-        cot_rows,
-        hidden_low,
-        gate_grad_low,
-        up_grad_low,
+        ffn_down_grad,
+        gate_wgrad,
+        up_wgrad,
     ) = ffn_block(
         gated_low,
         inputs,
@@ -928,78 +1350,45 @@
         ffn_up_weight,
         ffn_down_weight,
     )
-    ffn_gain_part = ffn_gain_part[0]
-    down_wgrad = contract_rows(hidden_low, cot_rows)
-    gate_wgrad = contract_rows(ffn_rows, gate_grad_low)
-    up_wgrad = contract_rows(ffn_rows, up_grad_low)
     gated_grad = contract_cols(back_rows, output_weight)
-    out_wgrad = contract_rows(gated_low, back_rows)
     attended_grad_low = (gated_grad * gate_sig).astype(jnp.bfloat16)
     gate_pre_grad_low = (gated_grad * attended * gate_sig * (1.0 - gate_sig)).astype(jnp.bfloat16)
-    query_rot_grad, key_natural, value_natural = attention_backward(
+    query_rot_grad, kv_parts = attention_backward(
         query_low, attended_grad_low, attended, inverse, key_entire, value_entire, starts, firsts
     )
-    key_terms = gathered_order(key_natural)
-    value_terms = gathered_order(value_natural)
-    key_rot_grad, value_sum = (
-        lax.psum_scatter(
-            key_terms.astype(jnp.bfloat16), "wide", scatter_dimension=0, tiled=True
-        ).astype(jnp.float32),
-        lax.psum_scatter(
-            value_terms.astype(jnp.bfloat16), "wide", scatter_dimension=0, tiled=True
-        ).astype(jnp.float32),
-    )
-    query_pre_grad, query_gain_part = query_back(query_rot_grad)
-    key_pre_grad, key_gain_part = key_back(key_rot_grad)
-    query_pre_low = query_pre_grad.astype(jnp.bfloat16)
-    key_pre_low = key_pre_grad.astype(jnp.bfloat16)
-    value_grad_low = value_sum.astype(jnp.bfloat16)
-    query_wgrad = contract_rows(gathered, query_pre_low)
-    key_wgrad = contract_rows(gathered, key_pre_low)
-    value_wgrad = contract_rows(gathered, value_grad_low)
-    attn_gate_wgrad = contract_rows(gathered, gate_pre_grad_low)
-    normed_terms = (
-        contract_cols(query_pre_low, query_weight)
-        + contract_cols(key_pre_low, key_projection)
-        + contract_cols(value_grad_low, value_projection)
-        + contract_cols(gate_pre_grad_low, attn_gate_weight)
-    )
-    normed_grad = lax.psum_scatter(
-        normed_terms.astype(jnp.bfloat16), "head", scatter_dimension=0, tiled=True
-    ).astype(jnp.float32)
-    input_norm_grad, attn_gain_part = input_norm_back(normed_grad)
-    input_grad = middle_grad + input_norm_grad
-    query_grad, key_grad, value_grad, attn_gate_grad, output_grad = (
-        lax.psum_scatter(
-            query_wgrad.astype(jnp.bfloat16), "wide", scatter_dimension=0, tiled=True
-        ).astype(jnp.float32),
-        lax.psum_scatter(
-            key_wgrad.astype(jnp.bfloat16), "wide", scatter_dimension=0, tiled=True
-        ).astype(jnp.float32),
-        lax.psum_scatter(
-            value_wgrad.astype(jnp.bfloat16), "wide", scatter_dimension=0, tiled=True
-        ).astype(jnp.float32),
-        lax.psum_scatter(
-            attn_gate_wgrad.astype(jnp.bfloat16), "wide", scatter_dimension=0, tiled=True
-        ).astype(jnp.float32),
-        lax.psum_scatter(
-            out_wgrad.astype(jnp.bfloat16), "wide", scatter_dimension=1, tiled=True
-        ).astype(jnp.float32),
-    )
-    ffn_gate_grad, ffn_up_grad, ffn_down_grad = (
-        lax.psum_scatter(
-            gate_wgrad.astype(jnp.bfloat16), "head", scatter_dimension=0, tiled=True
-        ).astype(jnp.float32),
-        lax.psum_scatter(
-            up_wgrad.astype(jnp.bfloat16), "head", scatter_dimension=0, tiled=True
-        ).astype(jnp.float32),
-        lax.psum_scatter(
-            down_wgrad.astype(jnp.bfloat16), "head", scatter_dimension=1, tiled=True
-        ).astype(jnp.float32),
-    )
-    attn_gain_grad, ffn_gain_grad, query_gain_grad, key_gain_grad = lax.psum(
-        (attn_gain_part, ffn_gain_part, query_gain_part, key_gain_part), ("head", "wide")
-    )
+    (
+        input_grad,
+        gains,
+        query_grad,
+        key_grad,
+        value_grad,
+        attn_gate_grad,
+        output_grad,
+        ffn_gate_grad,
+        ffn_up_grad,
+    ) = tail_block(
+        query_rot_grad,
+        kv_parts,
+        query_pre,
+        key_pre,
+        gate_pre_grad_low,
+        cosine,
+        sine_tab,
+        query_gain,
+        key_gain,
+        inputs,
+        middle_grad,
+        attn_gain,
+        ffn_gain_part,
+        gated_low,
+        gathered,
+        back_rows,
+        (query_weight, key_projection, value_projection, attn_gate_weight),
+        gate_wgrad,
+        up_wgrad,
+    )
+    attn_gain_grad, ffn_gain_grad = gains[0], gains[1]
+    query_gain_grad, key_gain_grad = gains[2, :head_width], gains[3, :head_width]
     return (
         outputs,
         input_grad,

time: 798 us -> 466 us (0.58)
  waiting for transfers between devices: 410 us -> 75.8 us
  Pallas kernels: 190 us -> 320 us
  matrix products: 63.7 us -> 16 us
  blocking collectives: 39.8 us -> 0 us
  other arithmetic: 30.7 us -> 9.08 us
  local copies, waits for them, and re-layouts: 40 us -> 30 us
    reduce_scatter x11 -> x0, waiting for transfers between devices: 346 us -> none  [the longest x1 44.5 us: shards(): lax.psum_scatter(gate_wgrad.astype(jnp.bfloat16), 'head', scatter_dimensi...]
    pallas_call x0 -> x1, Pallas kernels: none -> 124 us  [tail_block(): pl.pallas_call(tail_kernel, out_shape=(shape((tok, width), full), shape((...]
    dot_general x8 -> x0, matrix products: 39.9 us -> none  [contract_rows(): lax.dot_general(left_mat, right_mat, (((0,), (0,)), ((), ())), preferred_...]
    psum x1 -> x0, blocking collectives: 39.8 us -> none  [shards(): lax.psum((attn_gain_part, ffn_gain_part, query_gain_part, key_gain_part),...]
    all_gather x1, waiting for transfers between devices: 8.74 us -> 27.7 us  [shards(): lax.all_gather(key_low, 'wide', axis=0, tiled=True)]
    convert_element_type x11 -> x1, other arithmetic: 18.4 us -> 2.03 us  [shards(): normed_low = rms_apply(block_in, attn_gain).astype(jnp.bfloat16)]
    reshape x4 -> x0, local copies, waits for them, and re-layouts: 8.97 us -> none  [the longest x2 6.32 us: gathered_order(): matrix.reshape(head_count, wide_count, tok_dev, kv_width)]
  transfers between devices with their start and end apart: 14 -> 3, of which waited for: 13 -> 3; matrix products, arithmetic and copies ran while one was open for 13% -> 5% of each run, Pallas kernels for 0% -> 0%
where the time goes in v3:
time: 466 us; the launch traced here: 465 us
  Pallas kernels  320 us (69%)
  waiting for transfers between devices  75.8 us (16%)
  local copies, waits for them, and re-layouts  30 us (6%)
  matrix products  16 us (3%)
  between operations  14.1 us (3%)
  other arithmetic  9.08 us (2%)
    pallas_call x1, Pallas kernels, ffn_block(): pl.pallas_call(ffn_kernel, out_shape=(shape((tok, width), low), shape((to...  168 us
    pallas_call x1, Pallas kernels, tail_block(): pl.pallas_call(tail_kernel, out_shape=(shape((tok, width), full), shape((...  124 us
    all_gather x1, waiting for transfers between devices, shards(): gathered = lax.all_gather(normed_low, 'head', axis=0, tiled=True)  38.1 us
    all_gather x1, waiting for transfers between devices, shards(): lax.all_gather(key_low, 'wide', axis=0, tiled=True)  27.7 us
    pallas_call x1, Pallas kernels, attention_backward(): pl.pallas_call(attention_backward_kernel, out_shape=(jax.ShapeDtypeStruct...  17.7 us
    unnamed x53, local copies, waits for them, and re-layouts  12.8 us
    pallas_call x1, Pallas kernels, attention_forward(): pl.pallas_call(attention_forward_kernel, out_shape=(jax.ShapeDtypeStruct(...  11.2 us
    all_gather x1, waiting for transfers between devices, shards(): lax.all_gather(value_low, 'wide', axis=0, tiled=True)  9.97 us
  transfers between devices with their start and end apart: 3, of which 3 were waited for; matrix products, arithmetic and copies ran while one was open for 5% of the time, Pallas kernels for 0%

profile of v3, /device:TPU:0, one launch (start us, length us, event | category | flops | bytes accessed | tf_op | source)
XLA Modules:
  0.0 465.3 jit_solution(3167781679292076340)
XLA Ops:
  7.2 1.3 fusion
  8.6 2.0 fusion.2
  10.7 38.1 %all-gather.4.cloned.1.call-done.normed_any = bf16[512,2048]{1,0:T(8,128)(2,1)} async-done(((bf16[128,2048]{1,0:T(8,128)(2,1)}), bf16[512,2048]{1,0:T(8,128)(2,1)}) %all-gather.4.cloned.1.call-update) | async-done | bytes 2097168 | tf_op jit(solution)/shard_map/all_gather | solution.py:1302
  48.8 3.0 convolution_convert_fusion
  51.9 0.2 reduce-window.8
  52.2 1.0 multiply_cosine_fusion
  53.2 0.2 pad_maximum_fusion
  53.4 0.1 copy.67
  53.7 0.4 copy-done.2
  54.2 2.0 multiply_reduce_fusion.1
  56.5 0.9 fusion.5
  57.4 0.6 slice.27.start_ref
  58.0 0.9 copy.74.first_ref
  58.9 1.0 copy.78.kpre_ref
  59.9 3.5 multiply_reduce_fusion
  63.4 0.3 copy.66.qpre_ref
  63.8 0.2 multiply_multiply_fusion
  64.1 0.1 maximum_multiply_fusion
  64.2 0.3 copy.80
  64.7 1.3 copy.79
  66.0 0.2 mul.202
  66.3 2.7 fusion.4.query_ref
  68.9 2.2 fusion.20.gate_ref
  71.2 10.0 %all-gather.8.cloned.1.call-done = bf16[4096,256]{1,0:T(8,128)(2,1)} async-done(((bf16[512,256]{1,0:T(8,128)(2,1)}), bf16[4096,256]{1,0:T(8,128)(2,1)}) %all-gather.8.cloned.1.call-update) | async-done | bytes 2097168 | tf_op jit(solution)/shard_map/all_gather | solution.py:1318
  81.1 3.1 copy.72
  84.3 27.7 %all-gather.6.cloned.1.call-done = bf16[4096,256]{0,1:T(8,128)(2,1)} async-done(((bf16[512,256]{0,1:T(8,128)(2,1)}), bf16[4096,256]{0,1:T(8,128)(2,1)}) %all-gather.6.cloned.1.call-update) | async-done | bytes 2097168 | tf_op jit(solution)/shard_map/all_gather | solution.py:1317
  111.9 3.2 reshape.154
  115.2 0.4 copy.71
  115.5 1.0 copy.87
  116.5 2.6 copy.73.key_ref
  119.2 11.2 %attention_forward.1 = (f32[512,512]{1,0:T(8,128)}, f32[512,512]{1,0:T(8,128)}, bf16[512,512]{1,0:T(8,128)(2,1)}) custom-call(s32[4]{0:T(128)} %slice.27.start_ref, bf16[512,512]{1,0:T(8,128)(2,1)} %fusion.4.query_ref, bf16[4096,256]{1,0:T(8,128)(2,1)} %copy.73.key_ref, bf16[4096,256]{1,0:T(8,128)(2,1)} %bitcast.83, s32[512,1]{1,0:T(8,128)} %copy.74.first_ref, ...), custom_call_target="tpu_custom_call" | custom-call | flops 2147483648 | bytes 12582912 | tf_op jit(solution)/shard_map/attention_forward/pallas_call | solution.py:424
  130.3 167.5 %ffn_block.1 = (bf16[128,2048]{1,0:T(8,128)(2,1)}, f32[128,2048]{1,0:T(8,128)}, f32[1,2048]{1,0:T(1,128)}, bf16[512,2048]{1,0:T(8,128)(2,1)}, f32[768,512]{1,0:T...) custom-call(bf16[512,512]{1,0:T(8,128)(2,1)} %get-tuple-element.35.gated_ref, bf16[128,2048]{1,0:T(8,128)(2,1)} %x_ref.3, ...), custom_call_target="tpu_custom_call" | custom-call | flops 16106127360 | bytes 209715200 | tf_op jit(solution)/shard_map/ffn_block/pallas_call | solution.py:857
  297.9 5.3 %multiply_convert_fusion = (bf16[512,512]{1,0:T(8,128)(2,1)}, bf16[512,512]{1,0:T(8,128)(2,1)}) fusion(f32[512,512]{1,0:T(8,128)} %get-tuple-element.38.att_ref, f32[512,512]{1,0:T(8,128)} %fusion.20.gate_ref, bf16[512,2048]{1,0:T(8,128)(2,1)} %get-tuple-element.37.back_any, bf16[512,2048]{1,0:T(8,128)(2,1)} %wo_any.1), kind=kOutput, calls=%fused_computation.11 | convolution fusion | flops 1076363264 | bytes 7340032 | tf_op jit(solution)/shard_map/dot_general | solution.py:1266
  303.1 17.7 %attention_backward.1 = (f32[512,512]{1,0:T(8,128)}, bf16[4096,512]{1,0:T(8,128)(2,1)}) custom-call(s32[4]{0:T(128)} %slice.27.start_ref, bf16[512,512]{1,0:T(8,128)(2,1)} %fusion.4.query_ref, bf16[512,512]{1,0:T(8,128)(2,1)} %get-tuple-element.57.grad_ref, f32[512,512]{1,0:T(8,128)} %get-tuple-element.38.att_ref, f32[512,512]{1,0:T(8,128)} %get-tuple-element.39.inv_ref, ...), custom_call_target="tpu_custom_call" | custom-call | flops 5368709120 | bytes 20971520 | tf_op jit(solution)/shard_map/attention_backward/pallas_call | solution.py:537
  320.8 123.9 %tail_block.1 = (f32[128,2048]{1,0:T(8,128)}, f32[8,2048]{1,0:T(8,128)}, f32[256,512]{1,0:T(8,128)}, f32[256,256]{1,0:T(8,128)}, f32[256,256]{1,0:T(8,128)}, /*i...) custom-call(f32[512,512]{1,0:T(8,128)} %get-tuple-element.40.dq_ref, ...), custom_call_target="tpu_custom_call" | custom-call | flops 10737418240 | bytes 314572800 | tf_op jit(solution)/shard_map/tail_block/pallas_call | solution.py:1216
  444.7 1.3 slice_bitcast_fusion
  446.0 1.5 fusion.19
  447.6 0.8 copy.98
  448.4 2.4 copy.99
  450.7 0.8 copy.100
  451.5 0.7 copy.101
  452.2 0.7 copy.102
  452.9 0.8 copy.103
  453.7 0.8 copy.104
  454.5 1.1 copy.105
  455.7 1.1 copy.106
  456.8 0.8 copy-done.4
  457.7 1.1 copy.107
  (61 shorter events, 1.1 us)
Async XLA Ops:
  7.2 41.6 %copy-start.20 = (bf16[2048,256]{1,0:T(8,128)(2,1)S(1)}, bf16[2048,256]{1,0:T(8,128)(2,1)}, u32[]{:S(2)}) copy-start(bf16[2048,256]{1,0:T(8,128)(2,1)} %wv_any.1) | copy-start | bytes 3145732
  7.2 41.6 %all-gather.4.cloned.1.call-start = ((), (), s32[]{:S(2)}) async-start(), calls=%async_computation | async-start | bytes 2621440 | tf_op jit(solution)/shard_map/all_gather | solution.py:1302
  10.6 41.3 %copy-start.16 = (s32[1,8]{1,0:T(1,128)S(1)}, s32[1,8]{1,0:T(1,128)}, u32[]{:S(2)}) copy-start(s32[1,8]{1,0:T(1,128)} %param.28) | copy-start | bytes 100
  10.6 70.5 %all-gather.8.cloned.1.call-start = ((), (), s32[]{:S(2)}) async-start(), calls=%async_computation.2 | async-start | bytes 2359296 | tf_op jit(solution)/shard_map/all_gather | solution.py:1318
  51.8 2.4 copy-start.15
  51.8 2.4 copy-start.18
  51.8 60.1 %all-gather.6.cloned.1.call-start = ((), (), s32[]{:S(2)}) async-start(), calls=%async_computation.1 | async-start | bytes 2359296 | tf_op jit(solution)/shard_map/all_gather | solution.py:1317
  53.4 0.7 copy-start.2
  53.4 0.8 copy-start.7
  56.3 2.5 copy-start.14
  63.7 2.5 copy-start.1
  64.6 1.4 copy-start.3
  66.2 2.7 copy-start.17
  66.2 2.7 copy-start.19
  116.5 2.6 copy-start
  320.8 126.7 %copy-start.8 = (bf16[128,2048]{1,0:T(8,128)(2,1)S(1)}, bf16[128,2048]{1,0:T(8,128)(2,1)}, u32[]{:S(2)}) copy-start(bf16[128,2048]{1,0:T(8,128)(2,1)} %get-tuple-element.90) | copy-start | bytes 1572868
  444.7 6.0 %copy-start.11 = (f32[256,512]{1,0:T(8,128)S(1)}, f32[256,512]{1,0:T(8,128)}, u32[]{:S(2)}) copy-start(f32[256,512]{1,0:T(8,128)} %get-tuple-element.93) | copy-start | bytes 1572868
  447.5 4.0 copy-start.13
  447.5 4.7 %copy-start.12 = (f32[256,256]{1,0:T(8,128)S(1)}, f32[256,256]{1,0:T(8,128)}, u32[]{:S(2)}) copy-start(f32[256,256]{1,0:T(8,128)} %get-tuple-element.95) | copy-start | bytes 786436
  448.4 4.6 copy-start.10
  448.4 5.4 %copy-start.9 = (f32[512,256]{1,0:T(8,128)S(1)}, f32[512,256]{1,0:T(8,128)}, u32[]{:S(2)}) copy-start(f32[512,256]{1,0:T(8,128)} %get-tuple-element.97) | copy-start | bytes 1572868
  450.7 3.8 copy-start.6
  453.7 1.9 copy-start.5
  455.7 2.0 copy-start.4
Sparse Core Ops, SparseCore 0:
  10.7 38.0 all-gather.3
  51.9 29.1 all-gather.7
  83.3 28.5 all-gather.5

commit v4 on v3

--- a/solution.py
+++ b/solution.py
@@ -8,10 +8,6 @@
 EPS = 1e-06
 THETA = 1000000.0
 VMEM_LIMIT = 63 << 20
-
-
-def rms_apply(values, gain_vec):
-    return values * lax.rsqrt(jnp.mean(values * values, axis=-1, keepdims=True) + EPS) * gain_vec
 
 
 def token_tables(doc_lengths, token_ids):
@@ -33,16 +29,6 @@
         jnp.concatenate([cosine, cosine], axis=1),
         jnp.concatenate([sine_tab, sine_tab], axis=1),
     )
-
-
-def head_prep(pre_proj, gain_vec, cosine, sine_tab):
-    row_count = pre_proj.shape[0]
-    head_width = gain_vec.shape[0]
-    half_width = head_width // 2
-    per_head = rms_apply(pre_proj.reshape(row_count, -1, head_width), gain_vec)
-    turned = jnp.concatenate([-per_head[..., half_width:], per_head[..., :half_width]], axis=-1)
-    rotated = per_head * cosine[:, None, :] + turned * sine_tab[:, None, :]
-    return rotated.reshape(row_count, -1)
 
 
 MESH = pl.DeviceIdType.MESH
@@ -353,13 +339,14 @@
 
 
 def attention_forward_kernel(
-    start_ref, query_ref, key_ref, value_ref, first_ref, gate_ref, att_ref, inv_ref, gated_ref, acc
+    start_ref, query_ref, kv_ref, first_ref, gate_ref, att_ref, inv_ref, gated_ref, acc
 ):
     blocks = start_ref.shape[0]
-    groups = key_ref.shape[1] // LANES
-    per = query_ref.shape[1] // key_ref.shape[1]
+    kv_width = kv_ref.shape[1] // 2
+    groups = kv_width // LANES
+    per = query_ref.shape[1] // kv_width
     rows = query_ref.shape[0] // blocks
-    wide_count = key_ref.shape[0] // query_ref.shape[0]
+    wide_count = kv_ref.shape[0] // query_ref.shape[0]
     wide_pos = lax.axis_index("wide")
     step = KEY_BLOCK
     factor = LANES ** (-0.5) * LOG2E
@@ -392,13 +379,14 @@
             allowed = jnp.concatenate([allowed] * per, axis=0)
             for g in range(groups):
                 cols = slice(g * LANES, (g + 1) * LANES)
+                value_cols = slice(kv_width + g * LANES, kv_width + (g + 1) * LANES)
                 scores = lax.dot_general(
-                    queries[g], key_ref[there, cols], (((1,), (1,)), ((), ())),
+                    queries[g], kv_ref[there, cols], (((1,), (1,)), ((), ())),
                     preferred_element_type=jnp.float32,
                 )
                 probs = jnp.where(allowed, jnp.exp2(scores * factor), 0.0).astype(jnp.bfloat16)
                 values = jnp.concatenate(
-                    [value_ref[there, cols], jnp.ones((step, LANES), jnp.bfloat16)], axis=1
+                    [kv_ref[there, value_cols], jnp.ones((step, LANES), jnp.bfloat16)], axis=1
                 )
                 acc[g] += jnp.dot(probs, values, preferred_element_type=jnp.float32)
 
@@ -415,10 +403,10 @@
                 )
 
 
-def attention_forward(query_low, key_all, value_all, starts, firsts, gate_pre):
+def attention_forward(query_low, kv_all, starts, firsts, gate_pre):
     rows, width = query_low.shape
-    groups = key_all.shape[1] // LANES
-    per = width // key_all.shape[1]
+    groups = (kv_all.shape[1] // 2) // LANES
+    per = width // (kv_all.shape[1] // 2)
     blocks = starts.shape[0]
     vmem = pl.BlockSpec(memory_space=pltpu.VMEM)
     return pl.pallas_call(
@@ -428,7 +416,7 @@
             jax.ShapeDtypeStruct((rows, width), jnp.float32),
             jax.ShapeDtypeStruct((rows, width), jnp.bfloat16),
         ),
-        in_specs=[pl.BlockSpec(memory_space=pltpu.SMEM)] + [vmem] * 5,
+        in_specs=[pl.BlockSpec(memory_space=pltpu.SMEM)] + [vmem] * 4,
         out_specs=(vmem, vmem, vmem),
         scratch_shapes=[pltpu.VMEM((groups, per * (rows // blocks), 2 * LANES), jnp.float32)],
         compiler_params=pltpu.CompilerParams(vmem_limit_bytes=VMEM_LIMIT),
@@ -436,23 +424,31 @@
             flops=4 * rows * width * 2048, bytes_accessed=12 << 20, transcendentals=0
         ),
         name="attention_forward",
-    )(starts, query_low, key_all, value_all, firsts, gate_pre)
+    )(starts, query_low, kv_all, firsts, gate_pre)
 
 
 def attention_backward_kernel(
-    start_ref, query_ref, grad_ref, att_ref, inv_ref, key_ref, keyt_ref, value_ref, first_ref,
-    dq_ref, kv_ref, dk_acc, dv_acc, dqt,
+    start_ref, query_ref, grad_ref, att_ref, inv_ref, kvs_ref, first_ref,
+    dq_ref, kv_ref, dk_acc, dv_acc, dqt, keyt,
 ):
     blocks = start_ref.shape[0]
-    groups = key_ref.shape[1] // LANES
-    per = query_ref.shape[1] // key_ref.shape[1]
+    kv_width = kvs_ref.shape[1] // 2
+    groups = kv_width // LANES
+    per = query_ref.shape[1] // kv_width
     rows = query_ref.shape[0] // blocks
-    wide_count = key_ref.shape[0] // query_ref.shape[0]
+    wide_count = kvs_ref.shape[0] // query_ref.shape[0]
     wide_pos = lax.axis_index("wide")
     step = KEY_BLOCK
     scale = LANES ** (-0.5)
     dk_acc[...] = jnp.zeros_like(dk_acc)
     dv_acc[...] = jnp.zeros_like(dv_acc)
+
+    @pl.loop(0, kvs_ref.shape[0] // step)
+    def _(tile):
+        there = pl.ds(pl.multiple_of(tile * step, step), step)
+        for g in range(groups):
+            cols = slice(g * LANES, (g + 1) * LANES)
+            keyt[cols, there] = jnp.transpose(kvs_ref[there, cols])
 
     @pl.loop(0, blocks)
     def _(blk):
@@ -489,13 +485,14 @@
             allowed = jnp.concatenate([allowed] * per, axis=1)
             for g in range(groups):
                 cols = slice(g * LANES, (g + 1) * LANES)
+                value_cols = slice(kv_width + g * LANES, kv_width + (g + 1) * LANES)
                 scores = lax.dot_general(
-                    key_ref[there, cols], queries[g], (((1,), (1,)), ((), ())),
+                    kvs_ref[there, cols], queries[g], (((1,), (1,)), ((), ())),
                     preferred_element_type=jnp.float32,
                 )
                 probs = jnp.where(allowed, jnp.exp2(scores * (scale * LOG2E)), 0.0)
                 dprobs = lax.dot_general(
-                    value_ref[there, cols], grads[g], (((1,), (1,)), ((), ())),
+                    kvs_ref[there, value_cols], grads[g], (((1,), (1,)), ((), ())),
                     preferred_element_type=jnp.float32,
                 )
                 dscores = (probs * (dprobs - deltas[g]) * scale).astype(jnp.bfloat16)
@@ -506,7 +503,7 @@
                     dscores, queries[g], preferred_element_type=jnp.float32
                 )
                 dqt[g] += jnp.dot(
-                    keyt_ref[cols, there], dscores, preferred_element_type=jnp.float32
+                    keyt[cols, there], dscores, preferred_element_type=jnp.float32
                 )
 
         for g in range(groups):
@@ -526,10 +523,10 @@
 
 
 def attention_backward(
-    query_low, grad_low, attended, inverse, key_all, value_all, starts, firsts
+    query_low, grad_low, attended, inverse, kv_all, starts, firsts
 ):
     rows, width = query_low.shape
-    keys, kv_width = key_all.shape
+    keys, kv_width = kv_all.shape[0], kv_all.shape[1] // 2
     groups = kv_width // LANES
     per = width // kv_width
     blocks = starts.shape[0]
@@ -540,19 +537,20 @@
             jax.ShapeDtypeStruct((rows, width), jnp.float32),
             jax.ShapeDtypeStruct((keys, 2 * kv_width), jnp.bfloat16),
         ),
-        in_specs=[pl.BlockSpec(memory_space=pltpu.SMEM)] + [vmem] * 8,
+        in_specs=[pl.BlockSpec(memory_space=pltpu.SMEM)] + [vmem] * 6,
         out_specs=(vmem, vmem),
         scratch_shapes=[
             pltpu.VMEM((keys, kv_width), jnp.float32),
             pltpu.VMEM((keys, kv_width), jnp.float32),
             pltpu.VMEM((groups, LANES, per * (rows // blocks)), jnp.float32),
+            pltpu.VMEM((kv_width, keys), jnp.bfloat16),
         ],
         compiler_params=pltpu.CompilerParams(vmem_limit_bytes=VMEM_LIMIT),
         cost_estimate=pl.CostEstimate(
             flops=10 * rows * width * 2048, bytes_accessed=20 << 20, transcendentals=0
         ),
         name="attention_backward",
-    )(starts, query_low, grad_low, attended, inverse, key_all, key_all.T, value_all, firsts)
+    )(starts, query_low, grad_low, attended, inverse, kv_all, firsts)
 
 
 def ffn_kernel(
@@ -901,6 +899,187 @@
         ),
         name="ffn_block",
     )(gated_low, inputs, cotangent, ffn_gain[None], out_w, gate_w, up_w, down_w)
+
+
+def turn(values, cosine, sine_tab):
+    half = LANES // 2
+    lane = lax.broadcasted_iota(jnp.int32, values.shape, 1)
+    turned = pltpu.roll(values, half, 1)
+    return values * cosine + jnp.where(lane < half, -turned, turned) * sine_tab
+
+
+def prep(pre_proj, gain, cosine, sine_tab):
+    scale = lax.rsqrt(jnp.mean(pre_proj * pre_proj, axis=-1, keepdims=True) + EPS)
+    return turn(pre_proj * scale * gain, cosine, sine_tab).astype(jnp.bfloat16)
+
+
+def front_kernel(
+    x_ref, gain_ref, cos_ref, sin_ref, qgain_ref, kgain_ref, wq_any, wk_any, wv_any, wg_any,
+    query_ref, qpre_ref, kpre_ref, gpre_ref, normed_any, kv_any,
+    wq, wk, wv, wg, normed, kv, local_sem, hs, hr, ks, kr, kps, kpr,
+):
+    tok, width = x_ref.shape
+    kv_width = wk_any.shape[1]
+    q_width = wq_any.shape[1]
+    wide_count, head_count = lax.axis_size("wide"), lax.axis_size("head")
+    head, wide = head_ring(), wide_ring()
+    loads = [
+        pltpu.make_async_copy(src, dst, local_sem.at[i])
+        for i, (src, dst) in enumerate(((wk_any, wk), (wv_any, wv), (wq_any, wq), (wg_any, wg)))
+    ]
+    for load in loads:
+        load.start()
+    own = pl.multiple_of(lax.axis_index("head") * tok, tok)
+    own_wide = lax.axis_index("wide")
+
+    def norm(row):
+        here = pl.ds(row, 32)
+        value = x_ref[here, :].astype(jnp.float32)
+        scale = lax.rsqrt(jnp.mean(value * value, axis=-1, keepdims=True) + EPS)
+        normed[pl.ds(pl.multiple_of(own + row, 32), 32), :] = (
+            value * scale * gain_ref[...]
+        ).astype(jnp.bfloat16)
+
+    row_loop(tok, 32, norm)
+    meet(neighbours(head, wide))
+    gather = Gather(
+        head, lambda index, start, size: normed.at[pl.ds(index * tok + start, size)], tok, hs, hr
+    )
+    gather.start(1)
+
+    def kv_gather(offset):
+        slot = offset % head_count
+        block = head.index(offset)
+
+        def place(index, start, size):
+            return kv.at[pl.ds((block * wide_count + index) * tok + start, size)]
+
+        return PairGather(
+            wide, place, tok, ks.at[slot], kr.at[slot], kps.at[slot], kpr.at[slot]
+        )
+
+    def project(offset):
+        block = head.index(offset)
+        here = pl.ds(pl.multiple_of(block * tok, tok), tok)
+        there = pl.ds(pl.multiple_of((block * wide_count + own_wide) * tok, tok), tok)
+        left = normed[here, :]
+        cosine, sine_tab = cos_ref[here, :], sin_ref[here, :]
+        pre = dot_nn(left, wk[...])
+        kpre_ref[here, :] = pre
+        for j in range(kv_width // LANES):
+            cols = slice(j * LANES, (j + 1) * LANES)
+            kv[there, cols] = prep(pre[:, cols], kgain_ref[...], cosine, sine_tab)
+        kv[there, kv_width:] = dot_nn(left, wv[...]).astype(jnp.bfloat16)
+
+    def project_rest(offset):
+        block = head.index(offset)
+        here = pl.ds(pl.multiple_of(block * tok, tok), tok)
+        left = normed[here, :]
+        cosine, sine_tab = cos_ref[here, :], sin_ref[here, :]
+        pre = dot_nn(left, wq[...])
+        qpre_ref[here, :] = pre
+        for j in range(q_width // LANES):
+            cols = slice(j * LANES, (j + 1) * LANES)
+            query_ref[here, cols] = prep(pre[:, cols], qgain_ref[...], cosine, sine_tab)
+        gpre_ref[here, :] = dot_nn(left, wg[...])
+
+    gathers = {}
+
+    def launch(offset):
+        project(offset)
+        gathers[offset] = kv_gather(offset)
+        gathers[offset].begin()
+
+    def step(offset, hop):
+        gathers[offset].arrive(hop)
+        if hop < wide.half:
+            gathers[offset].start(hop + 1)
+        gathers[offset].hand(hop)
+
+    loads[0].wait()
+    loads[1].wait()
+    launch(0)
+    loads[2].wait()
+    loads[3].wait()
+    project_rest(0)
+    done = [0]
+    for hop in range(1, head.half + 1):
+        gather.arrive(hop)
+        if hop < head.half:
+            gather.start(hop + 1)
+            launch(hop)
+            launch(-hop)
+            for offset in done:
+                step(offset, 1)
+            project_rest(hop)
+            project_rest(-hop)
+            done = [hop, -hop]
+        else:
+            launch(hop)
+            for offset in done:
+                step(offset, 1)
+            project_rest(hop)
+            done = [hop]
+    gather.finish()
+    keep = pltpu.make_async_copy(normed, normed_any, local_sem.at[4])
+    keep.start()
+    for offset in done:
+        step(offset, 1)
+    for hop in range(2, wide.half + 1):
+        for offset in gathers:
+            step(offset, hop)
+    for each in gathers.values():
+        for hop in range(wide.half + 1):
+            each.take(hop)
+    store = pltpu.make_async_copy(kv, kv_any, local_sem.at[5])
+    store.start()
+    for each in gathers.values():
+        each.finish()
+    store.wait()
+    keep.wait()
+
+
+def front_block(inputs, attn_gain, cosine, sine_tab, query_gain, key_gain, weights):
+    tok, width = inputs.shape
+    head_count, wide_count = lax.axis_size("head"), lax.axis_size("wide")
+    chips = wide_count // 2
+    q_width, kv_width = weights[0].shape[1], weights[1].shape[1]
+    rows = head_count * tok
+    low, full = jnp.bfloat16, jnp.float32
+    shape, vm = jax.ShapeDtypeStruct, pltpu.VMEM
+    half = chips // 2
+    return pl.pallas_call(
+        front_kernel,
+        out_shape=(
+            shape((rows, q_width), low),
+            shape((rows, q_width), full),
+            shape((rows, kv_width), full),
+            shape((rows, q_width), full),
+            shape((rows, width), low),
+            shape((rows * wide_count, 2 * kv_width), low),
+        ),
+        in_specs=[VMEM] * 6 + [ANY] * 4,
+        out_specs=tuple([VMEM] * 4 + [ANY] * 2),
+        scratch_shapes=[
+            *[vm(weight.shape, low) for weight in weights],
+            vm((rows, width), low),
+            vm((rows * wide_count, 2 * kv_width), low),
+            DMA((6,)),
+            *ring_sems(head_count),
+            DMA((head_count, 2, half)), DMA((head_count, 2, half)),
+            DMA((head_count, 2, half + 1)), DMA((head_count, 2, half + 1)),
+        ],
+        compiler_params=pltpu.CompilerParams(
+            collective_id=3, has_side_effects=True, vmem_limit_bytes=VMEM_LIMIT
+        ),
+        cost_estimate=pl.CostEstimate(
+            flops=2 * rows * width * (2 * q_width + 2 * kv_width), bytes_accessed=100 << 20,
+            transcendentals=0,
+        ),
+        name="front_block",
+    )(
+        inputs, attn_gain[None], cosine, sine_tab, query_gain[None], key_gain[None], *weights
+    )
 
 
 def turn_back(grad, cosine, sine_tab):
@@ -1297,39 +1476,12 @@
     starts = query_first[::tok_dev]
     firsts = query_first[:, None]
     cosine, sine_tab = rotary(query_pos, head_width)
-    block_in = inputs.astype(jnp.float32)
-    normed_low = rms_apply(block_in, attn_gain).astype(jnp.bfloat16)
-    gathered = lax.all_gather(normed_low, "head", axis=0, tiled=True)
-    query_pre = jnp.dot(gathered, query_weight, preferred_element_type=jnp.float32)
-    key_pre = jnp.dot(gathered, key_projection, preferred_element_type=jnp.float32)
-    value_pre = jnp.dot(gathered, value_projection, preferred_element_type=jnp.float32)
-    gate_pre = jnp.dot(gathered, attn_gate_weight, preferred_element_type=jnp.float32)
-
-    def prep_heads(pre_proj, gain_vec):
-        return head_prep(pre_proj, gain_vec, cosine, sine_tab)
-
-    query_rot = prep_heads(query_pre, query_gain)
-    key_rot = prep_heads(key_pre, key_gain)
-    query_low = query_rot.astype(jnp.bfloat16)
-    key_low = key_rot.astype(jnp.bfloat16)
-    value_low = value_pre.astype(jnp.bfloat16)
-    key_wide, value_wide = (
-        lax.all_gather(key_low, "wide", axis=0, tiled=True),
-        lax.all_gather(value_low, "wide", axis=0, tiled=True),
-    )
-    kv_width = key_wide.shape[1]
-
-    def natural_order(matrix):
-        return (
-            matrix.reshape(wide_count, head_count, tok_dev, kv_width)
-            .transpose(1, 0, 2, 3)
-            .reshape(-1, kv_width)
-        )
-
-    key_entire = natural_order(key_wide)
-    value_entire = natural_order(value_wide)
+    weights = (query_weight, key_projection, value_projection, attn_gate_weight)
+    query_low, query_pre, key_pre, gate_pre, gathered, kv_all = front_block(
+        inputs, attn_gain, cosine, sine_tab, query_gain, key_gain, weights
+    )
     attended, inverse, gated_low = attention_forward(
-        query_low, key_entire, value_entire, starts, firsts, gate_pre
+        query_low, kv_all, starts, firsts, gate_pre
     )
     gate_sig = jax.nn.sigmoid(gate_pre)
     (
@@ -1354,7 +1506,7 @@
     attended_grad_low = (gated_grad * gate_sig).astype(jnp.bfloat16)
     gate_pre_grad_low = (gated_grad * attended * gate_sig * (1.0 - gate_sig)).astype(jnp.bfloat16)
     query_rot_grad, kv_parts = attention_backward(
-        query_low, attended_grad_low, attended, inverse, key_entire, value_entire, starts, firsts
+        query_low, attended_grad_low, attended, inverse, kv_all, starts, firsts
     )
     (
         input_grad,
@@ -1383,7 +1535,7 @@
         gated_low,
         gathered,
         back_rows,
-        (query_weight, key_projection, value_projection, attn_gate_weight),
+        weights,
         gate_wgrad,
         up_wgrad,
     )

time: 466 us -> 403 us (0.86)
  waiting for transfers between devices: 75.8 us -> 0 us
  Pallas kernels: 320 us -> 379 us
  local copies, waits for them, and re-layouts: 30 us -> 15.5 us
  between operations: 14.1 us -> 0.71 us
  matrix products: 16 us -> 5.26 us
  other arithmetic: 9.08 us -> 3.58 us
    all_gather x3 -> x0, waiting for transfers between devices: 75.7 us -> none  [the longest x1 38.1 us: shards(): gathered = lax.all_gather(normed_low, 'head', axis=0, tiled=True)]
    pallas_call x0 -> x1, Pallas kernels: none -> 53.8 us  [front_block(): pl.pallas_call(front_kernel, out_shape=(shape((rows, q_width), low), shap...]
    dot_general x4 -> x0, matrix products: 10.8 us -> none  [the longest x1 3.53 us: shards(): jnp.dot(gathered, query_weight, preferred_element_type=jnp.float32)]
    reshape x4 -> x0, local copies, waits for them, and re-layouts: 9.33 us -> none  [the longest x3 6.72 us: natural_order(): matrix.reshape(wide_count, head_count, tok_dev, kv_width)]
    convert_element_type x3 -> x0, other arithmetic: 5.58 us -> none  [the longest x1 2.69 us: shards(): query_low = query_rot.astype(jnp.bfloat16)]
    unnamed x53 -> x28, local copies, waits for them, and re-layouts: 12.8 us -> 11.2 us
  transfers between devices with their start and end apart: 3 -> 0, of which waited for: 3 -> 0; matrix products, arithmetic and copies ran while one was open for 5% -> 0% of each run, Pallas kernels for 0% -> 0%
where the time goes in v4:
time: 403 us; the launch traced here: 404 us
  Pallas kernels  379 us (94%)
  local copies, waits for them, and re-layouts  15.5 us (4%)
  matrix products  5.26 us (1%)
    pallas_call x1, Pallas kernels, ffn_block(): pl.pallas_call(ffn_kernel, out_shape=(shape((tok, width), low), shape((to...  168 us
    pallas_call x1, Pallas kernels, tail_block(): pl.pallas_call(tail_kernel, out_shape=(shape((tok, width), full), shape((...  125 us
    pallas_call x1, Pallas kernels, front_block(): pl.pallas_call(front_kernel, out_shape=(shape((rows, q_width), low), shap...  53.8 us
    pallas_call x1, Pallas kernels, attention_backward(): pl.pallas_call(attention_backward_kernel, out_shape=(jax.ShapeDtypeStruct...  19.7 us
    pallas_call x1, Pallas kernels, attention_forward(): pl.pallas_call(attention_forward_kernel, out_shape=(jax.ShapeDtypeStruct(...  12.3 us
    unnamed x28, local copies, waits for them, and re-layouts  11.2 us

profile of v4, /device:TPU:0, one launch (start us, length us, event | category | flops | bytes accessed | tf_op | source)
XLA Modules:
  0.0 403.9 jit_solution(13137431926731340981)
XLA Ops:
  0.6 0.8 reduce-window.8
  1.5 0.7 select_reduce_fusion
  2.2 0.6 slice.15.start_ref
  2.9 0.9 copy.31.first_ref
  3.7 1.0 multiply_sine_fusion
  4.7 1.0 pad_maximum_fusion
  5.7 53.8 %front_block.1 = (bf16[512,512]{1,0:T(8,128)(2,1)}, f32[512,512]{1,0:T(8,128)}, f32[512,256]{1,0:T(8,128)}, f32[512,512]{1,0:T(8,128)}, bf16[512,2048]{1,0:T(8,128)(2,1)}, /*index=5*/bf16[4096,512]{1,0:T(8,128)(2,1)}) custom-call(bf16[128,2048]{1,0:T(8,128)(2,1)} %x_ref.5, f32[1,2048]{1,0:T(1,128)} %bitcast.23, f32[512,128]{1,0:T(8,128)} %get-tuple-element.76.cos_ref, ...), custom_call_target="tpu_custom_call" | custom-call | flops 3221225472 | bytes 104857600 | tf_op jit(solution)/shard_map/front_block/pallas_call | solution.py:1051
  59.5 12.3 %attention_forward.1 = (f32[512,512]{1,0:T(8,128)}, f32[512,512]{1,0:T(8,128)}, bf16[512,512]{1,0:T(8,128)(2,1)}) custom-call(s32[4]{0:T(128)} %slice.15.start_ref, bf16[512,512]{1,0:T(8,128)(2,1)} %get-tuple-element.41.query_ref, bf16[4096,512]{1,0:T(8,128)(2,1)} %get-tuple-element.42.kv_ref.kvs_ref, s32[512,1]{1,0:T(8,128)} %copy.31.first_ref, ...), custom_call_target="tpu_custom_call" | custom-call | flops 2147483648 | bytes 12582912 | tf_op jit(solution)/shard_map/attention_forward/pallas_call | solution.py:412
  71.8 168.1 %ffn_block.1 = (bf16[128,2048]{1,0:T(8,128)(2,1)}, f32[128,2048]{1,0:T(8,128)}, f32[1,2048]{1,0:T(1,128)}, bf16[512,2048]{1,0:T(8,128)(2,1)}, f32[768,512]{1,0:T...) custom-call(bf16[512,512]{1,0:T(8,128)(2,1)} %get-tuple-element.44.gated_ref, bf16[128,2048]{1,0:T(8,128)(2,1)} %x_ref.5, ...), custom_call_target="tpu_custom_call" | custom-call | flops 16106127360 | bytes 209715200 | tf_op jit(solution)/shard_map/ffn_block/pallas_call | solution.py:855
  239.9 5.3 %multiply_convert_fusion = (bf16[512,512]{1,0:T(8,128)(2,1)}, bf16[512,512]{1,0:T(8,128)(2,1)}) fusion(f32[512,512]{1,0:T(8,128)} %get-tuple-element.47.att_ref, f32[512,512]{1,0:T(8,128)} %get-tuple-element.43.gate_ref, bf16[512,2048]{1,0:T(8,128)(2,1)} %get-tuple-element.46.back_any, bf16[512,2048]{1,0:T(8,128)(2,1)} %wo_any.1), kind=kOutput, calls=%fused_computation | convolution fusion | flops 1076363264 | bytes 7340032 | tf_op jit(solution)/shard_map/dot_general | solution.py:1445
  245.2 19.7 %attention_backward.1 = (f32[512,512]{1,0:T(8,128)}, bf16[4096,512]{1,0:T(8,128)(2,1)}) custom-call(s32[4]{0:T(128)} %slice.15.start_ref, bf16[512,512]{1,0:T(8,128)(2,1)} %get-tuple-element.41.query_ref, bf16[512,512]{1,0:T(8,128)(2,1)} %get-tuple-element.69.grad_ref, f32[512,512]{1,0:T(8,128)} %get-tuple-element.47.att_ref, ...), custom_call_target="tpu_custom_call" | custom-call | flops 5368709120 | bytes 20971520 | tf_op jit(solution)/shard_map/attention_backward/pallas_call | solution.py:534
  264.9 0.0 copy-start.3
  264.9 125.0 %tail_block.1 = (f32[128,2048]{1,0:T(8,128)}, f32[8,2048]{1,0:T(8,128)}, f32[256,512]{1,0:T(8,128)}, f32[256,256]{1,0:T(8,128)}, f32[256,256]{1,0:T(8,128)}, /*i...) custom-call(f32[512,512]{1,0:T(8,128)} %get-tuple-element.49.dq_ref, ...), custom_call_target="tpu_custom_call" | custom-call | flops 10737418240 | bytes 314572800 | tf_op jit(solution)/shard_map/tail_block/pallas_call | solution.py:1395
  389.9 0.0 copy-start.6
  389.9 1.3 slice_bitcast_fusion
  391.1 1.5 fusion.11
  392.7 0.0 copy-done.3
  392.7 0.0 copy-start.8
  392.7 0.8 copy.43
  393.5 0.0 copy-start.7
  393.5 0.0 copy-start.5
  393.5 2.4 copy.44
  395.8 0.0 copy-done.6
  395.8 0.0 copy-start.4
  395.8 0.0 copy-start.2
  395.8 0.8 copy.45
  396.6 0.0 copy-done.8
  396.6 0.7 copy.46
  397.3 0.0 copy-done.7
  397.3 0.7 copy.47
  398.0 0.0 copy-done.5
  398.0 0.8 copy.48
  398.8 0.0 copy-done.4
  398.8 0.0 copy-start.1
  398.8 0.8 copy.49
  399.6 0.0 copy-done.2
  399.6 1.1 copy.50
  400.8 0.0 copy-done.1
  400.8 0.0 copy-start
  400.8 1.1 copy.51
  401.9 0.8 copy-done
  402.8 1.1 copy.52
  (3 shorter events, 0.0 us)
Async XLA Ops:
  264.9 127.8 %copy-start.3 = (bf16[128,2048]{1,0:T(8,128)(2,1)S(1)}, bf16[128,2048]{1,0:T(8,128)(2,1)}, u32[]{:S(2)}) copy-start(bf16[128,2048]{1,0:T(8,128)(2,1)} %get-tuple-element.92) | copy-start | bytes 1572868
  389.9 6.0 %copy-start.6 = (f32[256,512]{1,0:T(8,128)S(1)}, f32[256,512]{1,0:T(8,128)}, u32[]{:S(2)}) copy-start(f32[256,512]{1,0:T(8,128)} %get-tuple-element.95) | copy-start | bytes 1572868
  392.7 4.0 copy-start.8
  393.5 3.9 copy-start.7
  393.5 4.6 %copy-start.5 = (f32[256,512]{1,0:T(8,128)S(1)}, f32[256,512]{1,0:T(8,128)}, u32[]{:S(2)}) copy-start(f32[256,512]{1,0:T(8,128)} %get-tuple-element.98) | copy-start | bytes 1572868
  395.8 3.0 copy-start.4
  395.8 3.8 copy-start.2
  398.8 1.9 copy-start.1
  400.8 2.0 copy-start

commit v5 on v4

--- a/solution.py
+++ b/solution.py
@@ -1,3 +1,5 @@
+import functools
+
 import jax
 import jax.numpy as jnp
 from jax import lax
@@ -10,13 +12,10 @@
 VMEM_LIMIT = 63 << 20
 
 
-def token_tables(doc_lengths, token_ids):
+def token_position(doc_lengths, token_ids):
     lengths = doc_lengths.reshape(-1)
-    doc_ends = jnp.cumsum(lengths)
-    before = doc_ends[None, :] <= token_ids[:, None]
-    document_segment = jnp.sum(before.astype(jnp.int32), axis=1)
-    doc_first = jnp.sum(jnp.where(before, lengths[None, :], 0), axis=1)
-    return (document_segment, token_ids - doc_first, doc_first)
+    before = jnp.cumsum(lengths)[None, :] <= token_ids[:, None]
+    return token_ids - jnp.sum(jnp.where(before, lengths[None, :], 0), axis=1)
 
 
 def rotary(position, head_width):
@@ -317,6 +316,274 @@
     return [DMA((2, size // 2 + 1)), DMA((2, size // 2 + 1))]
 
 
+NEAR, OTHER, FAR = 0, 1, 2
+
+
+class LineGather:
+    pieces = 2
+
+    def __init__(self, ring, slot, rows, send, recv, pass_send, pass_recv):
+        self.ring, self.slot, self.rows = ring, slot, rows // self.pieces
+        self.send, self.recv, self.pass_send, self.pass_recv = send, recv, pass_send, pass_recv
+        pos = ring.pos
+        half, odd = lax.div(pos, 2), lax.rem(pos, 2)
+        self.way = 1 - 2 * odd
+        self.middle = half + odd == 1
+
+    def offset(self, kind):
+        return {NEAR: self.way, OTHER: -self.way, FAR: 2}[kind]
+
+    def ref(self, offset, piece):
+        index = 2 * self.ring.index(offset) + self.ring.core
+        return self.slot(index, piece * self.rows, self.rows)
+
+    def copy(self, which, offset, kind, piece, way):
+        ref = self.ref(offset, piece)
+        return remote(
+            ref, ref, self.send.at[which, piece], self.recv.at[kind, piece],
+            self.ring.device(way),
+        )
+
+    def own(self, piece):
+        return self.copy(0, 0, NEAR, piece, self.way)
+
+    def own_other(self, piece):
+        return self.copy(1, 0, OTHER, piece, -self.way)
+
+    def onward(self, kind, piece):
+        arrives = {NEAR: FAR, OTHER: FAR, FAR: OTHER}[kind]
+        way = -self.way if kind == NEAR else self.way
+        return self.copy(2 + kind, self.offset(kind), arrives, piece, way)
+
+    def incoming(self, kind, piece):
+        return self.copy(0, self.offset(kind), kind, piece, self.way)
+
+    def handed(self, kind, piece):
+        ref = self.ref(0 if kind is None else self.offset(kind), piece)
+        slot = 3 if kind is None else kind
+        return remote(
+            ref, ref, self.pass_send.at[slot, piece], self.pass_recv.at[slot, piece],
+            self.ring.sibling,
+        )
+
+    def begin(self):
+        for piece in range(self.pieces):
+            self.own(piece).start()
+
+            @pl.when(self.middle)
+            def _():
+                self.own_other(piece).start()
+
+            self.handed(None, piece).start()
+
+    def arrive(self, kind):
+        for piece in range(self.pieces):
+            self.incoming(kind, piece).wait_recv()
+
+            @pl.when(self.middle)
+            def _():
+                self.onward(kind, piece).start()
+
+            self.handed(kind, piece).start()
+
+    def take(self, kind):
+        for piece in range(self.pieces):
+            self.handed(kind, piece).wait_recv()
+
+    def finish(self):
+        for piece in range(self.pieces):
+            self.own(piece).wait_send()
+
+            @pl.when(self.middle)
+            def _():
+                self.own_other(piece).wait_send()
+                for kind in (NEAR, OTHER, FAR):
+                    self.onward(kind, piece).wait_send()
+
+            for kind in (None, NEAR, OTHER, FAR):
+                self.handed(kind, piece).wait_send()
+
+
+class LineScatter(PairScatter):
+    pieces = 2
+
+    def __init__(self, *args):
+        super().__init__(*args)
+        pos = self.ring.pos
+        half, odd = lax.div(pos, 2), lax.rem(pos, 2)
+        self.way = 1 - 2 * odd
+        self.middle = half + odd == 1
+        self.waited = set()
+
+    def offset(self, kind):
+        return {NEAR: self.way, OTHER: -self.way, FAR: 2, None: 0}[kind]
+
+    def piece_of(self, piece):
+        size = self.rows // self.pieces
+        return piece * size, size
+
+    def outgoing(self, kind, slot, piece, way):
+        first, size = self.piece_of(piece)
+        ref, base = self.part(self.ring.index(self.offset(kind)))
+        return remote(
+            ref.at[pl.ds(pl.multiple_of(base + first, size), size)],
+            self.into.at[slot, pl.ds(first, size)],
+            self.send.at[kind, piece], self.recv.at[slot, piece], self.ring.device(way),
+        )
+
+    def from_end(self, kind, piece):
+        return self.outgoing(kind, {OTHER: 0, FAR: 1, NEAR: 2}[kind], piece, self.way)
+
+    def from_middle(self, kind, piece):
+        slot = {FAR: 3, OTHER: 4, NEAR: 0}[kind]
+        return self.outgoing(kind, slot, piece, self.way if kind == NEAR else -self.way)
+
+    def landed(self, slot, piece):
+        first, size = self.piece_of(piece)
+        ref = self.into.at[slot, pl.ds(first, size)]
+        remote(
+            ref, ref, self.send.at[0, piece], self.recv.at[slot, piece], self.ring.device(self.way)
+        ).wait_recv()
+
+    def hand_kind(self, kind):
+        self.swap(kind).start()
+
+    def swap(self, kind):
+        index = self.ring.index(self.offset(kind))
+        other = pl.multiple_of((2 * index + 1 - self.ring.core) * self.rows, self.rows)
+        slot = 3 if kind is None else kind
+        return remote(
+            self.terms.at[pl.ds(other, self.rows)], self.passed.at[slot],
+            self.pass_send.at[slot], self.pass_recv.at[slot], self.ring.sibling,
+        )
+
+    def merge_kind(self, kind):
+        self.swap(kind).wait_recv()
+        slot = 3 if kind is None else kind
+        ref, base = self.part(self.ring.index(self.offset(kind)))
+
+        def add(row):
+            there = pl.ds(pl.multiple_of(base + row, 32), 32)
+            ref[there, :] = (
+                ref[there, :].astype(jnp.float32)
+                + self.passed[slot, pl.ds(row, 32), :].astype(jnp.float32)
+            ).astype(ref.dtype)
+
+        row_loop(self.rows, 32, add)
+
+    def launch(self, *kinds):
+        @pl.when(~self.middle)
+        def _():
+            for kind in kinds:
+                for piece in range(self.pieces):
+                    self.from_end(kind, piece).start()
+
+    def sent(self, kind):
+        self.waited.add(kind)
+
+        @pl.when(~self.middle)
+        def _():
+            for piece in range(self.pieces):
+                self.from_end(kind, piece).wait_send()
+
+    def relay(self, kind):
+        slot = {FAR: 0, OTHER: 1, NEAR: 3}[kind]
+
+        @pl.when(self.middle)
+        def _():
+            ref, base = self.part(self.ring.index(self.offset(kind)))
+            for piece in range(self.pieces):
+                first, size = self.piece_of(piece)
+                self.landed(slot, piece)
+
+                def add(row):
+                    there = pl.ds(pl.multiple_of(base + first + row, 32), 32)
+                    here = pl.ds(pl.multiple_of(first + row, 32), 32)
+                    ref[there, :] = (
+                        ref[there, :].astype(jnp.float32)
+                        + self.into[slot, here, :].astype(jnp.float32)
+                    ).astype(ref.dtype)
+
+                row_loop(size, 32, add)
+                self.from_middle(kind, piece).start()
+
+    def arrive(self):
+        @pl.when(self.middle)
+        def _():
+            for piece in range(self.pieces):
+                self.landed(2, piece)
+                self.landed(4, piece)
+
+            def add(row):
+                here = pl.ds(row, 32)
+                self.into[0, here, :] = (
+                    self.into[2, here, :].astype(jnp.float32)
+                    + self.into[4, here, :].astype(jnp.float32)
+                ).astype(self.into.dtype)
+
+            row_loop(self.rows, 32, add)
+
+        @pl.when(~self.middle)
+        def _():
+            for piece in range(self.pieces):
+                self.landed(0, piece)
+
+    def total(self, row, count):
+        ref, base = self.part(self.ring.index(0))
+        there = pl.ds(pl.multiple_of(base + row, count), count)
+        return ref[there, :].astype(jnp.float32) + self.into[0, pl.ds(row, count), :].astype(
+            jnp.float32
+        )
+
+    def finish(self):
+        for piece in range(self.pieces):
+
+            @pl.when(self.middle)
+            def _():
+                for kind in (NEAR, OTHER, FAR):
+                    self.from_middle(kind, piece).wait_send()
+
+            @pl.when(~self.middle)
+            def _():
+                for kind in (NEAR, OTHER, FAR):
+                    if kind not in self.waited:
+                        self.from_end(kind, piece).wait_send()
+
+        for kind in (NEAR, OTHER, FAR, None):
+            self.swap(kind).wait_send()
+
+
+def scatter_of(ring):
+    return LineScatter if ring.size == 4 else PairScatter
+
+
+def scatter_into(size, rows, columns):
+    if size == 4:
+        return pltpu.VMEM((5, rows, columns), jnp.bfloat16)
+    return into_shape(size, rows, columns)
+
+
+def scatter_sems(size):
+    passed = [DMA((size,)), DMA((size,))]
+    if size == 4:
+        pieces = LineScatter.pieces
+        return [DMA((3, pieces)), DMA((5, pieces)), *passed]
+    return [*ring_sems(size), *passed]
+
+
+def line_sems():
+    pieces = LineGather.pieces
+    return [DMA((5, pieces)), DMA((3, pieces)), DMA((4, pieces)), DMA((4, pieces))]
+
+
+def gather_sems(size):
+    return line_sems() if size == 4 else [*ring_sems(size), *pass_sems(size)]
+
+
+def row_gather_of(ring):
+    return LineGather if ring.size == 4 else PairGather
+
+
 def dot_nn(left, right):
     return jnp.dot(left, right, preferred_element_type=jnp.float32)
 
@@ -334,44 +601,88 @@
 
 
 LANES = 128
-KEY_BLOCK = 512
+FORWARD_KEYS = 1024
+BACKWARD_KEYS = 512
 LOG2E = 1.4426950408889634
 
 
+def doc_ends(doc_ref):
+    ends, total = [], jnp.int32(0)
+    for row in range(doc_ref.shape[0]):
+        for doc in range(doc_ref.shape[1]):
+            total = total + doc_ref[row, doc]
+            ends.append(total)
+    return ends
+
+
+def first_of(ends, tokens):
+    first = jnp.zeros_like(tokens)
+    for end in ends:
+        first = jnp.maximum(first, jnp.where(tokens >= end, end, 0))
+    return first
+
+
+def start_all(copies):
+    for copy in copies:
+        copy.start()
+
+
 def attention_forward_kernel(
-    start_ref, query_ref, kv_ref, first_ref, gate_ref, att_ref, inv_ref, gated_ref, acc
+    doc_ref, query_any, kv_any, gate_any, att_any, inv_any, gated_any,
+    query, kv, gate, att, inv, gated, acc, kv_sem, in_sem, out_sem,
 ):
-    blocks = start_ref.shape[0]
-    kv_width = kv_ref.shape[1] // 2
+    wide_count = lax.axis_size("wide")
+    wide_pos = lax.axis_index("wide")
+    kv_width = kv.shape[1] // 2
     groups = kv_width // LANES
-    per = query_ref.shape[1] // kv_width
-    rows = query_ref.shape[0] // blocks
-    wide_count = kv_ref.shape[0] // query_ref.shape[0]
-    wide_pos = lax.axis_index("wide")
-    step = KEY_BLOCK
+    per = query.shape[1] // kv_width
+    blocks = kv_sem.shape[0]
+    rows = query.shape[0] // blocks
+    step = min(FORWARD_KEYS, rows * wide_count)
     factor = LANES ** (-0.5) * LOG2E
+    chunk = rows * wide_count
+
+    def kv_copy(blk):
+        there = pl.ds(pl.multiple_of(blk * chunk, chunk), chunk)
+        return pltpu.make_async_copy(kv_any.at[there], kv.at[there], kv_sem.at[blk])
+
+    early = [
+        pltpu.make_async_copy(query_any, query, in_sem.at[0]),
+        pltpu.make_async_copy(gate_any, gate, in_sem.at[1]),
+    ]
+    early[0].start()
+    for blk in range(blocks):
+        kv_copy(blk).start()
+    early[1].start()
+    ends = doc_ends(doc_ref)
+    early[0].wait()
+
+    def out_copies(blk):
+        here = pl.ds(pl.multiple_of(blk * rows, rows), rows)
+        return [
+            pltpu.make_async_copy(src.at[here], dst.at[here], out_sem.at[i, blk])
+            for i, (src, dst) in enumerate(((att, att_any), (inv, inv_any), (gated, gated_any)))
+        ]
 
     @pl.loop(0, blocks)
     def _(blk):
         here = pl.ds(pl.multiple_of(blk * rows, rows), rows)
         first_tok = (blk * wide_count + wide_pos) * rows
         key_lane = lax.broadcasted_iota(jnp.int32, (rows, step), 1)
-        query_row = lax.broadcasted_iota(jnp.int32, (rows, step), 0) + first_tok
-        upper = key_lane - query_row
-        lower = key_lane - first_ref[here, :]
+        tokens = lax.broadcasted_iota(jnp.int32, (rows, 1), 0) + first_tok
+        upper = key_lane - tokens
+        lower = key_lane - first_of(ends, tokens)
         queries = [
             jnp.concatenate(
-                [
-                    query_ref[here, (g * per + j) * LANES : (g * per + j + 1) * LANES]
-                    for j in range(per)
-                ],
+                [query[here, (g * per + j) * LANES : (g * per + j + 1) * LANES] for j in range(per)],
                 axis=0,
             )
             for g in range(groups)
         ]
         acc[...] = jnp.zeros_like(acc)
-
-        @pl.loop(start_ref[blk] // step, (first_tok + rows + step - 1) // step)
+        kv_copy(blk).wait()
+
+        @pl.loop(first_of(ends, first_tok) // step, (first_tok + rows + step - 1) // step)
         def _(tile):
             base = tile * step
             there = pl.ds(pl.multiple_of(base, step), step)
@@ -380,15 +691,16 @@
             for g in range(groups):
                 cols = slice(g * LANES, (g + 1) * LANES)
                 value_cols = slice(kv_width + g * LANES, kv_width + (g + 1) * LANES)
-                scores = lax.dot_general(
-                    queries[g], kv_ref[there, cols], (((1,), (1,)), ((), ())),
-                    preferred_element_type=jnp.float32,
-                )
+                scores = dot_nt(queries[g], kv[there, cols])
                 probs = jnp.where(allowed, jnp.exp2(scores * factor), 0.0).astype(jnp.bfloat16)
                 values = jnp.concatenate(
-                    [kv_ref[there, value_cols], jnp.ones((step, LANES), jnp.bfloat16)], axis=1
+                    [kv[there, value_cols], jnp.ones((step, LANES), jnp.bfloat16)], axis=1
                 )
-                acc[g] += jnp.dot(probs, values, preferred_element_type=jnp.float32)
+                acc[g] += dot_nn(probs, values)
+
+        @pl.when(blk == 0)
+        def _():
+            early[1].wait()
 
         for g in range(groups):
             for j in range(per):
@@ -396,88 +708,130 @@
                 cols = slice((g * per + j) * LANES, (g * per + j + 1) * LANES)
                 inverse = 1.0 / part[:, LANES:]
                 out = part[:, :LANES] * inverse
-                att_ref[here, cols] = out
-                inv_ref[here, cols] = inverse
-                gated_ref[here, cols] = (out * jax.nn.sigmoid(gate_ref[here, cols])).astype(
-                    jnp.bfloat16
-                )
-
-
-def attention_forward(query_low, kv_all, starts, firsts, gate_pre):
+                att[here, cols] = out
+                inv[here, cols] = inverse
+                gated[here, cols] = (out * jax.nn.sigmoid(gate[here, cols])).astype(jnp.bfloat16)
+        start_all(out_copies(blk))
+
+    for blk in range(blocks):
+        for copy in out_copies(blk):
+            copy.wait()
+
+
+def attention_forward(doc_lengths, query_low, kv_all, gate_pre):
     rows, width = query_low.shape
-    groups = (kv_all.shape[1] // 2) // LANES
-    per = width // (kv_all.shape[1] // 2)
-    blocks = starts.shape[0]
-    vmem = pl.BlockSpec(memory_space=pltpu.VMEM)
+    kv_width = kv_all.shape[1] // 2
+    groups = kv_width // LANES
+    per = width // kv_width
+    blocks = lax.axis_size("head")
+    low, full = jnp.bfloat16, jnp.float32
+    shape, vm = jax.ShapeDtypeStruct, pltpu.VMEM
     return pl.pallas_call(
         attention_forward_kernel,
         out_shape=(
-            jax.ShapeDtypeStruct((rows, width), jnp.float32),
-            jax.ShapeDtypeStruct((rows, width), jnp.float32),
-            jax.ShapeDtypeStruct((rows, width), jnp.bfloat16),
+            shape((rows, width), full),
+            shape((rows, width), full),
+            shape((rows, width), low),
         ),
-        in_specs=[pl.BlockSpec(memory_space=pltpu.SMEM)] + [vmem] * 4,
-        out_specs=(vmem, vmem, vmem),
-        scratch_shapes=[pltpu.VMEM((groups, per * (rows // blocks), 2 * LANES), jnp.float32)],
+        in_specs=[pl.BlockSpec(memory_space=pltpu.SMEM)] + [ANY] * 3,
+        out_specs=(ANY, ANY, ANY),
+        scratch_shapes=[
+            vm((rows, width), low), vm(kv_all.shape, low), vm((rows, width), full),
+            vm((rows, width), full), vm((rows, width), full), vm((rows, width), low),
+            vm((groups, per * (rows // blocks), 2 * LANES), full),
+            DMA((blocks,)), DMA((2,)), DMA((3, blocks)),
+        ],
         compiler_params=pltpu.CompilerParams(vmem_limit_bytes=VMEM_LIMIT),
         cost_estimate=pl.CostEstimate(
             flops=4 * rows * width * 2048, bytes_accessed=12 << 20, transcendentals=0
         ),
         name="attention_forward",
-    )(starts, query_low, kv_all, firsts, gate_pre)
+    )(doc_lengths, query_low, kv_all, gate_pre)
 
 
 def attention_backward_kernel(
-    start_ref, query_ref, grad_ref, att_ref, inv_ref, kvs_ref, first_ref,
-    dq_ref, kv_ref, dk_acc, dv_acc, dqt, keyt,
+    doc_ref, query_any, att_any, inv_any, gate_any, kv_any, back_any, wo_any,
+    dq_any, parts_any, ggrad_any,
+    query, att, inv, gate, kv, back, wo, dq, parts, ggrad, dk_acc, dv_acc, dqt, keyt, dout,
+    in_sem, out_sem,
 ):
-    blocks = start_ref.shape[0]
-    kv_width = kvs_ref.shape[1] // 2
+    wide_count = lax.axis_size("wide")
+    wide_pos = lax.axis_index("wide")
+    kv_width = kv.shape[1] // 2
     groups = kv_width // LANES
-    per = query_ref.shape[1] // kv_width
-    rows = query_ref.shape[0] // blocks
-    wide_count = kvs_ref.shape[0] // query_ref.shape[0]
-    wide_pos = lax.axis_index("wide")
-    step = KEY_BLOCK
+    per = query.shape[1] // kv_width
+    blocks = out_sem.shape[1]
+    rows = query.shape[0] // blocks
+    step = min(BACKWARD_KEYS, rows * wide_count)
     scale = LANES ** (-0.5)
+    loads = [
+        pltpu.make_async_copy(src, dst, in_sem.at[i])
+        for i, (src, dst) in enumerate(
+            (
+                (back_any, back), (wo_any, wo), (gate_any, gate), (att_any, att),
+                (inv_any, inv), (query_any, query), (kv_any, kv),
+            )
+        )
+    ]
+    start_all(loads)
+    ends = doc_ends(doc_ref)
     dk_acc[...] = jnp.zeros_like(dk_acc)
     dv_acc[...] = jnp.zeros_like(dv_acc)
-
-    @pl.loop(0, kvs_ref.shape[0] // step)
+    for load in loads[:4]:
+        load.wait()
+
+    @pl.loop(0, blocks)
+    def _(blk):
+        here = pl.ds(pl.multiple_of(blk * rows, rows), rows)
+        gated_grad = dot_nt(back[here, :], wo[...])
+        sig = jax.nn.sigmoid(gate[here, :])
+        grad = gated_grad * sig
+        dout[here, :] = grad
+        ggrad[here, :] = (grad * att[here, :] * (1.0 - sig)).astype(jnp.bfloat16)
+
+    for load in loads[4:]:
+        load.wait()
+
+    @pl.loop(0, kv.shape[0] // step)
     def _(tile):
         there = pl.ds(pl.multiple_of(tile * step, step), step)
         for g in range(groups):
             cols = slice(g * LANES, (g + 1) * LANES)
-            keyt[cols, there] = jnp.transpose(kvs_ref[there, cols])
+            keyt[cols, there] = jnp.transpose(kv[there, cols])
+
+    def out_copies(blk):
+        here = pl.ds(pl.multiple_of(blk * rows, rows), rows)
+        return [
+            pltpu.make_async_copy(dq.at[here], dq_any.at[here], out_sem.at[0, blk]),
+            pltpu.make_async_copy(parts.at[:, here], parts_any.at[:, here], out_sem.at[1, blk]),
+            pltpu.make_async_copy(ggrad.at[here], ggrad_any.at[here], out_sem.at[2, blk]),
+        ]
 
     @pl.loop(0, blocks)
-    def _(blk):
+    def _(turn_of):
+        blk = blocks - 1 - turn_of
         here = pl.ds(pl.multiple_of(blk * rows, rows), rows)
         first_tok = (blk * wide_count + wide_pos) * rows
         key_row = lax.broadcasted_iota(jnp.int32, (step, rows), 0)
-        query_lane = lax.broadcasted_iota(jnp.int32, (step, rows), 1) + first_tok
-        upper = key_row - query_lane
-        lower = key_row - jnp.transpose(
-            jnp.broadcast_to(first_ref[here, :], (rows, LANES))
-        )[0:1, :]
+        tokens = lax.broadcasted_iota(jnp.int32, (1, rows), 1) + first_tok
+        upper = key_row - tokens
+        lower = key_row - first_of(ends, tokens)
         queries, grads, deltas = [], [], []
         for g in range(groups):
             qs, gs, ds = [], [], []
             for j in range(per):
                 cols = slice((g * per + j) * LANES, (g * per + j + 1) * LANES)
-                grad = grad_ref[here, cols].astype(jnp.float32)
-                inverse = inv_ref[here, cols]
-                both = grad * inverse
-                delta = jnp.sum(both * att_ref[here, cols], axis=1, keepdims=True)
+                both = dout[here, cols] * inv[here, cols]
+                delta = jnp.sum(both * att[here, cols], axis=1, keepdims=True)
                 ds.append(jnp.transpose(jnp.broadcast_to(delta, (rows, LANES)))[0:1, :])
-                qs.append(query_ref[here, cols])
+                qs.append(query[here, cols])
                 gs.append(both.astype(jnp.bfloat16))
             queries.append(jnp.concatenate(qs, axis=0))
             grads.append(jnp.concatenate(gs, axis=0))
             deltas.append(jnp.concatenate(ds, axis=1))
         dqt[...] = jnp.zeros_like(dqt)
 
-        @pl.loop(start_ref[blk] // step, (first_tok + rows + step - 1) // step)
+        @pl.loop(first_of(ends, first_tok) // step, (first_tok + rows + step - 1) // step)
         def _(tile):
             base = tile * step
             there = pl.ds(pl.multiple_of(base, step), step)
@@ -486,110 +840,123 @@
             for g in range(groups):
                 cols = slice(g * LANES, (g + 1) * LANES)
                 value_cols = slice(kv_width + g * LANES, kv_width + (g + 1) * LANES)
-                scores = lax.dot_general(
-                    kvs_ref[there, cols], queries[g], (((1,), (1,)), ((), ())),
-                    preferred_element_type=jnp.float32,
-                )
+                scores = dot_nt(kv[there, cols], queries[g])
                 probs = jnp.where(allowed, jnp.exp2(scores * (scale * LOG2E)), 0.0)
-                dprobs = lax.dot_general(
-                    kvs_ref[there, value_cols], grads[g], (((1,), (1,)), ((), ())),
-                    preferred_element_type=jnp.float32,
-                )
-                dscores = (probs * (dprobs - deltas[g]) * scale).astype(jnp.bfloat16)
-                dv_acc[there, cols] += jnp.dot(
-                    probs.astype(jnp.bfloat16), grads[g], preferred_element_type=jnp.float32
-                )
-                dk_acc[there, cols] += jnp.dot(
-                    dscores, queries[g], preferred_element_type=jnp.float32
-                )
-                dqt[g] += jnp.dot(
-                    keyt[cols, there], dscores, preferred_element_type=jnp.float32
-                )
+                dprobs = dot_nt(kv[there, value_cols], grads[g])
+                dscores = (probs * (dprobs - deltas[g])).astype(jnp.bfloat16)
+                dv_acc[there, cols] += dot_nn(probs.astype(jnp.bfloat16), grads[g])
+                dk_acc[there, cols] += dot_nn(dscores, queries[g])
+                dqt[g] += dot_nn(keyt[cols, there], dscores)
 
         for g in range(groups):
             for j in range(per):
                 cols = slice((g * per + j) * LANES, (g * per + j + 1) * LANES)
-                dq_ref[here, cols] = jnp.transpose(dqt[g, :, j * rows : (j + 1) * rows])
-
-    width = dk_acc.shape[1]
-
-    @pl.loop(0, wide_count)
-    def _(target):
-        for blk in range(blocks):
+                dq[here, cols] = jnp.transpose(dqt[g, :, j * rows : (j + 1) * rows]) * scale
+
+        @pl.loop(0, wide_count)
+        def _(target):
             source = pl.ds(pl.multiple_of((blk * wide_count + target) * rows, rows), rows)
-            there = pl.ds(pl.multiple_of((target * blocks + blk) * rows, rows), rows)
-            kv_ref[there, :width] = dk_acc[source, :].astype(jnp.bfloat16)
-            kv_ref[there, width:] = dv_acc[source, :].astype(jnp.bfloat16)
+            parts[target, here, :kv_width] = (dk_acc[source, :] * scale).astype(jnp.bfloat16)
+            parts[target, here, kv_width:] = dv_acc[source, :].astype(jnp.bfloat16)
+
+        start_all(out_copies(blk))
+
+    for blk in range(blocks):
+        for copy in out_copies(blk):
+            copy.wait()
 
 
 def attention_backward(
-    query_low, grad_low, attended, inverse, kv_all, starts, firsts
+    doc_lengths, query_low, attended, inverse, gate_pre, kv_all, back_rows, out_w
 ):
     rows, width = query_low.shape
     keys, kv_width = kv_all.shape[0], kv_all.shape[1] // 2
     groups = kv_width // LANES
     per = width // kv_width
-    blocks = starts.shape[0]
-    vmem = pl.BlockSpec(memory_space=pltpu.VMEM)
+    blocks, wide_count = lax.axis_size("head"), lax.axis_size("wide")
+    low, full = jnp.bfloat16, jnp.float32
+    shape, vm = jax.ShapeDtypeStruct, pltpu.VMEM
     return pl.pallas_call(
         attention_backward_kernel,
         out_shape=(
-            jax.ShapeDtypeStruct((rows, width), jnp.float32),
-            jax.ShapeDtypeStruct((keys, 2 * kv_width), jnp.bfloat16),
+            shape((rows, width), full),
+            shape((wide_count, rows, 2 * kv_width), low),
+            shape((rows, width), low),
         ),
-        in_specs=[pl.BlockSpec(memory_space=pltpu.SMEM)] + [vmem] * 6,
-        out_specs=(vmem, vmem),
+        in_specs=[pl.BlockSpec(memory_space=pltpu.SMEM)] + [ANY] * 7,
+        out_specs=(ANY, ANY, ANY),
         scratch_shapes=[
-            pltpu.VMEM((keys, kv_width), jnp.float32),
-            pltpu.VMEM((keys, kv_width), jnp.float32),
-            pltpu.VMEM((groups, LANES, per * (rows // blocks)), jnp.float32),
-            pltpu.VMEM((kv_width, keys), jnp.bfloat16),
+            vm((rows, width), low), vm((rows, width), full), vm((rows, width), full),
+            vm((rows, width), full), vm(kv_all.shape, low), vm(back_rows.shape, low),
+            vm(out_w.shape, low), vm((rows, width), full),
+            vm((wide_count, rows, 2 * kv_width), low), vm((rows, width), low),
+            vm((keys, kv_width), full), vm((keys, kv_width), full),
+            vm((groups, LANES, per * (rows // blocks)), full), vm((kv_width, keys), low),
+            vm((rows, width), full),
+            DMA((7,)), DMA((3, blocks)),
         ],
         compiler_params=pltpu.CompilerParams(vmem_limit_bytes=VMEM_LIMIT),
         cost_estimate=pl.CostEstimate(
             flops=10 * rows * width * 2048, bytes_accessed=20 << 20, transcendentals=0
         ),
         name="attention_backward",
-    )(starts, query_low, grad_low, attended, inverse, kv_all, firsts)
+    )(
+        doc_lengths, query_low, attended, inverse, gate_pre, kv_all, back_rows, out_w
+    )
 
 
 def ffn_kernel(
-    gated_ref, x_ref, cot_ref, gain_ref, wo_any, wg_any, wu_any, wd_any,
-    out_any, mgrad_ref, gain_out, back_any, down_ref, fgate_any, fup_any,
-    wo, wg, wu, wd, cots, rows, hidden_grad, hid, gg, ug, terms_own, passed, into,
+    gated_ref, gain_ref, x_any, cot_any, left_any, wo_any, wg_any, wu_any, wd_any,
+    out_any, mgrad_ref, gain_out, back_any, down_any, fgate_any, fup_any, owg_any,
+    wo, wg, wu, wd, cots, rows, hid, gg, ug, terms_own, outs_own, passed, into,
     passed2, into2, dterms, dinto, stage, hterms, hinto, middle, back, local_sem,
     ds, dr, hs, hr, cs, cr, cps, cpr, fs, fr, fps, fpr, s1, r1, ps1, pr1, s2, r2, ps2, pr2, bs, br,
 ):
-    tok, width = x_ref.shape
+    tok, width = x_any.shape
     hidden_width = wg_any.shape[1]
     head, wide = head_ring(), wide_ring()
     pair = 2 * tok
     separate = terms_own.shape[0] > 16
     terms = terms_own if separate else cots
+    outs = outs_own if separate else rows
     part = wo_any.shape[1] // lax.axis_size("head")
     loads = [
         pltpu.make_async_copy(src, dst, local_sem.at[i])
         for i, (src, dst) in enumerate(((wo_any, wo), (wd_any, wd), (wg_any, wg), (wu_any, wu)))
     ]
+    split = left_any.shape[1]
+    loads.append(pltpu.make_async_copy(left_any, cots.at[:, pl.ds(0, split)], local_sem.at[10]))
     for load in loads:
         load.start()
     own_wide = pl.multiple_of(lax.axis_index("wide") * tok, tok)
     own_head = pl.multiple_of(lax.axis_index("head") * tok, tok)
-    cots[pl.ds(own_wide, tok), :] = cot_ref[...]
+    own_loads = [
+        pltpu.make_async_copy(
+            cot_any.at[:, pl.ds(split, width - split)],
+            cots.at[pl.ds(own_wide, tok), pl.ds(split, width - split)],
+            local_sem.at[12],
+        ),
+        pltpu.make_async_copy(x_any, back.at[pl.ds(own_head, tok)], local_sem.at[13]),
+    ]
+    start_all(own_loads)
+    own_loads[0].wait()
     meet(neighbours(head, wide))
 
     def slot_of(ref):
         return lambda index, start, size: ref.at[pl.ds(index * tok + start, size)]
 
-    cot_gather = PairGather(wide, slot_of(cots), tok, cs, cr, cps, cpr)
-    row_gather = PairGather(wide, slot_of(rows), tok, fs, fr, fps, fpr)
+    def cot_slot(index, start, size):
+        return cots.at[pl.ds(index * tok + start, size), pl.ds(split, width - split)]
+
+    cot_gather = PairGather(wide, cot_slot, tok, cs, cr, cps, cpr)
+    row_gather = row_gather_of(wide)(wide, slot_of(rows), tok, fs, fr, fps, fpr)
     back_gather = Gather(head, slot_of(back), tok, bs, br)
     head_scatter = Scatter(head, lambda index: (hterms, index * tok), tok, hinto, hs, hr)
-    grad_scatter = PairScatter(wide, terms, tok, passed, into, s1, r1, ps1, pr1)
+    grad_scatter = scatter_of(wide)(wide, terms, tok, passed, into, s1, r1, ps1, pr1)
     down_scatter = Scatter(
         head, lambda index: (dterms, index * hidden_width), hidden_width, dinto, ds, dr
     )
-    out_scatter = PairScatter(wide, rows, tok, passed2, into2, s2, r2, ps2, pr2)
+    out_scatter = scatter_of(wide)(wide, outs, tok, passed2, into2, s2, r2, ps2, pr2)
 
     def group_of(offset):
         return pl.ds(pl.multiple_of(wide.index(offset) * pair, pair), pair)
@@ -600,6 +967,7 @@
             body(pl.ds(pl.multiple_of(i * step, step), step))
 
     tile = 256
+    line = wide.size == 4
     cot_gather.begin()
 
     def out_part(offset, own):
@@ -609,7 +977,7 @@
         def body(cols):
             value = dot_nn(gated_ref[here, :], wo[:, cols])
             if own:
-                middle[:, cols] = x_ref[:, cols].astype(jnp.float32) + value
+                middle[:, cols] = back[pl.ds(own_head, tok), cols].astype(jnp.float32) + value
             else:
                 hterms[here, cols] = value.astype(jnp.bfloat16)
 
@@ -619,13 +987,12 @@
         here = group_of(offset)
 
         def body(cols):
-            hidden_grad[here, cols] = dot_nt(cots[here, :], wd[cols, :]).astype(
-                hidden_grad.dtype
-            )
-
-        col_loop(hidden_width, tile if hidden_width % tile == 0 else LANES, body)
+            hid[here, cols] = dot_nt(cots[here, :], wd[cols, :]).astype(jnp.bfloat16)
+
+        col_loop(hidden_width, hidden_width, body)
 
     loads[0].wait()
+    own_loads[1].wait()
     out_part(head.half, False)
     head_scatter.start(head.half)
     for hop in range(head.half - 1, 0, -1):
@@ -633,6 +1000,8 @@
         out_part(-hop, False)
     out_part(0, True)
     loads[1].wait()
+    loads[4].wait()
+    mgrad_ref[...] = cots[pl.ds(own_wide, tok), :].astype(jnp.float32)
     cot_gather.take(0)
     hidden_part(0)
     for hop in range(head.half - 1, 0, -1):
@@ -677,7 +1046,7 @@
         def body(cols):
             gate = dot_nn(rows[here, :], wg[:, cols])
             up = dot_nn(rows[here, :], wu[:, cols])
-            grad = hidden_grad[here, cols].astype(jnp.float32)
+            grad = hid[here, cols].astype(jnp.float32)
             sig = jax.nn.sigmoid(gate)
             act = gate * sig
             hid[here, cols] = (act * up).astype(jnp.bfloat16)
@@ -686,19 +1055,27 @@
 
         col_loop(hidden_width, tile if hidden_width % tile == 0 else LANES, body)
 
-    row_gather.take(0)
-    unit(0)
-    for hop in range(1, wide.half):
-        row_gather.arrive(hop)
-        row_gather.start(hop + 1)
-        row_gather.hand(hop)
-        row_gather.take(hop)
-        unit(hop)
-        unit(-hop)
-    row_gather.arrive(wide.half)
-    row_gather.hand(wide.half)
-    row_gather.take(wide.half)
-    unit(wide.half)
+    def down_terms(offset):
+        here = group_of(offset)
+
+        def body(cols):
+            outs[here, cols] = dot_nn(hid[here, :], wd[:, cols]).astype(jnp.bfloat16)
+
+        col_loop(width, width, body)
+        if not line:
+            out_scatter.hand(offset)
+
+    def down_grads(group, add):
+        @pl.loop(0, lax.axis_size("head"))
+        def _(index):
+            cols = pl.ds(pl.multiple_of(index * part, part), part)
+            there = pl.ds(pl.multiple_of(index * hidden_width, LANES), hidden_width)
+            value = sum(
+                dot_tn(hid[group_of(offset), :], cots[group_of(offset), cols]) for offset in group
+            )
+            if add:
+                value += dterms[there, :].astype(jnp.float32)
+            dterms[there, :] = value.astype(jnp.bfloat16)
 
     def grad_terms(offset):
         here = group_of(offset)
@@ -707,32 +1084,7 @@
             value = dot_nt(gg[here, :], wg[cols, :]) + dot_nt(ug[here, :], wu[cols, :])
             terms[here, cols] = value.astype(jnp.bfloat16)
 
-        col_loop(width, tile, body)
-        grad_scatter.hand(offset)
-
-    def down_terms(offset):
-        here = group_of(offset)
-
-        def body(cols):
-            rows[here, cols] = dot_nn(hid[here, :], wd[:, cols]).astype(jnp.bfloat16)
-
-        col_loop(width, tile, body)
-        out_scatter.hand(offset)
-
-    def down_grads():
-        @pl.loop(0, lax.axis_size("head"))
-        def _(index):
-            cols = pl.ds(pl.multiple_of(index * part, part), part)
-
-            @pl.loop(0, hidden_width // LANES)
-            def _(i):
-                lanes = pl.ds(pl.multiple_of(i * LANES, LANES), LANES)
-                there = pl.ds(
-                    pl.multiple_of(index * hidden_width + i * LANES, LANES), LANES
-                )
-                dterms[there, :] = dot_tn(hid[:, lanes], cots[:, cols]).astype(jnp.bfloat16)
-
-        down_scatter.start(head.half)
+        col_loop(width, 1024, body)
 
     emit = stage.shape[2]
 
@@ -761,26 +1113,105 @@
                     stage_copy(step, out, any_ref, slot).start()
 
     order = offsets(wide)
-    if not separate:
-        down_grads()
-    grad_terms(order[0])
-    grad_terms(order[1])
-    grad_scatter.merge(order[0])
-    grad_scatter.start(wide.half)
-    for offset in order[2:]:
-        grad_terms(offset)
-    if separate:
-        down_grads()
-    for hop in range(wide.half - 1, 0, -1):
-        grad_scatter.merge(hop)
-        grad_scatter.merge(-hop)
-        grad_scatter.advance(hop)
-    grad_scatter.merge(0)
-    input_grads()
+
+    def near_part(offset):
+        unit(offset)
+        if separate:
+            down_terms(offset)
+
+    def down_pass(kind):
+        offset = out_scatter.offset(kind)
+        down_terms(offset)
+        out_scatter.hand_kind(kind)
+
+    if line:
+
+        def arrived(kind):
+            row_gather.arrive(kind)
+            row_gather.take(kind)
+            unit(row_gather.offset(kind))
+            grad_terms(grad_scatter.offset(kind))
+            grad_scatter.hand_kind(kind)
+
+        row_gather.take(None)
+        unit(0)
+        down_pass(None)
+        down_grads([0], False)
+        arrived(NEAR)
+        down_pass(NEAR)
+        grad_scatter.merge_kind(NEAR)
+        grad_scatter.launch(NEAR)
+
+        @pl.when(row_gather.middle)
+        def _():
+            arrived(OTHER)
+            down_pass(OTHER)
+            grad_scatter.merge_kind(OTHER)
+
+        arrived(FAR)
+        grad_scatter.merge_kind(FAR)
+        grad_scatter.launch(FAR)
+
+        @pl.when(~row_gather.middle)
+        def _():
+            arrived(OTHER)
+            grad_scatter.merge_kind(OTHER)
+
+        grad_scatter.launch(OTHER)
+        pl.when(~row_gather.middle)(functools.partial(down_pass, OTHER))
+        down_pass(FAR)
+        grad_terms(0)
+        grad_scatter.hand_kind(None)
+        down_grads([1, 2, 3], True)
+        down_scatter.start(head.half)
+        grad_scatter.relay(OTHER)
+        for kind in (OTHER, FAR, NEAR, None):
+            out_scatter.merge_kind(kind)
+        input_grads()
+        out_scatter.launch(OTHER, FAR, NEAR)
+        grad_scatter.merge_kind(None)
+        grad_scatter.relay(FAR)
+        grad_scatter.relay(NEAR)
+    else:
+        row_gather.take(0)
+        near_part(0)
+        if separate:
+            down_grads([0], False)
+        for hop in range(1, wide.half):
+            row_gather.arrive(hop)
+            row_gather.start(hop + 1)
+            row_gather.hand(hop)
+            row_gather.take(hop)
+            near_part(hop)
+            near_part(-hop)
+        row_gather.arrive(wide.half)
+        row_gather.hand(wide.half)
+        row_gather.take(wide.half)
+        unit(wide.half)
+        if not separate:
+            down_grads(order, False)
+            down_scatter.start(head.half)
+        for offset in order:
+            grad_terms(offset)
+            grad_scatter.hand(offset)
+        grad_scatter.merge(order[0])
+        grad_scatter.start(wide.half)
+        if separate:
+            down_grads(order[:-1], True)
+            down_scatter.start(head.half)
+            down_terms(order[0])
+        for hop in range(wide.half - 1, 0, -1):
+            grad_scatter.merge(hop)
+            grad_scatter.merge(-hop)
+            grad_scatter.advance(hop)
+        grad_scatter.merge(0)
+        input_grads()
     row_gather.finish()
-    for offset in order:
-        down_terms(offset)
-    out_scatter.merge(order[0])
+    if not line:
+        if not separate:
+            for offset in order:
+                down_terms(offset)
+        out_scatter.merge(order[0])
     for hop in range(head.half - 1, 0, -1):
         down_scatter.advance(hop)
     grad_scatter.arrive()
@@ -793,7 +1224,7 @@
         scaled = value * scale
         weighted = grad * gain
         mean = jnp.mean(scaled * weighted, axis=-1, keepdims=True)
-        total = cot_ref[here, :].astype(jnp.float32) + scale * (weighted - scaled * mean)
+        total = mgrad_ref[here, :] + scale * (weighted - scaled * mean)
         mgrad_ref[here, :] = total
         back[pl.ds(pl.multiple_of(own_head + row, 32), 32), :] = total.astype(jnp.bfloat16)
         return gain_sum + jnp.sum(grad * scaled, axis=0, keepdims=True)
@@ -804,11 +1235,15 @@
         jnp.zeros((1, width), jnp.float32),
     )
     back_gather.start(1)
-    out_scatter.start(wide.half)
-    for offset in order[1:]:
-        out_scatter.merge(offset)
-    for hop in range(wide.half - 1, 0, -1):
-        out_scatter.advance(hop)
+    if line:
+        for kind in (FAR, OTHER, NEAR):
+            out_scatter.relay(kind)
+    else:
+        out_scatter.start(wide.half)
+        for offset in order[1:]:
+            out_scatter.merge(offset)
+        for hop in range(wide.half - 1, 0, -1):
+            out_scatter.advance(hop)
     for hop in range(1, head.half):
         back_gather.arrive(hop)
         back_gather.start(hop + 1)
@@ -816,6 +1251,15 @@
     back_gather.finish()
     keep = pltpu.make_async_copy(back, back_any, local_sem.at[4])
     keep.start()
+    head_scatter.finish()
+    owners = gated_ref.shape[1]
+
+    def out_grads(cols):
+        hterms[pl.ds(0, owners), cols] = dot_tn(gated_ref[...], back[:, cols]).astype(jnp.bfloat16)
+
+    col_loop(width, 512, out_grads)
+    share = pltpu.make_async_copy(hterms.at[pl.ds(0, owners)], owg_any, local_sem.at[11])
+    share.start()
     out_scatter.arrive()
 
     def finish_out(row):
@@ -828,20 +1272,31 @@
     result.start()
     down_scatter.arrive()
 
-    def finish_down(row):
-        down_ref[pl.ds(row, 32), :] = down_scatter.total(row, 32)
-
-    row_loop(hidden_width, 32, finish_down)
-    for scatter in (head_scatter, grad_scatter, out_scatter, down_scatter):
+    pending = {}
+    places = width // part
+    for step in range(hidden_width // LANES):
+        place = step % places
+        if place in pending:
+            pending[place].wait()
+        spot = middle.at[:, place * part : (place + 1) * part]
+        middle[:, place * part : (place + 1) * part] = down_scatter.total(step * LANES, LANES)
+        pending[place] = pltpu.make_async_copy(
+            spot, down_any.at[pl.ds(step * LANES, LANES)], local_sem.at[14 + place % 4]
+        )
+        pending[place].start()
+    for scatter in (grad_scatter, out_scatter, down_scatter):
         scatter.finish()
     last = width // emit
     for slot in SIDES:
         for out, any_ref in enumerate((fgate_any, fup_any)):
             stage_copy(last - 2 + slot, out, any_ref, slot).wait()
     result.wait()
-
-
-def ffn_block(gated_low, inputs, cotangent, ffn_gain, out_w, gate_w, up_w, down_w):
+    share.wait()
+    for copy in pending.values():
+        copy.wait()
+
+
+def ffn_block(gated_low, inputs, cotangent, cot_left, ffn_gain, out_w, gate_w, up_w, down_w):
     tok, width = inputs.shape
     head_count, wide_count = lax.axis_size("head"), lax.axis_size("wide")
     chips = wide_count // 2
@@ -862,33 +1317,34 @@
             shape((hidden_width, width // head_count), full),
             shape((width, hidden_width), low),
             shape((width, hidden_width), low),
+            shape((gated_low.shape[1], width), low),
         ),
-        in_specs=[VMEM] * 4 + [ANY] * 4,
-        out_specs=(ANY, VMEM, VMEM, ANY, VMEM, ANY, ANY),
+        in_specs=[VMEM] * 2 + [ANY] * 7,
+        out_specs=(ANY, VMEM, VMEM, ANY, ANY, ANY, ANY, ANY),
         scratch_shapes=[
             vm(out_w.shape, low), vm(gate_w.shape, low), vm(up_w.shape, low),
             vm(down_w.shape, low),
             vm((all_rows, width), low), vm((all_rows, width), low),
-            vm((all_rows, hidden_width), full if roomy else low),
             vm((all_rows, hidden_width), low), vm((all_rows, hidden_width), low),
             vm((all_rows, hidden_width), low),
             vm((all_rows if roomy else 16, width), low),
+            vm((all_rows if roomy else 16, width), low),
             vm((chips, tok, width), low),
-            into_shape(chips, tok, width),
+            scatter_into(chips, tok, width),
             vm((chips, tok, width), low),
-            into_shape(chips, tok, width),
+            scatter_into(chips, tok, width),
             vm((head_count * hidden_width, width // head_count), low),
             into_shape(head_count, hidden_width, width // head_count),
-            vm((2, 2, 256 if roomy else 128, hidden_width), low),
+            vm((2, 2, 128, hidden_width), low),
             vm((back_rows, width), low), into_shape(head_count, tok, width),
             vm((tok, width), full), vm((back_rows, width), low),
-            DMA((10,)),
+            DMA((18,)),
             *ring_sems(head_count),
             *ring_sems(head_count),
             *ring_sems(chips), *pass_sems(chips),
-            *ring_sems(chips), *pass_sems(chips),
-            *ring_sems(chips), DMA((chips,)), DMA((chips,)),
-            *ring_sems(chips), DMA((chips,)), DMA((chips,)),
+            *gather_sems(chips),
+            *scatter_sems(chips),
+            *scatter_sems(chips),
             *ring_sems(head_count),
         ],
         compiler_params=pltpu.CompilerParams(
@@ -898,7 +1354,9 @@
             flops=10 * all_rows * width * hidden_width, bytes_accessed=200 << 20, transcendentals=0
         ),
         name="ffn_block",
-    )(gated_low, inputs, cotangent, ffn_gain[None], out_w, gate_w, up_w, down_w)
+    )(
+        gated_low, ffn_gain[None], inputs, cotangent, cot_left, out_w, gate_w, up_w, down_w
+    )
 
 
 def turn(values, cosine, sine_tab):
@@ -954,7 +1412,7 @@
         def place(index, start, size):
             return kv.at[pl.ds((block * wide_count + index) * tok + start, size)]
 
-        return PairGather(
+        return row_gather_of(wide)(
             wide, place, tok, ks.at[slot], kr.at[slot], kps.at[slot], kpr.at[slot]
         )
 
@@ -990,11 +1448,29 @@
         gathers[offset] = kv_gather(offset)
         gathers[offset].begin()
 
+    line = wide.size == 4
+
     def step(offset, hop):
-        gathers[offset].arrive(hop)
-        if hop < wide.half:
-            gathers[offset].start(hop + 1)
-        gathers[offset].hand(hop)
+        each = gathers[offset]
+        if line and hop == 1:
+            each.arrive(NEAR)
+
+            @pl.when(each.middle)
+            def _():
+                each.arrive(OTHER)
+
+        elif line:
+            each.arrive(FAR)
+
+            @pl.when(~each.middle)
+            def _():
+                each.arrive(OTHER)
+
+        else:
+            each.arrive(hop)
+            if hop < wide.half:
+                each.start(hop + 1)
+            each.hand(hop)
 
     loads[0].wait()
     loads[1].wait()
@@ -1029,7 +1505,7 @@
         for offset in gathers:
             step(offset, hop)
     for each in gathers.values():
-        for hop in range(wide.half + 1):
+        for hop in (None, NEAR, OTHER, FAR) if line else range(wide.half + 1):
             each.take(hop)
     store = pltpu.make_async_copy(kv, kv_any, local_sem.at[5])
     store.start()
@@ -1047,7 +1523,6 @@
     rows = head_count * tok
     low, full = jnp.bfloat16, jnp.float32
     shape, vm = jax.ShapeDtypeStruct, pltpu.VMEM
-    half = chips // 2
     return pl.pallas_call(
         front_kernel,
         out_shape=(
@@ -1066,8 +1541,7 @@
             vm((rows * wide_count, 2 * kv_width), low),
             DMA((6,)),
             *ring_sems(head_count),
-            DMA((head_count, 2, half)), DMA((head_count, 2, half)),
-            DMA((head_count, 2, half + 1)), DMA((head_count, 2, half + 1)),
+            *[DMA((head_count, *sem.shape)) for sem in gather_sems(chips)],
         ],
         compiler_params=pltpu.CompilerParams(
             collective_id=3, has_side_effects=True, vmem_limit_bytes=VMEM_LIMIT
@@ -1099,11 +1573,11 @@
 
 
 def tail_kernel(
-    dq_ref, qpre_ref, kpre_ref, ggrad_ref, cos_ref, sin_ref, qgain_ref, kgain_ref, x_ref,
-    mgrad_ref, gain_ref, ffn_gain_ref, gated_ref,
-    kvp_any, normed_any, back_any, wq_any, wk_any, wv_any, wg_any, fgate_any, fup_any,
-    igrad_ref, gains_ref, query_out, key_out, value_out, gate_out, output_out, fgate_out, fup_out,
-    kvp, normed, back, wq, wk, wv, wg, fgate, fup, qlow, klow, vlow, early, late, hterms,
+    cos_ref, sin_ref, qgain_ref, kgain_ref, gain_ref, ffn_gain_ref,
+    dq_any, qpre_any, kpre_any, ggrad_any, x_any, mgrad_any,
+    kvp_any, normed_any, wq_any, wk_any, wv_any, wg_any, fgate_any, fup_any,
+    igrad_ref, gains_ref, query_out, key_out, value_out, gate_out, fgate_out, fup_out,
+    dq_ref, qpre_ref, kpre_ref, ggrad_ref, x_ref, mgrad_ref, kvp, normed, wq, wk, wv, wg, fgate, fup, qlow, klow, vlow, early, late, hterms,
     kv_passed, kv_into, early_passed, early_into, late_passed, late_into, hinto, fgate_into,
     fup_into, gain_slots, stage, local_sem,
     kvs, kvr, kvps, kvpr, es, er, eps, epr, ls, lr, lps, lpr, hs, hr, gs, gr, us, ur, gain_send,
@@ -1119,12 +1593,20 @@
         for i, (src, dst) in enumerate(
             (
                 (kvp_any, kvp), (fgate_any, fgate), (fup_any, fup), (normed_any, normed),
-                (back_any, back), (wq_any, wq), (wk_any, wk), (wv_any, wv), (wg_any, wg),
+                (wq_any, wq), (wk_any, wk), (wv_any, wv), (wg_any, wg),
             )
         )
     ]
-    for load in loads:
-        load.start()
+    more = [
+        pltpu.make_async_copy(src, dst, local_sem.at[11 + i])
+        for i, (src, dst) in enumerate(
+            (
+                (dq_any, dq_ref), (qpre_any, qpre_ref), (ggrad_any, ggrad_ref),
+                (kpre_any, kpre_ref), (x_any, x_ref), (mgrad_any, mgrad_ref),
+            )
+        )
+    ]
+    start_all(loads[:1] + more[:3] + loads[1:] + more[3:])
     meet(everyone(head, wide))
     kv_width = wk.shape[1]
     q_width = wq.shape[1]
@@ -1148,6 +1630,8 @@
     loads[2].wait()
     up_scatter.start(head.half)
 
+    for load in more[:3]:
+        load.wait()
     chunk = 128
 
     def query_back(row, total):
@@ -1173,7 +1657,6 @@
     kv_scatter.merge(order[0])
     kv_scatter.start(wide.half)
     loads[3].wait()
-    loads[4].wait()
 
     def early_part(offset):
         index = wide.index(offset)
@@ -1185,29 +1668,23 @@
             there = pl.ds(pl.multiple_of(target * block, block), block)
             left = normed[:, cols]
             early[there, :q_width] = dot_tn(left, qlow[...]).astype(jnp.bfloat16)
-            early[there, q_width : 2 * q_width] = dot_tn(left, ggrad_ref[...]).astype(jnp.bfloat16)
-            out = dot_tn(gated_ref[...], back[:, cols]).astype(jnp.bfloat16)
-            for piece in range(q_width // block):
-                early[there, 2 * q_width + piece * block : 2 * q_width + (piece + 1) * block] = out[
-                    piece * block : (piece + 1) * block, :
-                ]
-
-        early_scatter.hand(offset)
+            early[there, q_width:] = dot_tn(left, ggrad_ref[...]).astype(jnp.bfloat16)
 
     for offset in order:
         early_part(offset)
+        early_scatter.hand(offset)
     for offset in order[1:]:
         kv_scatter.merge(offset)
     early_scatter.merge(order[0])
     for hop in range(wide.half - 1, 0, -1):
         kv_scatter.advance(hop)
     early_scatter.start(wide.half)
+    for offset in order[1:]:
+        early_scatter.merge(offset)
     for hop in range(head.half - 1, 0, -1):
         gate_scatter.advance(hop)
         up_scatter.advance(hop)
-    for offset in order[1:]:
-        early_scatter.merge(offset)
-    for load in loads[5:]:
+    for load in loads[4:] + more[3:]:
         load.wait()
     kv_scatter.arrive()
 
@@ -1251,13 +1728,11 @@
             late[cols, :kv_width] = dot_tn(left, klow[...]).astype(jnp.bfloat16)
             late[cols, kv_width:] = dot_tn(left, vlow[...]).astype(jnp.bfloat16)
 
+    for offset in order:
+        late_part(offset)
         late_scatter.hand(offset)
-
-    late_part(order[0])
     for hop in range(wide.half - 1, 0, -1):
         early_scatter.advance(hop)
-    for offset in order[1:]:
-        late_part(offset)
     late_scatter.merge(order[0])
     late_scatter.start(wide.half)
     for hop in range(head.half - 1, 0, -1):
@@ -1349,11 +1824,7 @@
         here = pl.ds(row, 32)
         both = early_scatter.total(row, 32)
         query_out[here, :] = both[:, :q_width]
-        gate_out[here, :] = both[:, q_width : 2 * q_width]
-        for piece in range(q_width // block):
-            output_out[pl.ds(pl.multiple_of(piece * block + row, 32), 32), :] = both[
-                :, 2 * q_width + piece * block : 2 * q_width + (piece + 1) * block
-            ]
+        gate_out[here, :] = both[:, q_width:]
 
     row_loop(block, 32, early_out)
     late_scatter.arrive()
@@ -1377,7 +1848,7 @@
 
 def tail_block(
     dq, kv_parts, query_pre, key_pre, gate_grad, cosine, sine_tab, query_gain, key_gain, inputs,
-    middle_grad, attn_gain, ffn_gain_part, gated_low, normed, back_rows, weights, fgate, fup,
+    middle_grad, attn_gain, ffn_gain_part, normed, weights, fgate, fup,
 ):
     tok, width = inputs.shape
     head_count, wide_count = lax.axis_size("head"), lax.axis_size("wide")
@@ -1389,7 +1860,7 @@
     ffn_rows = width // head_count
     low, full = jnp.bfloat16, jnp.float32
     shape, vm = jax.ShapeDtypeStruct, pltpu.VMEM
-    early_width = 3 * q_width
+    early_width = 2 * q_width
     pair = [*ring_sems(chips), DMA((chips,)), DMA((chips,))]
     peers = chips + head_count
     return pl.pallas_call(
@@ -1401,14 +1872,15 @@
             shape((block, kv_width), full),
             shape((block, kv_width), full),
             shape((block, q_width), full),
-            shape((q_width, block), full),
             shape((ffn_rows, hidden_width), full),
             shape((ffn_rows, hidden_width), full),
         ),
-        in_specs=[VMEM] * 13 + [ANY] * 9,
-        out_specs=tuple([VMEM] * 7 + [ANY] * 2),
+        in_specs=[VMEM] * 6 + [ANY] * 14,
+        out_specs=tuple([VMEM] * 6 + [ANY] * 2),
         scratch_shapes=[
-            vm(kv_parts.shape, low), vm(normed.shape, low), vm(back_rows.shape, low),
+            vm(dq.shape, full), vm(query_pre.shape, full), vm(key_pre.shape, full),
+            vm(gate_grad.shape, low), vm(inputs.shape, low), vm(middle_grad.shape, full),
+            vm(kv_parts.shape, low), vm(normed.shape, low),
             *[vm(weight.shape, low) for weight in weights],
             vm(fgate.shape, low), vm(fup.shape, low),
             vm((rows, q_width), low), vm((rows, kv_width), low), vm((rows, kv_width), low),
@@ -1422,7 +1894,7 @@
             into_shape(head_count, ffn_rows, hidden_width),
             vm((2 + chips + head_count, 8, width), full),
             vm((2, 64, hidden_width), full),
-            DMA((11,)),
+            DMA((17,)),
             *pair, *pair, *pair,
             *ring_sems(head_count), *ring_sems(head_count), *ring_sems(head_count),
             DMA((peers,)), DMA((peers,)),
@@ -1435,15 +1907,9 @@
         ),
         name="tail_block",
     )(
-        dq, query_pre, key_pre, gate_grad, cosine, sine_tab, query_gain[None], key_gain[None],
-        inputs, middle_grad, attn_gain[None], ffn_gain_part, gated_low,
-        kv_parts, normed, back_rows, *weights, fgate, fup,
-    )
-
-
-def contract_cols(left_mat, right_mat):
-    return lax.dot_general(
-        left_mat, right_mat, (((1,), (1,)), ((), ())), preferred_element_type=jnp.float32
+        cosine, sine_tab, query_gain[None], key_gain[None], attn_gain[None], ffn_gain_part,
+        dq, query_pre, key_pre, gate_grad, inputs, middle_grad,
+        kv_parts, normed, *weights, fgate, fup,
     )
 
 
@@ -1472,18 +1938,16 @@
     wide_pos = lax.axis_index("wide")
     local_ids = jnp.arange(query_rows, dtype=jnp.int32)
     query_tok = (local_ids // tok_dev * wide_count + wide_pos) * tok_dev + local_ids % tok_dev
-    query_seg, query_pos, query_first = token_tables(doc_lengths, query_tok)
-    starts = query_first[::tok_dev]
-    firsts = query_first[:, None]
+    query_pos = token_position(doc_lengths, query_tok)
     cosine, sine_tab = rotary(query_pos, head_width)
+    cot_left = lax.all_gather(
+        cotangent[:, : cotangent.shape[1] // 4], "wide", axis=0, tiled=True
+    )
     weights = (query_weight, key_projection, value_projection, attn_gate_weight)
     query_low, query_pre, key_pre, gate_pre, gathered, kv_all = front_block(
         inputs, attn_gain, cosine, sine_tab, query_gain, key_gain, weights
     )
-    attended, inverse, gated_low = attention_forward(
-        query_low, kv_all, starts, firsts, gate_pre
-    )
-    gate_sig = jax.nn.sigmoid(gate_pre)
+    attended, inverse, gated_low = attention_forward(doc_lengths, query_low, kv_all, gate_pre)
     (
         outputs,
         middle_grad,
@@ -1492,22 +1956,25 @@
         ffn_down_grad,
         gate_wgrad,
         up_wgrad,
+        out_wgrad,
     ) = ffn_block(
         gated_low,
         inputs,
         cotangent,
+        cot_left,
         ffn_gain,
         output_weight,
         ffn_gate_weight,
         ffn_up_weight,
         ffn_down_weight,
     )
-    gated_grad = contract_cols(back_rows, output_weight)
-    attended_grad_low = (gated_grad * gate_sig).astype(jnp.bfloat16)
-    gate_pre_grad_low = (gated_grad * attended * gate_sig * (1.0 - gate_sig)).astype(jnp.bfloat16)
-    query_rot_grad, kv_parts = attention_backward(
-        query_low, attended_grad_low, attended, inverse, kv_all, starts, firsts
-    )
+    output_grad = lax.psum_scatter(
+        out_wgrad, "wide", scatter_dimension=1, tiled=True
+    ).astype(jnp.float32)
+    query_rot_grad, kv_parts, gate_pre_grad = attention_backward(
+        doc_lengths, query_low, attended, inverse, gate_pre, kv_all, back_rows, output_weight
+    )
+    kv_parts = kv_parts.reshape(-1, kv_parts.shape[2])
     (
         input_grad,
         gains,
@@ -1515,7 +1982,6 @@
         key_grad,
         value_grad,
         attn_gate_grad,
-        output_grad,
         ffn_gate_grad,
         ffn_up_grad,
     ) = tail_block(
@@ -1523,7 +1989,7 @@
         kv_parts,
         query_pre,
         key_pre,
-        gate_pre_grad_low,
+        gate_pre_grad,
         cosine,
         sine_tab,
         query_gain,
@@ -1532,9 +1998,7 @@
         middle_grad,
         attn_gain,
         ffn_gain_part,
-        gated_low,
         gathered,
-        back_rows,
         weights,
         gate_wgrad,
         up_wgrad,

time: 403 us -> 384 us (0.953)
  Pallas kernels: 379 us -> 351 us
  between operations: 0.71 us -> 14.1 us
  matrix products: 5.26 us -> 0 us
    pallas_call x1, Pallas kernels: 168 us -> 148 us  [ffn_block(): pl.pallas_call(ffn_kernel, out_shape=(shape((tok, width), low), shape((to...]
    pallas_call x1, Pallas kernels: 125 us -> 115 us  [tail_block(): pl.pallas_call(tail_kernel, out_shape=(shape((tok, width), full), shape((...]
    dot_general x1 -> x0, matrix products: 5.26 us -> none  [contract_cols(): lax.dot_general(left_mat, right_mat, (((1,), (1,)), ((), ())), preferred_...]
    unnamed x28 -> x27, local copies, waits for them, and re-layouts: 11.2 us -> 9.05 us
  transfers between devices with their start and end apart: 0 -> 2, of which waited for: 0 -> 0; matrix products, arithmetic and copies ran while one was open for 0% -> 2% of each run, Pallas kernels for 0% -> 53%
where the time goes in v5:
time: 384 us
  Pallas kernels  351 us (91%)
  between operations  14.1 us (4%)
  local copies, waits for them, and re-layouts  13.4 us (3%)
  other arithmetic  5.36 us (1%)
    pallas_call x1, Pallas kernels, ffn_block(): pl.pallas_call(ffn_kernel, out_shape=(shape((tok, width), low), shape((to...  148 us
    pallas_call x1, Pallas kernels, tail_block(): pl.pallas_call(tail_kernel, out_shape=(shape((tok, width), full), shape((...  115 us
    pallas_call x1, Pallas kernels, front_block(): pl.pallas_call(front_kernel, out_shape=(shape((rows, q_width), low), shap...  57.3 us
    pallas_call x1, Pallas kernels, attention_backward(): pl.pallas_call(attention_backward_kernel, out_shape=(shape((rows, width),...  20.2 us
    pallas_call x1, Pallas kernels, attention_forward(): pl.pallas_call(attention_forward_kernel, out_shape=(shape((rows, width),...  11 us
    unnamed x27, local copies, waits for them, and re-layouts  9.05 us
  transfers between devices with their start and end apart: 2, of which 0 were waited for; matrix products, arithmetic and copies ran while one was open for 2% of the time, Pallas kernels for 53%

profile of v5, /device:TPU:0, one launch (start us, length us, event | category | flops | bytes accessed | tf_op | source)
XLA Modules:
  0.0 383.9 jit_solution(1075157536202336859)
XLA Ops:
  7.2 0.0 all-gather.2.cloned.1.call-start
  7.2 1.6 slice.15
  8.8 0.0 all-gather.2.cloned.1.call-update
  8.8 0.0 reduce-scatter.2.cloned.1.call-start
  8.9 0.8 reduce-window.8
  9.7 0.7 select_reduce_fusion
  10.5 1.0 multiply_sine_fusion
  11.5 1.0 pad_maximum_fusion
  12.5 57.3 %front_block.1 = (bf16[512,512]{1,0:T(8,128)(2,1)}, f32[512,512]{1,0:T(8,128)}, f32[512,256]{1,0:T(8,128)}, f32[512,512]{1,0:T(8,128)}, bf16[512,2048]{1,0:T(8,128)(2,1)}, /*index=5*/bf16[4096,512]{1,0:T(8,128)(2,1)}) custom-call(bf16[128,2048]{1,0:T(8,128)(2,1)} %x_any.3, f32[1,2048]{1,0:T(1,128)} %bitcast.20, f32[512,128]{1,0:T(8,128)} %get-tuple-element.76.cos_ref, ...), custom_call_target="tpu_custom_call" | custom-call | flops 3221225472 | bytes 104857600 | tf_op jit(solution)/shard_map/front_block/pallas_call | solution.py:1526
  69.8 11.0 %attention_forward.1 = (f32[512,512]{1,0:T(8,128)}, f32[512,512]{1,0:T(8,128)}, bf16[512,512]{1,0:T(8,128)(2,1)}) custom-call(s32[1,8]{1,0:T(1,128)} %doc_ref.3, bf16[512,512]{1,0:T(8,128)(2,1)} %get-tuple-element.42.query_any, bf16[4096,512]{1,0:T(8,128)(2,1)} %get-tuple-element.43.kv_any, f32[512,512]{1,0:T(8,128)} %get-tuple-element.44.gate_any), custom_call_target="tpu_custom_call" | custom-call | flops 2147483648 | bytes 12582912 | tf_op jit(solution)/shard_map/attention_forward/pallas_call | solution.py:729
  80.8 0.0 all-gather.2.cloned.1.call-done.left_any
  80.8 147.5 %ffn_block.1 = (bf16[128,2048]{1,0:T(8,128)(2,1)}, f32[128,2048]{1,0:T(8,128)}, f32[1,2048]{1,0:T(1,128)}, bf16[512,2048]{1,0:T(8,128)(2,1)}, f32[768,512]{1,0:T...) custom-call(bf16[512,512]{1,0:T(8,128)(2,1)} %get-tuple-element.45.gated_ref, ...), custom_call_target="tpu_custom_call" | custom-call | flops 16106127360 | bytes 209715200 | tf_op jit(solution)/shard_map/ffn_block/pallas_call | solution.py:1310
  228.4 0.0 reduce-scatter.2.cloned.1.call-update
  228.4 20.2 %attention_backward.1 = (f32[512,512]{1,0:T(8,128)}, bf16[8,512,512]{2,1,0:T(8,128)(2,1)}, bf16[512,512]{1,0:T(8,128)(2,1)}) custom-call(s32[1,8]{1,0:T(1,128)} %doc_ref.3, bf16[512,512]{1,0:T(8,128)(2,1)} %get-tuple-element.42.query_any, f32[512,512]{1,0:T(8,128)} %get-tuple-element.48.att_any, f32[512,512]{1,0:T(8,128)} %get-tuple-element.49.inv_any, ...), custom_call_target="tpu_custom_call" | custom-call | flops 5368709120 | bytes 20971520 | tf_op jit(solution)/shard_map/attention_backward/pallas_call | solution.py:879
  248.6 0.0 copy-start.4
  248.6 114.7 %tail_block.1 = (f32[128,2048]{1,0:T(8,128)}, f32[8,2048]{1,0:T(8,128)}, f32[256,512]{1,0:T(8,128)}, f32[256,256]{1,0:T(8,128)}, f32[256,256]{1,0:T(8,128)}, /*i...) custom-call(f32[512,128]{1,0:T(8,128)} %get-tuple-element.76.cos_ref, ...), custom_call_target="tpu_custom_call" | custom-call | flops 10737418240 | bytes 314572800 | tf_op jit(solution)/shard_map/tail_block/pallas_call | solution.py:1866
  363.3 0.0 copy-start.3
  363.3 0.0 copy-start.6
  363.4 1.3 slice_bitcast_fusion
  364.7 1.5 fusion.11
  366.2 0.0 reduce-scatter.2.cloned.1.call-done
  366.2 1.8 convert_element_type.11
  368.0 0.0 copy-done.4
  368.0 0.0 copy-start.8
  368.0 0.8 copy.38
  368.8 0.0 copy-done.3
  368.8 0.0 copy-start.7
  368.8 0.0 copy-start.5
  368.8 1.0 copy.39
  369.7 0.0 copy-done.6
  369.7 0.0 copy-start.2
  369.8 0.8 copy.40
  370.5 0.0 copy-done.8
  370.5 0.7 copy.41
  371.2 0.0 copy-done.7
  371.3 0.7 copy.42
  372.0 0.0 copy-done.5
  372.0 0.0 copy-start.1
  372.0 0.8 copy.43
  372.8 0.0 copy-done.2
  372.8 1.1 copy.44
  373.9 0.0 copy-done.1
  373.9 0.0 copy-start
  373.9 1.1 copy.45
  375.0 0.8 copy-done
  375.9 1.1 copy.46
  (3 shorter events, 0.0 us)
Async XLA Ops:
  7.2 73.6 %all-gather.2.cloned.1.call-start = ((), (), s32[]{:S(2)}) async-start(), calls=%async_computation.1 | async-start | bytes 1179648 | tf_op jit(solution)/shard_map/all_gather | solution.py:1943
  8.8 357.4 %reduce-scatter.2.cloned.1.call-start = ((), (), s32[]{:S(2)}) async-start(), calls=%async_computation.2 | async-start | bytes 2359296 | tf_op jit(solution)/shard_map/reduce_scatter | solution.py:1971
  248.6 119.3 %copy-start.4 = (bf16[128,2048]{1,0:T(8,128)(2,1)S(1)}, bf16[128,2048]{1,0:T(8,128)(2,1)}, u32[]{:S(2)}) copy-start(bf16[128,2048]{1,0:T(8,128)(2,1)} %get-tuple-element.92) | copy-start | bytes 1572868
  363.3 5.4 %copy-start.3 = (f32[128,2048]{1,0:T(8,128)S(1)}, f32[128,2048]{1,0:T(8,128)}, u32[]{:S(2)}) copy-start(f32[128,2048]{1,0:T(8,128)} %get-tuple-element.93) | copy-start | bytes 3145732
  363.3 6.4 %copy-start.6 = (f32[256,512]{1,0:T(8,128)S(1)}, f32[256,512]{1,0:T(8,128)}, u32[]{:S(2)}) copy-start(f32[256,512]{1,0:T(8,128)} %get-tuple-element.95) | copy-start | bytes 1572868
  368.0 2.6 copy-start.8
  368.8 2.5 copy-start.7
  368.8 3.2 copy-start.5
  369.7 3.0 copy-start.2
  372.0 1.9 copy-start.1
  373.9 2.0 copy-start
Sparse Core Ops, SparseCore 0:
  10.2 25.4 all-gather.1
  228.5 42.2 reduce-scatter.1

commit v6 on v5

--- a/solution.py
+++ b/solution.py
@@ -12,22 +12,9 @@
 VMEM_LIMIT = 63 << 20
 
 
-def token_position(doc_lengths, token_ids):
-    lengths = doc_lengths.reshape(-1)
-    before = jnp.cumsum(lengths)[None, :] <= token_ids[:, None]
-    return token_ids - jnp.sum(jnp.where(before, lengths[None, :], 0), axis=1)
-
-
-def rotary(position, head_width):
-    half_width = head_width // 2
-    inverse = THETA ** (-(jnp.arange(half_width, dtype=jnp.float32) * 2.0 / head_width))
-    angles = position.astype(jnp.float32)[:, None] * inverse[None, :]
-    cosine = jnp.cos(angles)
-    sine_tab = jnp.sin(angles)
-    return (
-        jnp.concatenate([cosine, cosine], axis=1),
-        jnp.concatenate([sine_tab, sine_tab], axis=1),
-    )
+def rotation_speed(head_width):
+    inverse = THETA ** (-(jnp.arange(head_width // 2, dtype=jnp.float32) * 2.0 / head_width))
+    return jnp.concatenate([inverse, inverse])
 
 
 MESH = pl.DeviceIdType.MESH
@@ -909,7 +896,7 @@
     gated_ref, gain_ref, x_any, cot_any, left_any, wo_any, wg_any, wu_any, wd_any,
     out_any, mgrad_ref, gain_out, back_any, down_any, fgate_any, fup_any, owg_any,
     wo, wg, wu, wd, cots, rows, hid, gg, ug, terms_own, outs_own, passed, into,
-    passed2, into2, dterms, dinto, stage, hterms, hinto, middle, back, local_sem,
+    passed2, into2, dterms, dinto, hterms, hinto, middle, back, local_sem,
     ds, dr, hs, hr, cs, cr, cps, cpr, fs, fr, fps, fpr, s1, r1, ps1, pr1, s2, r2, ps2, pr2, bs, br,
 ):
     tok, width = x_any.shape
@@ -939,8 +926,8 @@
         pltpu.make_async_copy(x_any, back.at[pl.ds(own_head, tok)], local_sem.at[13]),
     ]
     start_all(own_loads)
+    meet(neighbours(head, wide))
     own_loads[0].wait()
-    meet(neighbours(head, wide))
 
     def slot_of(ref):
         return lambda index, start, size: ref.at[pl.ds(index * tok + start, size)]
@@ -1086,15 +1073,21 @@
 
         col_loop(width, 1024, body)
 
-    emit = stage.shape[2]
+    emit = 256
+
+    def stage_of(out, slot):
+        cols = pl.ds(out * hidden_width, hidden_width)
+        return hterms.at[pl.ds(slot * emit, emit), cols]
 
     def stage_copy(step, out, any_ref, slot):
         there = pl.ds(pl.multiple_of(step * emit, emit), emit)
         return pltpu.make_async_copy(
-            stage.at[slot, out], any_ref.at[there], local_sem.at[5 + 2 * slot + out]
+            stage_of(out, slot), any_ref.at[there], local_sem.at[5 + 2 * slot + out]
         )
 
     def input_grads():
+        head_scatter.finish()
+
         @pl.loop(0, width // emit // 2)
         def _(i):
             for slot in SIDES:
@@ -1107,8 +1100,8 @@
                         stage_copy(step - 2, out, any_ref, slot).wait()
 
                 left = rows[:, cols]
-                stage[slot, 0] = dot_tn(left, gg[...]).astype(jnp.bfloat16)
-                stage[slot, 1] = dot_tn(left, ug[...]).astype(jnp.bfloat16)
+                stage_of(0, slot)[...] = dot_tn(left, gg[...]).astype(jnp.bfloat16)
+                stage_of(1, slot)[...] = dot_tn(left, ug[...]).astype(jnp.bfloat16)
                 for out, any_ref in enumerate((fgate_any, fup_any)):
                     stage_copy(step, out, any_ref, slot).start()
 
@@ -1251,7 +1244,10 @@
     back_gather.finish()
     keep = pltpu.make_async_copy(back, back_any, local_sem.at[4])
     keep.start()
-    head_scatter.finish()
+    last = width // emit
+    for slot in SIDES:
+        for out, any_ref in enumerate((fgate_any, fup_any)):
+            stage_copy(last - 2 + slot, out, any_ref, slot).wait()
     owners = gated_ref.shape[1]
 
     def out_grads(cols):
@@ -1260,6 +1256,18 @@
     col_loop(width, 512, out_grads)
     share = pltpu.make_async_copy(hterms.at[pl.ds(0, owners)], owg_any, local_sem.at[11])
     share.start()
+    down_scatter.arrive()
+    own_down = pl.multiple_of(lax.axis_index("head") * hidden_width, LANES)
+
+    def finish_down(row):
+        there = pl.ds(pl.multiple_of(own_down + row, LANES), LANES)
+        dterms[there, :] = down_scatter.total(row, LANES).astype(jnp.bfloat16)
+
+    row_loop(hidden_width, LANES, finish_down)
+    down_out = pltpu.make_async_copy(
+        dterms.at[pl.ds(own_down, hidden_width)], down_any, local_sem.at[14]
+    )
+    down_out.start()
     out_scatter.arrive()
 
     def finish_out(row):
@@ -1270,30 +1278,12 @@
     row_loop(tok, 32, finish_out)
     result = pltpu.make_async_copy(back.at[pl.ds(0, tok)], out_any, local_sem.at[9])
     result.start()
-    down_scatter.arrive()
-
-    pending = {}
-    places = width // part
-    for step in range(hidden_width // LANES):
-        place = step % places
-        if place in pending:
-            pending[place].wait()
-        spot = middle.at[:, place * part : (place + 1) * part]
-        middle[:, place * part : (place + 1) * part] = down_scatter.total(step * LANES, LANES)
-        pending[place] = pltpu.make_async_copy(
-            spot, down_any.at[pl.ds(step * LANES, LANES)], local_sem.at[14 + place % 4]
-        )
-        pending[place].start()
+
     for scatter in (grad_scatter, out_scatter, down_scatter):
         scatter.finish()
-    last = width // emit
-    for slot in SIDES:
-        for out, any_ref in enumerate((fgate_any, fup_any)):
-            stage_copy(last - 2 + slot, out, any_ref, slot).wait()
     result.wait()
     share.wait()
-    for copy in pending.values():
-        copy.wait()
+    down_out.wait()
 
 
 def ffn_block(gated_low, inputs, cotangent, cot_left, ffn_gain, out_w, gate_w, up_w, down_w):
@@ -1314,7 +1304,7 @@
             shape((tok, width), full),
             shape((1, width), full),
             shape((back_rows, width), low),
-            shape((hidden_width, width // head_count), full),
+            shape((hidden_width, width // head_count), low),
             shape((width, hidden_width), low),
             shape((width, hidden_width), low),
             shape((gated_low.shape[1], width), low),
@@ -1335,10 +1325,9 @@
             scatter_into(chips, tok, width),
             vm((head_count * hidden_width, width // head_count), low),
             into_shape(head_count, hidden_width, width // head_count),
-            vm((2, 2, 128, hidden_width), low),
             vm((back_rows, width), low), into_shape(head_count, tok, width),
             vm((tok, width), full), vm((back_rows, width), low),
-            DMA((18,)),
+            DMA((15,)),
             *ring_sems(head_count),
             *ring_sems(head_count),
             *ring_sems(chips), *pass_sems(chips),
@@ -1372,8 +1361,8 @@
 
 
 def front_kernel(
-    x_ref, gain_ref, cos_ref, sin_ref, qgain_ref, kgain_ref, wq_any, wk_any, wv_any, wg_any,
-    query_ref, qpre_ref, kpre_ref, gpre_ref, normed_any, kv_any,
+    doc_ref, x_ref, gain_ref, speed_ref, qgain_ref, kgain_ref, wq_any, wk_any, wv_any, wg_any,
+    query_ref, qpre_ref, kpre_ref, gpre_ref, cos_ref, sin_ref, normed_any, kv_any,
     wq, wk, wv, wg, normed, kv, local_sem, hs, hr, ks, kr, kps, kpr,
 ):
     tok, width = x_ref.shape
@@ -1404,6 +1393,16 @@
         head, lambda index, start, size: normed.at[pl.ds(index * tok + start, size)], tok, hs, hr
     )
     gather.start(1)
+    ends = doc_ends(doc_ref)
+
+    @pl.loop(0, head_count)
+    def _(block):
+        here = pl.ds(pl.multiple_of(block * tok, tok), tok)
+        first_tok = (block * wide_count + own_wide) * tok
+        tokens = lax.broadcasted_iota(jnp.int32, (tok, LANES), 0) + first_tok
+        angles = (tokens - first_of(ends, tokens)).astype(jnp.float32) * speed_ref[...]
+        cos_ref[here, :] = jnp.cos(angles)
+        sin_ref[here, :] = jnp.sin(angles)
 
     def kv_gather(offset):
         slot = offset % head_count
@@ -1515,7 +1514,7 @@
     keep.wait()
 
 
-def front_block(inputs, attn_gain, cosine, sine_tab, query_gain, key_gain, weights):
+def front_block(doc_lengths, inputs, attn_gain, speed, query_gain, key_gain, weights):
     tok, width = inputs.shape
     head_count, wide_count = lax.axis_size("head"), lax.axis_size("wide")
     chips = wide_count // 2
@@ -1530,11 +1529,13 @@
             shape((rows, q_width), full),
             shape((rows, kv_width), full),
             shape((rows, q_width), full),
+            shape((rows, LANES), full),
+            shape((rows, LANES), full),
             shape((rows, width), low),
             shape((rows * wide_count, 2 * kv_width), low),
         ),
-        in_specs=[VMEM] * 6 + [ANY] * 4,
-        out_specs=tuple([VMEM] * 4 + [ANY] * 2),
+        in_specs=[pl.BlockSpec(memory_space=pltpu.SMEM)] + [VMEM] * 5 + [ANY] * 4,
+        out_specs=tuple([VMEM] * 6 + [ANY] * 2),
         scratch_shapes=[
             *[vm(weight.shape, low) for weight in weights],
             vm((rows, width), low),
@@ -1552,7 +1553,8 @@
         ),
         name="front_block",
     )(
-        inputs, attn_gain[None], cosine, sine_tab, query_gain[None], key_gain[None], *weights
+        doc_lengths, inputs, attn_gain[None], speed[None], query_gain[None], key_gain[None],
+        *weights,
     )
 
 
@@ -1579,7 +1581,7 @@
     igrad_ref, gains_ref, query_out, key_out, value_out, gate_out, fgate_out, fup_out,
     dq_ref, qpre_ref, kpre_ref, ggrad_ref, x_ref, mgrad_ref, kvp, normed, wq, wk, wv, wg, fgate, fup, qlow, klow, vlow, early, late, hterms,
     kv_passed, kv_into, early_passed, early_into, late_passed, late_into, hinto, fgate_into,
-    fup_into, gain_slots, stage, local_sem,
+    fup_into, gain_slots, local_sem,
     kvs, kvr, kvps, kvpr, es, er, eps, epr, ls, lr, lps, lpr, hs, hr, gs, gr, us, ur, gain_send,
     gain_recv,
 ):
@@ -1687,6 +1689,8 @@
     for load in loads[4:] + more[3:]:
         load.wait()
     kv_scatter.arrive()
+    for hop in range(wide.half - 1, 0, -1):
+        early_scatter.advance(hop)
 
     def key_back(row, total):
         here = pl.ds(row, chunk)
@@ -1731,8 +1735,6 @@
     for offset in order:
         late_part(offset)
         late_scatter.hand(offset)
-    for hop in range(wide.half - 1, 0, -1):
-        early_scatter.advance(hop)
     late_scatter.merge(order[0])
     late_scatter.start(wide.half)
     for hop in range(head.half - 1, 0, -1):
@@ -1747,17 +1749,21 @@
 
     gate_scatter.arrive()
     up_scatter.arrive()
-    emit = 64
-    pending = [None, None]
-    for step in range(ffn_rows // emit):
-        for which, (scatter, out) in enumerate(((gate_scatter, fgate_out), (up_scatter, fup_out))):
-            if pending[which] is not None:
-                pending[which].wait()
-            stage[which] = scatter.total(step * emit, emit)
-            pending[which] = pltpu.make_async_copy(
-                stage.at[which], out.at[pl.ds(step * emit, emit)], local_sem.at[9 + which]
+    own_ffn = pl.multiple_of(lax.axis_index("head") * ffn_rows, ffn_rows)
+    pending = []
+    for scatter, ref, out in ((gate_scatter, fgate, fgate_out), (up_scatter, fup, fup_out)):
+
+        def finish_ffn(row, scatter=scatter, ref=ref):
+            there = pl.ds(pl.multiple_of(own_ffn + row, 64), 64)
+            ref[there, :] = scatter.total(row, 64).astype(jnp.bfloat16)
+
+        row_loop(ffn_rows, 64, finish_ffn)
+        pending.append(
+            pltpu.make_async_copy(
+                ref.at[pl.ds(own_ffn, ffn_rows)], out, local_sem.at[9 + len(pending)]
             )
-            pending[which].start()
+        )
+        pending[-1].start()
 
     head_scatter.arrive()
     gain = gain_ref[...]
@@ -1823,8 +1829,8 @@
     def early_out(row):
         here = pl.ds(row, 32)
         both = early_scatter.total(row, 32)
-        query_out[here, :] = both[:, :q_width]
-        gate_out[here, :] = both[:, q_width:]
+        query_out[here, :] = both[:, :q_width].astype(jnp.bfloat16)
+        gate_out[here, :] = both[:, q_width:].astype(jnp.bfloat16)
 
     row_loop(block, 32, early_out)
     late_scatter.arrive()
@@ -1832,8 +1838,8 @@
     def late_out(row):
         here = pl.ds(row, 32)
         both = late_scatter.total(row, 32)
-        key_out[here, :] = both[:, :kv_width]
-        value_out[here, :] = both[:, kv_width:]
+        key_out[here, :] = both[:, :kv_width].astype(jnp.bfloat16)
+        value_out[here, :] = both[:, kv_width:].astype(jnp.bfloat16)
 
     row_loop(block, 32, late_out)
     for scatter in (
@@ -1868,12 +1874,12 @@
         out_shape=(
             shape((tok, width), full),
             shape((8, width), full),
-            shape((block, q_width), full),
-            shape((block, kv_width), full),
-            shape((block, kv_width), full),
-            shape((block, q_width), full),
-            shape((ffn_rows, hidden_width), full),
-            shape((ffn_rows, hidden_width), full),
+            shape((block, q_width), low),
+            shape((block, kv_width), low),
+            shape((block, kv_width), low),
+            shape((block, q_width), low),
+            shape((ffn_rows, hidden_width), low),
+            shape((ffn_rows, hidden_width), low),
         ),
         in_specs=[VMEM] * 6 + [ANY] * 14,
         out_specs=tuple([VMEM] * 6 + [ANY] * 2),
@@ -1893,7 +1899,6 @@
             into_shape(head_count, ffn_rows, hidden_width),
             into_shape(head_count, ffn_rows, hidden_width),
             vm((2 + chips + head_count, 8, width), full),
-            vm((2, 64, hidden_width), full),
             DMA((17,)),
             *pair, *pair, *pair,
             *ring_sems(head_count), *ring_sems(head_count), *ring_sems(head_count),
@@ -1911,6 +1916,62 @@
         dq, query_pre, key_pre, gate_grad, inputs, middle_grad,
         kv_parts, normed, *weights, fgate, fup,
     )
+
+
+def finish_kernel(count, *refs):
+    sources, gains_any = refs[:count], refs[count]
+    results = refs[count + 1 : 2 * count + 1]
+    gain_outs = refs[2 * count + 1 : 2 * count + 5]
+    landed = refs[2 * count + 5 : 3 * count + 5]
+    *spare, gains, in_sem, out_sem = refs[3 * count + 5 :]
+    loads = [
+        pltpu.make_async_copy(sources[i], landed[i], in_sem.at[i]) for i in range(count)
+    ]
+    last = pltpu.make_async_copy(gains_any, gains, in_sem.at[count])
+    start_all([*loads, last])
+    stores = []
+    for i in range(count):
+        ready = landed[i]
+        loads[i].wait()
+        if sources[i].dtype != results[i].dtype:
+            ready = spare.pop(0)
+            rows = ready.shape[0]
+            step = min(rows, 128)
+
+            def convert(row, src=landed[i], dst=ready, step=step):
+                here = pl.ds(row, step)
+                dst[here, :] = src[here, :].astype(jnp.float32)
+
+            row_loop(rows, step, convert)
+        stores.append(pltpu.make_async_copy(ready, results[i], out_sem.at[i]))
+        stores[-1].start()
+    last.wait()
+    for row, out in enumerate(gain_outs):
+        out[...] = gains[row : row + 1, : out.shape[1]]
+    for store in stores:
+        store.wait()
+
+
+def finish_block(arrays, dtypes, gains, head_width):
+    shape, vm = jax.ShapeDtypeStruct, pltpu.VMEM
+    width = gains.shape[1]
+    sizes = (width, width, head_width, head_width)
+    outs = pl.pallas_call(
+        functools.partial(finish_kernel, len(arrays)),
+        out_shape=tuple(shape(a.shape, d) for a, d in zip(arrays, dtypes))
+        + tuple(shape((1, size), jnp.float32) for size in sizes),
+        in_specs=[ANY] * (len(arrays) + 1),
+        out_specs=tuple([ANY] * len(arrays) + [VMEM] * 4),
+        scratch_shapes=[
+            *[vm(a.shape, a.dtype) for a in arrays],
+            *[vm(a.shape, d) for a, d in zip(arrays, dtypes) if a.dtype != d],
+            vm(gains.shape, jnp.float32),
+            DMA((len(arrays) + 1,)), DMA((len(arrays),)),
+        ],
+        compiler_params=pltpu.CompilerParams(vmem_limit_bytes=VMEM_LIMIT),
+        name="finish_block",
+    )(*arrays, gains)
+    return outs[: len(arrays)], [gain.reshape(-1) for gain in outs[len(arrays) :]]
 
 
 def shards(
@@ -1930,22 +1991,13 @@
     doc_lengths,
     cotangent,
 ):
-    tok_dev = inputs.shape[0]
     head_width = query_gain.shape[0]
-    head_count = lax.axis_size("head")
-    wide_count = lax.axis_size("wide")
-    query_rows = tok_dev * head_count
-    wide_pos = lax.axis_index("wide")
-    local_ids = jnp.arange(query_rows, dtype=jnp.int32)
-    query_tok = (local_ids // tok_dev * wide_count + wide_pos) * tok_dev + local_ids % tok_dev
-    query_pos = token_position(doc_lengths, query_tok)
-    cosine, sine_tab = rotary(query_pos, head_width)
     cot_left = lax.all_gather(
         cotangent[:, : cotangent.shape[1] // 4], "wide", axis=0, tiled=True
     )
     weights = (query_weight, key_projection, value_projection, attn_gate_weight)
-    query_low, query_pre, key_pre, gate_pre, gathered, kv_all = front_block(
-        inputs, attn_gain, cosine, sine_tab, query_gain, key_gain, weights
+    query_low, query_pre, key_pre, gate_pre, cosine, sine_tab, gathered, kv_all = front_block(
+        doc_lengths, inputs, attn_gain, rotation_speed(head_width), query_gain, key_gain, weights
     )
     attended, inverse, gated_low = attention_forward(doc_lengths, query_low, kv_all, gate_pre)
     (
@@ -1968,9 +2020,7 @@
         ffn_up_weight,
         ffn_down_weight,
     )
-    output_grad = lax.psum_scatter(
-        out_wgrad, "wide", scatter_dimension=1, tiled=True
-    ).astype(jnp.float32)
+    output_grad = lax.psum_scatter(out_wgrad, "wide", scatter_dimension=1, tiled=True)
     query_rot_grad, kv_parts, gate_pre_grad = attention_backward(
         doc_lengths, query_low, attended, inverse, gate_pre, kv_all, back_rows, output_weight
     )
@@ -2003,8 +2053,27 @@
         gate_wgrad,
         up_wgrad,
     )
-    attn_gain_grad, ffn_gain_grad = gains[0], gains[1]
-    query_gain_grad, key_gain_grad = gains[2, :head_width], gains[3, :head_width]
+    full = jnp.float32
+    results, gain_grads = finish_block(
+        [
+            outputs,
+            input_grad,
+            query_grad,
+            key_grad,
+            value_grad,
+            attn_gate_grad,
+            output_grad,
+            ffn_gate_grad,
+            ffn_up_grad,
+            ffn_down_grad,
+        ],
+        [jnp.bfloat16] + [full] * 9,
+        gains,
+        head_width,
+    )
+    outputs, input_grad, query_grad, key_grad, value_grad = results[:5]
+    attn_gate_grad, output_grad, ffn_gate_grad, ffn_up_grad, ffn_down_grad = results[5:]
+    attn_gain_grad, ffn_gain_grad, query_gain_grad, key_gain_grad = gain_grads
     return (
         outputs,
         input_grad,

time: 384 us -> 374 us (0.974)
  local copies, waits for them, and re-layouts: 13.4 us -> 1.57 us
  Pallas kernels: 351 us -> 357 us
  other arithmetic: 5.36 us -> 0.6 us
    unnamed x27 -> x0, local copies, waits for them, and re-layouts: 9.05 us -> none
    pallas_call x0 -> x1, Pallas kernels: none -> 5.36 us  [finish_block(): pl.pallas_call(functools.partial(finish_kernel, len(arrays)), out_shape=t...]
    pallas_call x1, Pallas kernels: 148 us -> 143 us  [ffn_block(): pl.pallas_call(ffn_kernel, out_shape=(shape((tok, width), low), shape((to...]
  transfers between devices with their start and end apart: 2 -> 2, of which waited for: 0 -> 0; matrix products, arithmetic and copies ran while one was open for 2% -> 0% of each run, Pallas kernels for 53% -> 56%
where the time goes in v6:
time: 374 us; the launch traced here: 373 us
  Pallas kernels  357 us (95%)
  between operations  14.1 us (4%)
    pallas_call x1, Pallas kernels, ffn_block(): pl.pallas_call(ffn_kernel, out_shape=(shape((tok, width), low), shape((to...  143 us
    pallas_call x1, Pallas kernels, tail_block(): pl.pallas_call(tail_kernel, out_shape=(shape((tok, width), full), shape((...  114 us
    pallas_call x1, Pallas kernels, front_block(): pl.pallas_call(front_kernel, out_shape=(shape((rows, q_width), low), shap...  60 us
    pallas_call x1, Pallas kernels, attention_backward(): pl.pallas_call(attention_backward_kernel, out_shape=(shape((rows, width),...  21.8 us
    pallas_call x1, Pallas kernels, attention_forward(): pl.pallas_call(attention_forward_kernel, out_shape=(shape((rows, width),...  12.7 us
  transfers between devices with their start and end apart: 2, of which 0 were waited for; matrix products, arithmetic and copies ran while one was open for 0% of the time, Pallas kernels for 56%

profile of v6, /device:TPU:0, one launch (start us, length us, event | category | flops | bytes accessed | tf_op | source)
XLA Modules:
  0.0 373.5 jit_solution(9000027932891278055)
XLA Ops:
  7.2 0.0 all-gather.2.cloned.1.call-start
  7.2 1.6 slice.3
  8.8 0.0 all-gather.2.cloned.1.call-update
  8.8 0.0 reduce-scatter.2.cloned.1.call-start
  8.9 0.6 maximum_bitcast_fusion.speed_ref
  9.5 60.0 %front_block.1 = (bf16[512,512]{1,0:T(8,128)(2,1)}, f32[512,512]{1,0:T(8,128)}, f32[512,256]{1,0:T(8,128)}, f32[512,512]{1,0:T(8,128)}, f32[512,128]{1,0:T(8,128...) custom-call(s32[1,8]{1,0:T(1,128)} %doc_ref.5, bf16[128,2048]{1,0:T(8,128)(2,1)} %x_any.3, ...), custom_call_target="tpu_custom_call" | custom-call | flops 3221225472 | bytes 104857600 | tf_op jit(solution)/shard_map/front_block/pallas_call | solution.py:1525
  69.5 12.7 %attention_forward.1 = (f32[512,512]{1,0:T(8,128)}, f32[512,512]{1,0:T(8,128)}, bf16[512,512]{1,0:T(8,128)(2,1)}) custom-call(s32[1,8]{1,0:T(1,128)} %doc_ref.5, bf16[512,512]{1,0:T(8,128)(2,1)} %get-tuple-element.58.query_any, bf16[4096,512]{1,0:T(8,128)(2,1)} %get-tuple-element.59.kv_any, f32[512,512]{1,0:T(8,128)} %get-tuple-element.60.gate_any), custom_call_target="tpu_custom_call" | custom-call | flops 2147483648 | bytes 12582912 | tf_op jit(solution)/shard_map/attention_forward/pallas_call | solution.py:716
  82.2 0.0 all-gather.2.cloned.1.call-done.left_any
  82.2 143.1 %ffn_block.1 = (bf16[128,2048]{1,0:T(8,128)(2,1)}, f32[128,2048]{1,0:T(8,128)}, f32[1,2048]{1,0:T(1,128)}, bf16[512,2048]{1,0:T(8,128)(2,1)}, bf16[768,512]{1,0:...) custom-call(bf16[512,512]{1,0:T(8,128)(2,1)} %get-tuple-element.61.gated_ref, ...), custom_call_target="tpu_custom_call" | custom-call | flops 16106127360 | bytes 209715200 | tf_op jit(solution)/shard_map/ffn_block/pallas_call | solution.py:1300
  225.4 0.0 reduce-scatter.2.cloned.1.call-update
  225.4 21.8 %attention_backward.1 = (f32[512,512]{1,0:T(8,128)}, bf16[8,512,512]{2,1,0:T(8,128)(2,1)}, bf16[512,512]{1,0:T(8,128)(2,1)}) custom-call(s32[1,8]{1,0:T(1,128)} %doc_ref.5, bf16[512,512]{1,0:T(8,128)(2,1)} %get-tuple-element.58.query_any, f32[512,512]{1,0:T(8,128)} %get-tuple-element.66.att_any, f32[512,512]{1,0:T(8,128)} %get-tuple-element.67.inv_any, ...), custom_call_target="tpu_custom_call" | custom-call | flops 5368709120 | bytes 20971520 | tf_op jit(solution)/shard_map/attention_backward/pallas_call | solution.py:866
  247.3 113.9 %tail_block.1 = (f32[128,2048]{1,0:T(8,128)}, f32[8,2048]{1,0:T(8,128)}, bf16[256,512]{1,0:T(8,128)(2,1)}, bf16[256,256]{1,0:T(8,128)(2,1)}, bf16[256,256]{1,0:T...) custom-call(f32[512,128]{1,0:T(8,128)} %get-tuple-element.63.cos_ref, ...), custom_call_target="tpu_custom_call" | custom-call | flops 10737418240 | bytes 314572800 | tf_op jit(solution)/shard_map/tail_block/pallas_call | solution.py:1872
  361.2 0.0 reduce-scatter.2.cloned.1.call-done.refs_6_
  361.2 5.4 %finish_block.1 = (bf16[128,2048]{1,0:T(8,128)(2,1)}, f32[128,2048]{1,0:T(8,128)}, f32[256,512]{1,0:T(8,128)}, f32[256,256]{1,0:T(8,128)}, f32[256,256]{1,0:T(8,...) custom-call(bf16[128,2048]{1,0:T(8,128)(2,1)} %get-tuple-element.62., ...), custom_call_target="tpu_custom_call" | custom-call | tf_op jit(solution)/shard_map/finish_block/pallas_call | solution.py:1959
  (1 shorter events, 0.0 us)
Async XLA Ops:
  7.2 75.1 %all-gather.2.cloned.1.call-start = ((), (), s32[]{:S(2)}) async-start(), calls=%async_computation.1 | async-start | bytes 1179648 | tf_op jit(solution)/shard_map/all_gather | solution.py:1995
  8.8 352.4 %reduce-scatter.2.cloned.1.call-start = ((), (), s32[]{:S(2)}) async-start(), calls=%async_computation.2 | async-start | bytes 2359296 | tf_op jit(solution)/shard_map/reduce_scatter | solution.py:2023
Sparse Core Ops, SparseCore 0:
  10.2 26.0 all-gather.1
  225.5 42.6 reduce-scatter.1

commit v7 on v6

--- a/solution.py
+++ b/solution.py
@@ -88,36 +88,64 @@
     )
 
 
-class Gather:
+class Ways:
+    def span(self, hop, side, piece=None):
+        half = self.rows // 2
+        if hop == self.ring.half:
+            return side * half, half
+        if piece is not None:
+            return piece * half, half
+        return 0, self.rows
+
+    def halved(self, hop):
+        return hop == self.ring.half - 1
+
+    def pieces(self, hop, side):
+        return (side, 1 - side) if self.halved(hop) else (None,)
+
+    def all_copies(self, hop):
+        for nth in range(2 if self.halved(hop) else 1):
+            for side in SIDES:
+                yield self.copy(hop, side, self.pieces(hop, side)[nth])
+
+    def start(self, hop):
+        for copy in self.all_copies(hop):
+            copy.start()
+
+    def sems(self, hop, side, piece):
+        which = 0 if piece is None else piece
+        return self.send.at[side, hop - 1, which], self.recv.at[side, hop - 1, which]
+
+    def finish(self):
+        for hop in range(1, self.ring.half + 1):
+            for copy in self.all_copies(hop):
+                copy.wait_send()
+
+
+class Gather(Ways):
     def __init__(self, ring, slot, rows, send, recv):
         self.ring, self.slot, self.rows = ring, slot, rows
         self.send, self.recv = send, recv
 
-    def span(self, hop, side):
-        if 2 * hop == self.ring.size:
-            return side * (self.rows // 2), self.rows // 2
-        return 0, self.rows
-
-    def copy(self, hop, side):
+    def copy(self, hop, side, piece=None):
         way = 1 - 2 * side
-        ref = self.slot(self.ring.index(-way * (hop - 1)), *self.span(hop, side))
-        return remote(
-            ref, ref, self.send.at[side, hop - 1], self.recv.at[side, hop - 1],
-            self.ring.device(way),
-        )
-
-    def start(self, hop):
+        ref = self.slot(self.ring.index(-way * (hop - 1)), *self.span(hop, side, piece))
+        return remote(ref, ref, *self.sems(hop, side, piece), self.ring.device(way))
+
+    def arrive(self, hop):
+        for copy in self.all_copies(hop):
+            copy.wait_recv()
+
+    def step(self, hop):
+        if not self.halved(hop):
+            self.arrive(hop)
+            self.start(hop + 1)
+            return
         for side in SIDES:
-            self.copy(hop, side).start()
-
-    def arrive(self, hop):
+            self.copy(hop, side, side).wait_recv()
+            self.copy(hop + 1, side).start()
         for side in SIDES:
-            self.copy(hop, side).wait_recv()
-
-    def finish(self):
-        for hop in range(1, self.ring.half + 1):
-            for side in SIDES:
-                self.copy(hop, side).wait_send()
+            self.copy(hop, side, 1 - side).wait_recv()
 
 
 class PairGather(Gather):
@@ -162,36 +190,35 @@
         body(pl.multiple_of(step * chunk, chunk))
 
 
-class Scatter:
+class Scatter(Ways):
     def __init__(self, ring, part, rows, into, send, recv):
         self.ring, self.part, self.rows, self.into = ring, part, rows, into
         self.send, self.recv = send, recv
-
-    def span(self, hop, side):
-        if 2 * hop == self.ring.size:
-            return side * (self.rows // 2), self.rows // 2
-        return 0, self.rows
-
-    def copy(self, hop, side):
+        self.freed = False
+
+    def inside(self, hop, row):
+        return row % (self.rows // 2) if hop == self.ring.half else row
+
+    def copy(self, hop, side, piece=None):
         way = 1 - 2 * side
-        first, count = self.span(hop, side)
+        first, count = self.span(hop, side, piece)
         ref, base = self.part(self.ring.index(way * hop))
         return remote(
             ref.at[pl.ds(base + first, count)],
             self.into.at[side, pl.ds((hop - 1) * self.rows + self.inside(hop, first), count)],
-            self.send.at[side, hop - 1], self.recv.at[side, hop - 1], self.ring.device(way),
+            *self.sems(hop, side, piece), self.ring.device(way),
         )
 
-    def inside(self, hop, row):
-        return row % (self.rows // 2) if 2 * hop == self.ring.size else row
-
-    def start(self, hop):
-        for side in SIDES:
-            self.copy(hop, side).start()
+    def start_free(self):
+        self.freed = True
+        if self.ring.half > 1:
+            for side in SIDES:
+                self.copy(self.ring.half - 1, side, 1 - side).start()
 
     def fold(self, hop, side):
         way = 1 - 2 * side
-        self.copy(hop + 1, side).wait_recv()
+        for copy in [self.copy(hop + 1, side, piece) for piece in self.pieces(hop + 1, side)]:
+            copy.wait_recv()
         first, count = self.span(hop + 1, side)
         ref, base = self.part(self.ring.index(way * hop))
         chunk = min(count, 32)
@@ -207,13 +234,15 @@
         row_loop(count, chunk, add)
 
     def advance(self, hop):
+        if self.halved(hop) and not self.freed:
+            self.start_free()
         for side in SIDES:
             self.fold(hop, side)
-            self.copy(hop, side).start()
+            self.copy(hop, side, self.pieces(hop, side)[0]).start()
 
     def arrive(self):
-        for side in SIDES:
-            self.copy(1, side).wait_recv()
+        for copy in self.all_copies(1):
+            copy.wait_recv()
 
     def total(self, row, count):
         ref, base = self.part(self.ring.index(0))
@@ -224,11 +253,6 @@
             + self.into[0, here, :].astype(jnp.float32)
             + self.into[1, here, :].astype(jnp.float32)
         )
-
-    def finish(self):
-        for hop in range(1, self.ring.half + 1):
-            for side in SIDES:
-                self.copy(hop, side).wait_send()
 
 
 class PairScatter(Scatter):
@@ -296,7 +320,7 @@
 
 
 def ring_sems(size):
-    return [DMA((2, size // 2)), DMA((2, size // 2))]
+    return [DMA((2, size // 2, 2)), DMA((2, size // 2, 2))]
 
 
 def pass_sems(size):
@@ -985,6 +1009,8 @@
     for hop in range(head.half - 1, 0, -1):
         out_part(hop, False)
         out_part(-hop, False)
+        if hop == head.half - 1:
+            head_scatter.start_free()
     out_part(0, True)
     loads[1].wait()
     loads[4].wait()
@@ -1157,6 +1183,7 @@
         grad_scatter.hand_kind(None)
         down_grads([1, 2, 3], True)
         down_scatter.start(head.half)
+        down_scatter.start_free()
         grad_scatter.relay(OTHER)
         for kind in (OTHER, FAR, NEAR, None):
             out_scatter.merge_kind(kind)
@@ -1238,8 +1265,7 @@
         for hop in range(wide.half - 1, 0, -1):
             out_scatter.advance(hop)
     for hop in range(1, head.half):
-        back_gather.arrive(hop)
-        back_gather.start(hop + 1)
+        back_gather.step(hop)
     back_gather.arrive(head.half)
     back_gather.finish()
     keep = pltpu.make_async_copy(back, back_any, local_sem.at[4])
@@ -1479,9 +1505,8 @@
     project_rest(0)
     done = [0]
     for hop in range(1, head.half + 1):
-        gather.arrive(hop)
         if hop < head.half:
-            gather.start(hop + 1)
+            gather.step(hop)
             launch(hop)
             launch(-hop)
             for offset in done:
@@ -1490,6 +1515,7 @@
             project_rest(-hop)
             done = [hop, -hop]
         else:
+            gather.arrive(hop)
             launch(hop)
             for offset in done:
                 step(offset, 1)
@@ -1629,8 +1655,10 @@
         kv_scatter.hand(offset)
     loads[1].wait()
     gate_scatter.start(head.half)
+    gate_scatter.start_free()
     loads[2].wait()
     up_scatter.start(head.half)
+    up_scatter.start_free()
 
     for load in more[:3]:
         load.wait()
@@ -1658,6 +1686,9 @@
 
     kv_scatter.merge(order[0])
     kv_scatter.start(wide.half)
+    for offset in order[1:]:
+        kv_scatter.merge(offset)
+    kv_scatter.start_free()
     loads[3].wait()
 
     def early_part(offset):
@@ -1675,14 +1706,13 @@
     for offset in order:
         early_part(offset)
         early_scatter.hand(offset)
-    for offset in order[1:]:
-        kv_scatter.merge(offset)
     early_scatter.merge(order[0])
     for hop in range(wide.half - 1, 0, -1):
         kv_scatter.advance(hop)
     early_scatter.start(wide.half)
     for offset in order[1:]:
         early_scatter.merge(offset)
+    early_scatter.start_free()
     for hop in range(head.half - 1, 0, -1):
         gate_scatter.advance(hop)
         up_scatter.advance(hop)
@@ -1737,13 +1767,14 @@
         late_scatter.hand(offset)
     late_scatter.merge(order[0])
     late_scatter.start(wide.half)
+    for offset in order[1:]:
+        late_scatter.merge(offset)
+    late_scatter.start_free()
     for hop in range(head.half - 1, 0, -1):
         head_part(hop)
         head_part(-hop)
         head_scatter.advance(hop)
     head_part(0)
-    for offset in order[1:]:
-        late_scatter.merge(offset)
     for hop in range(wide.half - 1, 0, -1):
         late_scatter.advance(hop)
 

time: 374 us -> 364 us (0.973)
  Pallas kernels: 357 us -> 346 us
    pallas_call x1, Pallas kernels: 114 us -> 109 us  [tail_block(): pl.pallas_call(tail_kernel, out_shape=(shape((tok, width), full), shape((...]
  transfers between devices with their start and end apart: 2 -> 2, of which waited for: 0 -> 0; matrix products, arithmetic and copies ran while one was open for 0% -> 0% of each run, Pallas kernels for 56% -> 55%
where the time goes in v7:
time: 364 us; the launch traced here: 363 us
  Pallas kernels  346 us (95%)
  between operations  14.1 us (4%)
    pallas_call x1, Pallas kernels, ffn_block(): pl.pallas_call(ffn_kernel, out_shape=(shape((tok, width), low), shape((to...  141 us
    pallas_call x1, Pallas kernels, tail_block(): pl.pallas_call(tail_kernel, out_shape=(shape((tok, width), full), shape((...  109 us
    pallas_call x1, Pallas kernels, front_block(): pl.pallas_call(front_kernel, out_shape=(shape((rows, q_width), low), shap...  59.9 us
    pallas_call x1, Pallas kernels, attention_backward(): pl.pallas_call(attention_backward_kernel, out_shape=(shape((rows, width),...  20.2 us
    pallas_call x1, Pallas kernels, attention_forward(): pl.pallas_call(attention_forward_kernel, out_shape=(shape((rows, width),...  11 us
  transfers between devices with their start and end apart: 2, of which 0 were waited for; matrix products, arithmetic and copies ran while one was open for 0% of the time, Pallas kernels for 55%

profile of v7, /device:TPU:0, one launch (start us, length us, event | category | flops | bytes accessed | tf_op | source)
XLA Modules:
  0.0 362.9 jit_solution(8430132696124127792)
XLA Ops:
  7.2 0.0 all-gather.2.cloned.1.call-start
  7.2 1.6 slice.3
  8.8 0.0 all-gather.2.cloned.1.call-update
  8.8 0.0 reduce-scatter.2.cloned.1.call-start
  8.9 0.6 maximum_bitcast_fusion.speed_ref
  9.5 59.9 %front_block.1 = (bf16[512,512]{1,0:T(8,128)(2,1)}, f32[512,512]{1,0:T(8,128)}, f32[512,256]{1,0:T(8,128)}, f32[512,512]{1,0:T(8,128)}, f32[512,128]{1,0:T(8,128...) custom-call(s32[1,8]{1,0:T(1,128)} %doc_ref.5, bf16[128,2048]{1,0:T(8,128)(2,1)} %x_any.3, ...), custom_call_target="tpu_custom_call" | custom-call | flops 3221225472 | bytes 104857600 | tf_op jit(solution)/shard_map/front_block/pallas_call | solution.py:1551
  69.4 11.0 %attention_forward.1 = (f32[512,512]{1,0:T(8,128)}, f32[512,512]{1,0:T(8,128)}, bf16[512,512]{1,0:T(8,128)(2,1)}) custom-call(s32[1,8]{1,0:T(1,128)} %doc_ref.5, bf16[512,512]{1,0:T(8,128)(2,1)} %get-tuple-element.58.query_any, bf16[4096,512]{1,0:T(8,128)(2,1)} %get-tuple-element.59.kv_any, f32[512,512]{1,0:T(8,128)} %get-tuple-element.60.gate_any), custom_call_target="tpu_custom_call" | custom-call | flops 2147483648 | bytes 12582912 | tf_op jit(solution)/shard_map/attention_forward/pallas_call | solution.py:740
  80.4 0.0 all-gather.2.cloned.1.call-done.left_any
  80.5 141.4 %ffn_block.1 = (bf16[128,2048]{1,0:T(8,128)(2,1)}, f32[128,2048]{1,0:T(8,128)}, f32[1,2048]{1,0:T(1,128)}, bf16[512,2048]{1,0:T(8,128)(2,1)}, bf16[768,512]{1,0:...) custom-call(bf16[512,512]{1,0:T(8,128)(2,1)} %get-tuple-element.61.gated_ref, ...), custom_call_target="tpu_custom_call" | custom-call | flops 16106127360 | bytes 209715200 | tf_op jit(solution)/shard_map/ffn_block/pallas_call | solution.py:1326
  221.9 0.0 reduce-scatter.2.cloned.1.call-update
  221.9 20.2 %attention_backward.1 = (f32[512,512]{1,0:T(8,128)}, bf16[8,512,512]{2,1,0:T(8,128)(2,1)}, bf16[512,512]{1,0:T(8,128)(2,1)}) custom-call(s32[1,8]{1,0:T(1,128)} %doc_ref.5, bf16[512,512]{1,0:T(8,128)(2,1)} %get-tuple-element.58.query_any, f32[512,512]{1,0:T(8,128)} %get-tuple-element.66.att_any, f32[512,512]{1,0:T(8,128)} %get-tuple-element.67.inv_any, ...), custom_call_target="tpu_custom_call" | custom-call | flops 5368709120 | bytes 20971520 | tf_op jit(solution)/shard_map/attention_backward/pallas_call | solution.py:890
  242.1 108.5 %tail_block.1 = (f32[128,2048]{1,0:T(8,128)}, f32[8,2048]{1,0:T(8,128)}, bf16[256,512]{1,0:T(8,128)(2,1)}, bf16[256,256]{1,0:T(8,128)(2,1)}, bf16[256,256]{1,0:T...) custom-call(f32[512,128]{1,0:T(8,128)} %get-tuple-element.63.cos_ref, ...), custom_call_target="tpu_custom_call" | custom-call | flops 10737418240 | bytes 314572800 | tf_op jit(solution)/shard_map/tail_block/pallas_call | solution.py:1903
  350.6 0.0 reduce-scatter.2.cloned.1.call-done.refs_6_
  350.7 5.4 %finish_block.1 = (bf16[128,2048]{1,0:T(8,128)(2,1)}, f32[128,2048]{1,0:T(8,128)}, f32[256,512]{1,0:T(8,128)}, f32[256,256]{1,0:T(8,128)}, f32[256,256]{1,0:T(8,...) custom-call(bf16[128,2048]{1,0:T(8,128)(2,1)} %get-tuple-element.62., ...), custom_call_target="tpu_custom_call" | custom-call | tf_op jit(solution)/shard_map/finish_block/pallas_call | solution.py:1990
  (1 shorter events, 0.0 us)
Async XLA Ops:
  7.2 73.3 %all-gather.2.cloned.1.call-start = ((), (), s32[]{:S(2)}) async-start(), calls=%async_computation.1 | async-start | bytes 1179648 | tf_op jit(solution)/shard_map/all_gather | solution.py:2026
  8.8 341.8 %reduce-scatter.2.cloned.1.call-start = ((), (), s32[]{:S(2)}) async-start(), calls=%async_computation.2 | async-start | bytes 2359296 | tf_op jit(solution)/shard_map/reduce_scatter | solution.py:2054
Sparse Core Ops, SparseCore 0:
  10.2 25.8 all-gather.1
  222.0 38.7 reduce-scatter.1

commit v8 on v7

--- a/solution.py
+++ b/solution.py
@@ -613,7 +613,7 @@
 
 LANES = 128
 FORWARD_KEYS = 1024
-BACKWARD_KEYS = 512
+BACKWARD_KEYS = 1024
 LOG2E = 1.4426950408889634
 
 
@@ -920,7 +920,7 @@
     gated_ref, gain_ref, x_any, cot_any, left_any, wo_any, wg_any, wu_any, wd_any,
     out_any, mgrad_ref, gain_out, back_any, down_any, fgate_any, fup_any, owg_any,
     wo, wg, wu, wd, cots, rows, hid, gg, ug, terms_own, outs_own, passed, into,
-    passed2, into2, dterms, dinto, hterms, hinto, middle, back, local_sem,
+    passed2, into2, dterms, dinto, hterms, hinto, middle, back, local_sem, left_sem,
     ds, dr, hs, hr, cs, cr, cps, cpr, fs, fr, fps, fpr, s1, r1, ps1, pr1, s2, r2, ps2, pr2, bs, br,
 ):
     tok, width = x_any.shape
@@ -935,16 +935,22 @@
         pltpu.make_async_copy(src, dst, local_sem.at[i])
         for i, (src, dst) in enumerate(((wo_any, wo), (wd_any, wd), (wg_any, wg), (wu_any, wu)))
     ]
-    split = left_any.shape[1]
-    loads.append(pltpu.make_async_copy(left_any, cots.at[:, pl.ds(0, split)], local_sem.at[10]))
+    split = left_any.shape[0] // lax.axis_size("wide")
+    left = [
+        pltpu.make_async_copy(
+            left_any.at[pl.ds(i * split, split)], cots.at[pl.ds(i * tok, split)], left_sem.at[i]
+        )
+        for i in range(lax.axis_size("wide"))
+    ]
+    loads.extend(left)
     for load in loads:
         load.start()
     own_wide = pl.multiple_of(lax.axis_index("wide") * tok, tok)
     own_head = pl.multiple_of(lax.axis_index("head") * tok, tok)
     own_loads = [
         pltpu.make_async_copy(
-            cot_any.at[:, pl.ds(split, width - split)],
-            cots.at[pl.ds(own_wide, tok), pl.ds(split, width - split)],
+            cot_any.at[pl.ds(split, tok - split)],
+            cots.at[pl.ds(own_wide + split, tok - split)],
             local_sem.at[12],
         ),
         pltpu.make_async_copy(x_any, back.at[pl.ds(own_head, tok)], local_sem.at[13]),
@@ -957,9 +963,9 @@
         return lambda index, start, size: ref.at[pl.ds(index * tok + start, size)]
 
     def cot_slot(index, start, size):
-        return cots.at[pl.ds(index * tok + start, size), pl.ds(split, width - split)]
-
-    cot_gather = PairGather(wide, cot_slot, tok, cs, cr, cps, cpr)
+        return cots.at[pl.ds(index * tok + split + start, size)]
+
+    cot_gather = PairGather(wide, cot_slot, tok - split, cs, cr, cps, cpr)
     row_gather = row_gather_of(wide)(wide, slot_of(rows), tok, fs, fr, fps, fpr)
     back_gather = Gather(head, slot_of(back), tok, bs, br)
     head_scatter = Scatter(head, lambda index: (hterms, index * tok), tok, hinto, hs, hr)
@@ -1013,15 +1019,15 @@
             head_scatter.start_free()
     out_part(0, True)
     loads[1].wait()
-    loads[4].wait()
+    for load in left:
+        load.wait()
     mgrad_ref[...] = cots[pl.ds(own_wide, tok), :].astype(jnp.float32)
     cot_gather.take(0)
     hidden_part(0)
     for hop in range(head.half - 1, 0, -1):
         head_scatter.advance(hop)
     for hop in range(1, wide.half):
-        cot_gather.arrive(hop)
-        cot_gather.start(hop + 1)
+        cot_gather.step(hop)
         cot_gather.hand(hop)
         cot_gather.take(hop)
         hidden_part(hop)
@@ -1353,7 +1359,7 @@
             into_shape(head_count, hidden_width, width // head_count),
             vm((back_rows, width), low), into_shape(head_count, tok, width),
             vm((tok, width), full), vm((back_rows, width), low),
-            DMA((15,)),
+            DMA((15,)), DMA((wide_count,)),
             *ring_sems(head_count),
             *ring_sems(head_count),
             *ring_sems(chips), *pass_sems(chips),
@@ -1421,8 +1427,7 @@
     gather.start(1)
     ends = doc_ends(doc_ref)
 
-    @pl.loop(0, head_count)
-    def _(block):
+    def tables(block):
         here = pl.ds(pl.multiple_of(block * tok, tok), tok)
         first_tok = (block * wide_count + own_wide) * tok
         tokens = lax.broadcasted_iota(jnp.int32, (tok, LANES), 0) + first_tok
@@ -1430,6 +1435,8 @@
         cos_ref[here, :] = jnp.cos(angles)
         sin_ref[here, :] = jnp.sin(angles)
 
+    tables(lax.axis_index("head"))
+
     def kv_gather(offset):
         slot = offset % head_count
         block = head.index(offset)
@@ -1437,7 +1444,7 @@
         def place(index, start, size):
             return kv.at[pl.ds((block * wide_count + index) * tok + start, size)]
 
-        return row_gather_of(wide)(
+        return PairGather(
             wide, place, tok, ks.at[slot], kr.at[slot], kps.at[slot], kpr.at[slot]
         )
 
@@ -1473,33 +1480,18 @@
         gathers[offset] = kv_gather(offset)
         gathers[offset].begin()
 
-    line = wide.size == 4
-
     def step(offset, hop):
-        each = gathers[offset]
-        if line and hop == 1:
-            each.arrive(NEAR)
-
-            @pl.when(each.middle)
-            def _():
-                each.arrive(OTHER)
-
-        elif line:
-            each.arrive(FAR)
-
-            @pl.when(~each.middle)
-            def _():
-                each.arrive(OTHER)
-
+        if hop < wide.half:
+            gathers[offset].step(hop)
         else:
-            each.arrive(hop)
-            if hop < wide.half:
-                each.start(hop + 1)
-            each.hand(hop)
+            gathers[offset].arrive(hop)
+        gathers[offset].hand(hop)
 
     loads[0].wait()
     loads[1].wait()
     launch(0)
+    for offset in range(1, head_count):
+        tables(head.index(offset))
     loads[2].wait()
     loads[3].wait()
     project_rest(0)
@@ -1530,7 +1522,7 @@
         for offset in gathers:
             step(offset, hop)
     for each in gathers.values():
-        for hop in (None, NEAR, OTHER, FAR) if line else range(wide.half + 1):
+        for hop in range(wide.half + 1):
             each.take(hop)
     store = pltpu.make_async_copy(kv, kv_any, local_sem.at[5])
     store.start()
@@ -1568,7 +1560,7 @@
             vm((rows * wide_count, 2 * kv_width), low),
             DMA((6,)),
             *ring_sems(head_count),
-            *[DMA((head_count, *sem.shape)) for sem in gather_sems(chips)],
+            *[DMA((head_count, *sem.shape)) for sem in [*ring_sems(chips), *pass_sems(chips)]],
         ],
         compiler_params=pltpu.CompilerParams(
             collective_id=3, has_side_effects=True, vmem_limit_bytes=VMEM_LIMIT
@@ -2024,7 +2016,7 @@
 ):
     head_width = query_gain.shape[0]
     cot_left = lax.all_gather(
-        cotangent[:, : cotangent.shape[1] // 4], "wide", axis=0, tiled=True
+        cotangent[: cotangent.shape[0] // 4], "wide", axis=0, tiled=True
     )
     weights = (query_weight, key_projection, value_projection, attn_gate_weight)
     query_low, query_pre, key_pre, gate_pre, cosine, sine_tab, gathered, kv_all = front_block(

time: 364 us -> 361 us (level)
    pallas_call x1, Pallas kernels: 20.2 us -> 25.4 us  [attention_backward(): pl.pallas_call(attention_backward_kernel, out_shape=(shape((rows, width),...]
    pallas_call x1, Pallas kernels: 109 us -> 104 us  [tail_block(): pl.pallas_call(tail_kernel, out_shape=(shape((tok, width), full), shape((...]
where the time goes in v8:
time: 361 us; the launch traced here: 363 us
  Pallas kernels  347 us (96%)
  between operations  14.1 us (4%)
    pallas_call x1, Pallas kernels, ffn_block(): pl.pallas_call(ffn_kernel, out_shape=(shape((tok, width), low), shape((to...  142 us
    pallas_call x1, Pallas kernels, tail_block(): pl.pallas_call(tail_kernel, out_shape=(shape((tok, width), full), shape((...  104 us
    pallas_call x1, Pallas kernels, front_block(): pl.pallas_call(front_kernel, out_shape=(shape((rows, q_width), low), shap...  57.1 us
    pallas_call x1, Pallas kernels, attention_backward(): pl.pallas_call(attention_backward_kernel, out_shape=(shape((rows, width),...  25.4 us
    pallas_call x1, Pallas kernels, attention_forward(): pl.pallas_call(attention_forward_kernel, out_shape=(shape((rows, width),...  12.7 us
  transfers between devices with their start and end apart: 2, of which 0 were waited for; matrix products, arithmetic and copies ran while one was open for 0% of the time, Pallas kernels for 55%

profile of v8, /device:TPU:0, one launch (start us, length us, event | category | flops | bytes accessed | tf_op | source)
XLA Modules:
  0.0 363.1 jit_solution(16992318159508913352)
XLA Ops:
  7.2 0.0 all-gather.2.cloned.1.call-start
  7.2 1.6 slice.3
  8.8 0.0 all-gather.2.cloned.1.call-update
  8.8 0.0 reduce-scatter.2.cloned.1.call-start
  8.9 0.6 maximum_bitcast_fusion.speed_ref
  9.5 57.1 %front_block.1 = (bf16[512,512]{1,0:T(8,128)(2,1)}, f32[512,512]{1,0:T(8,128)}, f32[512,256]{1,0:T(8,128)}, f32[512,512]{1,0:T(8,128)}, f32[512,128]{1,0:T(8,128...) custom-call(s32[1,8]{1,0:T(1,128)} %doc_ref.5, bf16[128,2048]{1,0:T(8,128)(2,1)} %x_any.3, ...), custom_call_target="tpu_custom_call" | custom-call | flops 3221225472 | bytes 104857600 | tf_op jit(solution)/shard_map/front_block/pallas_call | solution.py:1543
  66.6 12.7 %attention_forward.1 = (f32[512,512]{1,0:T(8,128)}, f32[512,512]{1,0:T(8,128)}, bf16[512,512]{1,0:T(8,128)(2,1)}) custom-call(s32[1,8]{1,0:T(1,128)} %doc_ref.5, bf16[512,512]{1,0:T(8,128)(2,1)} %get-tuple-element.58.query_any, bf16[4096,512]{1,0:T(8,128)(2,1)} %get-tuple-element.59.kv_any, f32[512,512]{1,0:T(8,128)} %get-tuple-element.60.gate_any), custom_call_target="tpu_custom_call" | custom-call | flops 2147483648 | bytes 12582912 | tf_op jit(solution)/shard_map/attention_forward/pallas_call | solution.py:740
  79.3 0.0 all-gather.2.cloned.1.call-done.left_any
  79.3 142.3 %ffn_block.1 = (bf16[128,2048]{1,0:T(8,128)(2,1)}, f32[128,2048]{1,0:T(8,128)}, f32[1,2048]{1,0:T(1,128)}, bf16[512,2048]{1,0:T(8,128)(2,1)}, bf16[768,512]{1,0:...) custom-call(bf16[512,512]{1,0:T(8,128)(2,1)} %get-tuple-element.61.gated_ref, ...), custom_call_target="tpu_custom_call" | custom-call | flops 16106127360 | bytes 209715200 | tf_op jit(solution)/shard_map/ffn_block/pallas_call | solution.py:1332
  221.5 0.0 reduce-scatter.2.cloned.1.call-update
  221.6 25.4 %attention_backward.1 = (f32[512,512]{1,0:T(8,128)}, bf16[8,512,512]{2,1,0:T(8,128)(2,1)}, bf16[512,512]{1,0:T(8,128)(2,1)}) custom-call(s32[1,8]{1,0:T(1,128)} %doc_ref.5, bf16[512,512]{1,0:T(8,128)(2,1)} %get-tuple-element.58.query_any, f32[512,512]{1,0:T(8,128)} %get-tuple-element.66.att_any, f32[512,512]{1,0:T(8,128)} %get-tuple-element.67.inv_any, ...), custom_call_target="tpu_custom_call" | custom-call | flops 5368709120 | bytes 20971520 | tf_op jit(solution)/shard_map/attention_backward/pallas_call | solution.py:890
  247.0 103.9 %tail_block.1 = (f32[128,2048]{1,0:T(8,128)}, f32[8,2048]{1,0:T(8,128)}, bf16[256,512]{1,0:T(8,128)(2,1)}, bf16[256,256]{1,0:T(8,128)(2,1)}, bf16[256,256]{1,0:T...) custom-call(f32[512,128]{1,0:T(8,128)} %get-tuple-element.63.cos_ref, ...), custom_call_target="tpu_custom_call" | custom-call | flops 10737418240 | bytes 314572800 | tf_op jit(solution)/shard_map/tail_block/pallas_call | solution.py:1895
  350.9 0.0 reduce-scatter.2.cloned.1.call-done.refs_6_
  350.9 5.4 %finish_block.1 = (bf16[128,2048]{1,0:T(8,128)(2,1)}, f32[128,2048]{1,0:T(8,128)}, f32[256,512]{1,0:T(8,128)}, f32[256,256]{1,0:T(8,128)}, f32[256,256]{1,0:T(8,...) custom-call(bf16[128,2048]{1,0:T(8,128)(2,1)} %get-tuple-element.62., ...), custom_call_target="tpu_custom_call" | custom-call | tf_op jit(solution)/shard_map/finish_block/pallas_call | solution.py:1982
  (1 shorter events, 0.0 us)
Async XLA Ops:
  7.2 72.1 %all-gather.2.cloned.1.call-start = ((), (), s32[]{:S(2)}) async-start(), calls=%async_computation.1 | async-start | bytes 1179648 | tf_op jit(solution)/shard_map/all_gather | solution.py:2018
  8.8 342.1 %reduce-scatter.2.cloned.1.call-start = ((), (), s32[]{:S(2)}) async-start(), calls=%async_computation.2 | async-start | bytes 2359296 | tf_op jit(solution)/shard_map/reduce_scatter | solution.py:2046
Sparse Core Ops, SparseCore 0:
  10.2 28.7 all-gather.1
  221.7 33.2 reduce-scatter.1
